TPU v7x, 32 devices: a whole 2x2x4 slice. The times are simulated.
32 devices in a mesh: dp: 8 (over y, x, core), ctx: 4 (over z).
Axes of the slice: x: 2, y: 2, z: 4, core: 2. Of those that a mesh axis runs over, the one named last changes fastest.
Arguments:
- tokens: bfloat16 [8, 1536, 1024], P('dp', 'ctx'), may hold values from -6 to 6
- doc_starts: int32 [8, 4], P('dp'), may hold values from 0 to 1535, as said below
- attn_gain: bfloat16 [1024], P('dp'), may hold values from 0.5 to 1.5
- w_query: bfloat16 [1024, 2048], P('dp'), may hold values from -0.1875 to 0.1875
- w_key: bfloat16 [1024, 1024], P('dp'), may hold values from -0.1875 to 0.1875
- w_value: bfloat16 [1024, 1024], P('dp'), may hold values from -0.1875 to 0.1875
- w_out: bfloat16 [2048, 1024], P('dp'), may hold values from -0.75 to 0.75
- query_gain: bfloat16 [128], replicated, may hold values from 0.796875 to 2
- key_gain: bfloat16 [128], replicated, may hold values from 0.796875 to 2
- mlp_gain: bfloat16 [1024], P('dp'), may hold values from 0.5 to 1.5
- w_gate: bfloat16 [1024, 3072], P('dp'), may hold values from -0.1875 to 0.1875
- w_up: bfloat16 [1024, 3072], P('dp'), may hold values from -0.1875 to 0.1875
- w_down: bfloat16 [3072, 1024], P('dp'), may hold values from -0.109375 to 0.109375
- cotangent: bfloat16 [8, 1536, 1024], P('dp', 'ctx'), may hold values from -6 to 6
Outputs:
- output: bfloat16 [8, 1536, 1024], P('dp', 'ctx')
- input_grad: bfloat16 [8, 1536, 1024], P('dp', 'ctx')
- attn_gain_grad: float32 [1024], P('dp')
- w_query_grad: float32 [1024, 2048], P('dp')
- w_key_grad: float32 [1024, 1024], P('dp')
- w_value_grad: float32 [1024, 1024], P('dp')
- w_out_grad: float32 [2048, 1024], P('dp')
- query_gain_grad: float32 [128], replicated
- key_gain_grad: float32 [128], replicated
- mlp_gain_grad: float32 [1024], P('dp')
- w_gate_grad: float32 [1024, 3072], P('dp')
- w_up_grad: float32 [1024, 3072], P('dp')
- w_down_grad: float32 [3072, 1024], P('dp')
Inputs may be any that keep to these rules, and one draw needn't show every extreme that they name: `doc_starts`: row b holds the first stream positions of the 4 documents of pack b: it begins with 0 and rises strictly.
All inputs are finite; a program needn't handle non-finite values.
Results may differ from a plain program's by a relative error of at most 0.02.
Values may be sent and summed in bfloat16 or wider, within the bound.
No kernel may reach another device: no remote copies, remote signals or barrier semaphores. Data moves between devices by JAX's collectives and lax.ppermute only.
A program may use at most 192 MiB of HBM per device.

v0:
```python
import math

import jax
import jax.numpy as jnp
from jax import lax
from jax.sharding import PartitionSpec as P

HEADS = 16
KV_HEADS = 8
HEAD_DIM = 128


EPSILON = 1e-06
ROPE_BASE = 1000000.0
MASKED = -1e30


def stream_index(row_ids, stretch_rows, ctx_size):
    slab_index = row_ids // (2 * stretch_rows)
    within = row_ids % (2 * stretch_rows)
    mirrored = (2 * ctx_size - 1 - slab_index) * stretch_rows + within - stretch_rows
    return jnp.where(within < stretch_rows, slab_index * stretch_rows + within, mirrored)


def doc_place(stream, starts):
    started = (starts[None, :] <= stream[:, None]).astype(jnp.int32)
    doc_ids = jnp.sum(started, axis=1) - 1
    chosen = (doc_ids[:, None] == jnp.arange(starts.shape[0], dtype=jnp.int32)[None, :]).astype(
        jnp.int32
    )
    opening = jnp.sum(chosen * starts[None, :], axis=1)
    return (doc_ids, stream - opening)


def rotary(positions):
    half_dim = HEAD_DIM // 2
    inverse = jnp.exp(
        jnp.arange(half_dim, dtype=jnp.float32) * (-2.0 * math.log(ROPE_BASE) / HEAD_DIM)
    )
    angles = positions.astype(jnp.float32)[:, None] * inverse[None, :]
    angles = jnp.concatenate([angles, angles], axis=1)
    return (jnp.cos(angles), jnp.sin(angles))


def rotate(values, cos_table, sin_table):
    half_dim = values.shape[-1] // 2
    turned = jnp.concatenate([-values[..., half_dim:], values[..., :half_dim]], axis=-1)
    return values * cos_table + turned * sin_table


def rotate_back(gradients, cos_table, sin_table):
    half_dim = gradients.shape[-1] // 2
    scaled = gradients * sin_table
    turned = jnp.concatenate([scaled[..., half_dim:], -scaled[..., :half_dim]], axis=-1)
    return gradients * cos_table + turned


def norm_keep(values, gain):
    factor = lax.rsqrt(jnp.mean(values * values, axis=-1, keepdims=True) + EPSILON)
    return (values * factor * gain, factor)


def norm_back(values, factor, gain, incoming):
    weighted = incoming * gain
    inner_mean = jnp.mean(weighted * values, axis=-1, keepdims=True)
    return (
        factor * weighted - values * factor * factor * factor * inner_mean,
        incoming * values * factor,
    )


def on_device(
    tokens,
    doc_starts,
    attn_gain,
    w_query,
    w_key,
    w_value,
    w_out,
    query_gain,
    key_gain,
    mlp_gain,
    w_gate,
    w_up,
    w_down,
    cotangent,
):
    local_rows = tokens.shape[1]
    stretch_rows = local_rows // 2
    ctx_size = lax.axis_size("ctx")
    pack_rows = local_rows * ctx_size
    groups_per = HEADS // KV_HEADS
    score_scale = HEAD_DIM ** (-0.5)
    inputs_f = tokens[0].astype(jnp.float32)
    starts = doc_starts[0]
    key_stream = stream_index(jnp.arange(pack_rows, dtype=jnp.int32), stretch_rows, ctx_size)
    query_stream = stream_index(
        lax.axis_index("ctx") * local_rows + jnp.arange(local_rows, dtype=jnp.int32),
        stretch_rows,
        ctx_size,
    )
    key_doc, key_offset = doc_place(key_stream, starts)
    query_doc, query_offset = doc_place(query_stream, starts)
    cos_table, sin_table = rotary(query_offset)
    cos_heads = cos_table[:, None, :]
    sin_heads = sin_table[:, None, :]
    attn_set = (
        lax.all_gather(attn_gain, "dp", axis=0, tiled=True),
        lax.all_gather(w_query, "dp", axis=0, tiled=True),
        lax.all_gather(w_key, "dp", axis=0, tiled=True),
        lax.all_gather(w_value, "dp", axis=0, tiled=True),
        lax.all_gather(w_out, "dp", axis=0, tiled=True),
    )
    gain_attn = attn_set[0].astype(jnp.float32)
    normed_f, factor_one = norm_keep(inputs_f, gain_attn)
    normed = normed_f.astype(jnp.bfloat16)
    query_raw = jnp.dot(normed, attn_set[1], preferred_element_type=jnp.float32).reshape(
        local_rows, HEADS, HEAD_DIM
    )
    key_raw = jnp.dot(normed, attn_set[2], preferred_element_type=jnp.float32).reshape(
        local_rows, KV_HEADS, HEAD_DIM
    )
    value_raw = jnp.dot(normed, attn_set[3], preferred_element_type=jnp.float32)
    gain_query = query_gain.astype(jnp.float32)
    gain_key = key_gain.astype(jnp.float32)
    query_normed, factor_query = norm_keep(query_raw, gain_query)
    queries = (
        rotate(query_normed, cos_heads, sin_heads)
        .astype(jnp.bfloat16)
        .reshape(local_rows, KV_HEADS, groups_per, HEAD_DIM)
    )
    key_normed, factor_key = norm_keep(key_raw, gain_key)
    keys_low = (
        rotate(key_normed, cos_heads, sin_heads)
        .astype(jnp.bfloat16)
        .reshape(local_rows, KV_HEADS * HEAD_DIM)
    )
    values_low = value_raw.astype(jnp.bfloat16)
    keys_all, values_all = (
        lax.all_gather(keys_low, "ctx", axis=0, tiled=True),
        lax.all_gather(values_low, "ctx", axis=0, tiled=True),
    )
    block_rows = min(pack_rows, 512)
    num_blocks = pack_rows // block_rows
    key_blocks = keys_all.reshape(num_blocks, block_rows, KV_HEADS, HEAD_DIM)
    value_blocks = values_all.reshape(num_blocks, block_rows, KV_HEADS, HEAD_DIM)
    doc_blocks = key_doc.reshape(num_blocks, block_rows)
    stream_blocks = key_stream.reshape(num_blocks, block_rows)

    def scores_of(key_block, doc_block, stream_block):
        scores = (
            jnp.einsum("tgjd,kgd->gjtk", queries, key_block, preferred_element_type=jnp.float32)
            * score_scale
        )
        allowed = (query_doc[:, None] == doc_block[None, :]) & (
            stream_block[None, :] <= query_stream[:, None]
        )
        return (scores, allowed)

    def first_pass(running, element):
        row_max, row_total = running
        scores, allowed = scores_of(element[0], element[1], element[2])
        scores = jnp.where(allowed, scores, MASKED)
        new_max = jnp.maximum(row_max, jnp.max(scores, axis=-1))
        shifted = jnp.where(allowed, jnp.exp(scores - new_max[..., None]), 0.0)
        row_total = row_total * jnp.exp(row_max - new_max) + jnp.sum(shifted, axis=-1)
        return ((new_max, row_total), None)

    start_max = jnp.full((KV_HEADS, groups_per, local_rows), MASKED, jnp.float32)
    (row_max, row_total), ignored = lax.scan(
        first_pass, (start_max, jnp.zeros_like(start_max)), (key_blocks, doc_blocks, stream_blocks)
    )
    log_total = row_max + jnp.log(row_total)

    def probs_of(scores, allowed):
        return jnp.where(allowed, jnp.exp(scores - log_total[..., None]), 0.0)

    def second_pass(attended, element):
        scores, allowed = scores_of(element[0], element[2], element[3])
        weights_low = probs_of(scores, allowed).astype(jnp.bfloat16)
        return (
            attended
            + jnp.einsum(
                "gjtk,kgd->tgjd", weights_low, element[1], preferred_element_type=jnp.float32
            ),
            None,
        )

    start_attended = jnp.zeros((local_rows, KV_HEADS, groups_per, HEAD_DIM), jnp.float32)
    attended, ignored = lax.scan(
        second_pass, start_attended, (key_blocks, value_blocks, doc_blocks, stream_blocks)
    )
    mixed_out = attended.reshape(local_rows, HEADS * HEAD_DIM).astype(jnp.bfloat16)
    middle = inputs_f + jnp.dot(mixed_out, attn_set[4], preferred_element_type=jnp.float32)
    mlp_set = (
        lax.all_gather(mlp_gain, "dp", axis=0, tiled=True),
        lax.all_gather(w_gate, "dp", axis=0, tiled=True),
        lax.all_gather(w_up, "dp", axis=0, tiled=True),
        lax.all_gather(w_down, "dp", axis=0, tiled=True),
    )
    gain_mlp = mlp_set[0].astype(jnp.float32)
    normed_mid_f, factor_two = norm_keep(middle, gain_mlp)
    normed_mid = normed_mid_f.astype(jnp.bfloat16)
    gate_proj = jnp.dot(normed_mid, mlp_set[1], preferred_element_type=jnp.float32)
    up_proj = jnp.dot(normed_mid, mlp_set[2], preferred_element_type=jnp.float32)
    sigmoid_gate = jax.nn.sigmoid(gate_proj)
    activated = gate_proj * sigmoid_gate
    hidden = (activated * up_proj).astype(jnp.bfloat16)
    output = (middle + jnp.dot(hidden, mlp_set[3], preferred_element_type=jnp.float32)).astype(
        jnp.bfloat16
    )
    mlp_set = (
        lax.all_gather(mlp_gain, "dp", axis=0, tiled=True),
        lax.all_gather(w_gate, "dp", axis=0, tiled=True),
        lax.all_gather(w_up, "dp", axis=0, tiled=True),
        lax.all_gather(w_down, "dp", axis=0, tiled=True),
    )
    gain_mlp = mlp_set[0].astype(jnp.float32)
    grad_low = cotangent[0]
    grad_out_f = grad_low.astype(jnp.float32)
    grad_down = jnp.einsum("tf,td->fd", hidden, grad_low, preferred_element_type=jnp.float32)
    grad_hidden = jnp.einsum("td,fd->tf", grad_low, mlp_set[3], preferred_element_type=jnp.float32)
    grad_gate_act = (
        grad_hidden * up_proj * sigmoid_gate * (1.0 + gate_proj * (1.0 - sigmoid_gate))
    ).astype(jnp.bfloat16)
    grad_up_act = (grad_hidden * activated).astype(jnp.bfloat16)
    grad_gate = jnp.einsum(
        "td,tf->df", normed_mid, grad_gate_act, preferred_element_type=jnp.float32
    )
    grad_up = jnp.einsum("td,tf->df", normed_mid, grad_up_act, preferred_element_type=jnp.float32)
    grad_normed_mid = jnp.einsum(
        "tf,df->td", grad_gate_act, mlp_set[1], preferred_element_type=jnp.float32
    )
    grad_normed_mid = grad_normed_mid + jnp.einsum(
        "tf,df->td", grad_up_act, mlp_set[2], preferred_element_type=jnp.float32
    )
    grad_mid_norm, mlp_terms = norm_back(middle, factor_two, gain_mlp, grad_normed_mid)
    grad_middle = grad_out_f + grad_mid_norm
    grad_branch = grad_middle.astype(jnp.bfloat16)
    attn_set = (
        lax.all_gather(attn_gain, "dp", axis=0, tiled=True),
        lax.all_gather(w_query, "dp", axis=0, tiled=True),
        lax.all_gather(w_key, "dp", axis=0, tiled=True),
        lax.all_gather(w_value, "dp", axis=0, tiled=True),
        lax.all_gather(w_out, "dp", axis=0, tiled=True),
    )
    gain_attn = attn_set[0].astype(jnp.float32)
    grad_wout = jnp.einsum("th,td->hd", mixed_out, grad_branch, preferred_element_type=jnp.float32)
    grad_mixed = jnp.einsum(
        "td,hd->th", grad_branch, attn_set[4], preferred_element_type=jnp.float32
    ).astype(jnp.bfloat16)
    grad_mixed = grad_mixed.reshape(local_rows, KV_HEADS, groups_per, HEAD_DIM)
    delta_rows = jnp.einsum("tgjd,tgjd->gjt", grad_mixed.astype(jnp.float32), attended)

    def back_pass(grad_queries, element):
        scores, allowed = scores_of(element[0], element[2], element[3])
        probs = probs_of(scores, allowed)
        grad_probs = jnp.einsum(
            "tgjd,kgd->gjtk", grad_mixed, element[1], preferred_element_type=jnp.float32
        )
        grad_scores = (probs * (grad_probs - delta_rows[..., None])).astype(jnp.bfloat16)
        grad_queries = (
            grad_queries
            + jnp.einsum(
                "gjtk,kgd->tgjd", grad_scores, element[0], preferred_element_type=jnp.float32
            )
            * score_scale
        )
        grad_keys = (
            jnp.einsum("gjtk,tgjd->kgd", grad_scores, queries, preferred_element_type=jnp.float32)
            * score_scale
        )
        grad_values = jnp.einsum(
            "gjtk,tgjd->kgd",
            probs.astype(jnp.bfloat16),
            grad_mixed,
            preferred_element_type=jnp.float32,
        )
        return (grad_queries, (grad_keys, grad_values))

    grad_queries, (key_terms, value_terms) = lax.scan(
        back_pass,
        jnp.zeros_like(start_attended),
        (key_blocks, value_blocks, doc_blocks, stream_blocks),
    )
    key_sums = key_terms.reshape(pack_rows, KV_HEADS * HEAD_DIM)
    value_sums = value_terms.reshape(pack_rows, KV_HEADS * HEAD_DIM)
    grad_keys_own, grad_values_own = (
        lax.psum_scatter(
            key_sums.astype(jnp.bfloat16), "ctx", scatter_dimension=0, tiled=True
        ).astype(jnp.float32),
        lax.psum_scatter(
            value_sums.astype(jnp.bfloat16), "ctx", scatter_dimension=0, tiled=True
        ).astype(jnp.float32),
    )
    grad_query_rot = rotate_back(
        grad_queries.reshape(local_rows, HEADS, HEAD_DIM), cos_heads, sin_heads
    )
    grad_query_raw, query_terms = norm_back(query_raw, factor_query, gain_query, grad_query_rot)
    grad_query_low = grad_query_raw.reshape(local_rows, HEADS * HEAD_DIM).astype(jnp.bfloat16)
    grad_key_rot = rotate_back(
        grad_keys_own.reshape(local_rows, KV_HEADS, HEAD_DIM), cos_heads, sin_heads
    )
    grad_key_raw, key_gain_terms = norm_back(key_raw, factor_key, gain_key, grad_key_rot)
    grad_key_low = grad_key_raw.reshape(local_rows, KV_HEADS * HEAD_DIM).astype(jnp.bfloat16)
    grad_value_low = grad_values_own.astype(jnp.bfloat16)
    grad_wq = jnp.einsum("td,th->dh", normed, grad_query_low, preferred_element_type=jnp.float32)
    grad_wk = jnp.einsum("td,th->dh", normed, grad_key_low, preferred_element_type=jnp.float32)
    grad_wv = jnp.einsum("td,th->dh", normed, grad_value_low, preferred_element_type=jnp.float32)
    grad_normed = jnp.einsum(
        "th,dh->td", grad_query_low, attn_set[1], preferred_element_type=jnp.float32
    )
    grad_normed = grad_normed + jnp.einsum(
        "th,dh->td", grad_key_low, attn_set[2], preferred_element_type=jnp.float32
    )
    grad_normed = grad_normed + jnp.einsum(
        "th,dh->td", grad_value_low, attn_set[3], preferred_element_type=jnp.float32
    )
    grad_in_norm, attn_terms = norm_back(inputs_f, factor_one, gain_attn, grad_normed)
    grad_input = (grad_middle + grad_in_norm).astype(jnp.bfloat16)
    query_gain_sum, key_gain_sum = lax.psum(
        (jnp.sum(query_terms, axis=(0, 1)), jnp.sum(key_gain_terms, axis=(0, 1))), ("dp", "ctx")
    )
    attn_gain_local = jnp.sum(attn_terms, axis=0)
    mlp_gain_local = jnp.sum(mlp_terms, axis=0)
    slices = (
        lax.psum_scatter(
            attn_gain_local.astype(jnp.bfloat16), "dp", scatter_dimension=0, tiled=True
        ).astype(jnp.float32),
        lax.psum_scatter(
            grad_wq.astype(jnp.bfloat16), "dp", scatter_dimension=0, tiled=True
        ).astype(jnp.float32),
        lax.psum_scatter(
            grad_wk.astype(jnp.bfloat16), "dp", scatter_dimension=0, tiled=True
        ).astype(jnp.float32),
        lax.psum_scatter(
            grad_wv.astype(jnp.bfloat16), "dp", scatter_dimension=0, tiled=True
        ).astype(jnp.float32),
        lax.psum_scatter(
            grad_wout.astype(jnp.bfloat16), "dp", scatter_dimension=0, tiled=True
        ).astype(jnp.float32),
        lax.psum_scatter(
            mlp_gain_local.astype(jnp.bfloat16), "dp", scatter_dimension=0, tiled=True
        ).astype(jnp.float32),
        lax.psum_scatter(
            grad_gate.astype(jnp.bfloat16), "dp", scatter_dimension=0, tiled=True
        ).astype(jnp.float32),
        lax.psum_scatter(
            grad_up.astype(jnp.bfloat16), "dp", scatter_dimension=0, tiled=True
        ).astype(jnp.float32),
        lax.psum_scatter(
            grad_down.astype(jnp.bfloat16), "dp", scatter_dimension=0, tiled=True
        ).astype(jnp.float32),
    )
    (
        part_gain_one,
        part_query,
        part_key,
        part_value,
        part_out,
        part_gain_two,
        part_gate,
        part_up,
        part_down,
    ) = slices
    shards = (
        lax.psum(part_gain_one.astype(jnp.bfloat16), "ctx").astype(jnp.float32),
        lax.psum(part_query.astype(jnp.bfloat16), "ctx").astype(jnp.float32),
        lax.psum(part_key.astype(jnp.bfloat16), "ctx").astype(jnp.float32),
        lax.psum(part_value.astype(jnp.bfloat16), "ctx").astype(jnp.float32),
        lax.psum(part_out.astype(jnp.bfloat16), "ctx").astype(jnp.float32),
        lax.psum(part_gain_two.astype(jnp.bfloat16), "ctx").astype(jnp.float32),
        lax.psum(part_gate.astype(jnp.bfloat16), "ctx").astype(jnp.float32),
        lax.psum(part_up.astype(jnp.bfloat16), "ctx").astype(jnp.float32),
        lax.psum(part_down.astype(jnp.bfloat16), "ctx").astype(jnp.float32),
    )
    return (
        output[None],
        grad_input[None],
        shards[0],
        shards[1],
        shards[2],
        shards[3],
        shards[4],
        query_gain_sum,
        key_gain_sum,
        shards[5],
        shards[6],
        shards[7],
        shards[8],
    )


def solution(mesh):
    in_specs = (
        P("dp", "ctx", None),
        P("dp", None),
        P("dp"),
        P("dp", None),
        P("dp", None),
        P("dp", None),
        P("dp", None),
        P(),
        P(),
        P("dp"),
        P("dp", None),
        P("dp", None),
        P("dp", None),
        P("dp", "ctx", None),
    )
    out_specs = (
        P("dp", "ctx", None),
        P("dp", "ctx", None),
        P("dp"),
        P("dp", None),
        P("dp", None),
        P("dp", None),
        P("dp", None),
        P(),
        P(),
        P("dp"),
        P("dp", None),
        P("dp", None),
        P("dp", None),
    )
    return jax.shard_map(
        on_device, mesh=mesh, in_specs=in_specs, out_specs=out_specs, check_vma=False
    )
```

profile of v0, /device:TPU:0, one launch (start us, length us, event | category | flops | bytes accessed | tf_op | source)
XLA Modules:
  0.0 1254.6 jit_solution(3806843207605236605)
XLA Ops:
  9.4 10.3 all-gather
  21.2 19.4 %all-gather.12.cloned.1.call-done = bf16[1024,1024]{1,0:T(8,128)(2,1)} async-done(((bf16[128,1024]{1,0:T(8,128)(2,1)}), bf16[1024,1024]{1,0:T(8,128)(2,1)}) %all-gather.12.cloned.1.call-update) | async-done | bytes 2097168 | tf_op jit(solution)/shard_map/all_gather | solution.py:111
  45.5 24.9 %all-gather.16.cloned.1.call-done = bf16[1024,1024]{1,0:T(8,128)(2,1)} async-done(((bf16[128,1024]{1,0:T(8,128)(2,1)}), bf16[1024,1024]{1,0:T(8,128)(2,1)}) %all-gather.16.cloned.1.call-update) | async-done | bytes 2097168 | tf_op jit(solution)/shard_map/all_gather | solution.py:110
  80.6 9.2 all-gather.1
  89.8 19.2 %all-gather.20.cloned.1.call-done = bf16[1024,2048]{1,0:T(8,128)(2,1)} async-done(((bf16[128,2048]{1,0:T(8,128)(2,1)}), bf16[1024,2048]{1,0:T(8,128)(2,1)}) %all-gather.20.cloned.1.call-update) | async-done | bytes 4194320 | tf_op jit(solution)/shard_map/all_gather | solution.py:109
  125.8 48.8 %all-gather.14.cloned.1.call-done = bf16[1536,1024]{1,0:T(8,128)(2,1)} async-done(((bf16[384,1024]{1,0:T(8,128)(2,1)}), bf16[1536,1024]{1,0:T(8,128)(2,1)}) %all-gather.14.cloned.1.call-update) | async-done | bytes 3145744 | tf_op jit(solution)/shard_map/all_gather | solution.py:141
  178.9 59.8 %all-gather.18.cloned.1.call-done = bf16[1536,1024]{1,0:T(8,128)(2,1)} async-done(((bf16[384,1024]{1,0:T(8,128)(2,1)}), bf16[1536,1024]{1,0:T(8,128)(2,1)}) %all-gather.18.cloned.1.call-update) | async-done | bytes 3145744 | tf_op jit(solution)/shard_map/all_gather | solution.py:140
  243.7 44.5 %while.39 = (s32[]{:T(128)}, f32[8,2,384]{2,1,0:T(2,128)S(1)}, f32[8,2,384]{2,1,0:T(2,128)S(1)}, s32[384]{0:T(512)S(1)}, s32[3,512]{1,0:T(4,128)S(1)}, /*index=5...) while((s32[]{:T(128)}, f32[8,2,384]{2,1,0:T(2,128)S(1)}, ...), condition=%wide.region_9.10_spmd.clone, body=%wide.region_6.9_spmd.clone.sunk | while | flops 831100800 | bytes 28713612 | solution.py:170
  244.0 7.8 fusion.203
  258.7 7.8 fusion.203
  273.4 7.8 fusion.203
  288.2 34.0 %while.40 = (s32[]{:T(128)}, f32[384,8,2,128]{0,3,2,1:T(8,128)}, bf16[3,512,8,128]{3,2,1,0:T(8,128)(2,1)}, s32[384]{0:T(512)S(1)}, s32[3,512]{1,0:T(4,128)S(1)},...) while((s32[]{:T(128)}, f32[384,8,2,128]{0,3,2,1:T(8,128)}, ...), condition=%wide.region_11.12_spmd.clone, body=%wide.region_10.11_spmd.clone.sunk | while | flops 1625366400 | bytes 14590615 | solution.py:190
  302.5 8.1 bitcast_add_fusion.4
  314.4 7.8 bitcast_add_fusion.4
  331.5 7.9 fusion.138
  339.3 31.4 %all-gather.26.cloned.1.call-done = bf16[1024,3072]{1,0:T(8,128)(2,1)} async-done(((bf16[128,3072]{1,0:T(8,128)(2,1)}), bf16[1024,3072]{1,0:T(8,128)(2,1)}) %all-gather.26.cloned.1.call-update) | async-done | bytes 6291472 | tf_op jit(solution)/shard_map/all_gather | solution.py:198
  377.8 40.4 %all-gather.28.cloned.1.call-done = bf16[3072,1024]{1,0:T(8,128)(2,1)} async-done(((bf16[384,1024]{1,0:T(8,128)(2,1)}), bf16[3072,1024]{1,0:T(8,128)(2,1)}) %all-gather.28.cloned.1.call-update) | async-done | bytes 6291472 | tf_op jit(solution)/shard_map/all_gather | solution.py:199
  418.2 10.8 multiply_convert_fusion
  461.5 99.6 %while.41 = (s32[]{:T(128)}, f32[384,8,2,128]{0,3,2,1:T(8,128)}, bf16[3,512,8,128]{3,1,2,0:T(8,128)(2,1)}, bf16[3,512,8,128]{3,1,2,0:T(8,128)(2,1)}, bf16[3,512,...) while((s32[]{:T(128)}, f32[384,8,2,128]{0,3,2,1:T(8,128)}, ...), condition=%wide.region_15.16_spmd.clone, body=%wide.region_14.15_spmd.clone.sunk | while | flops 4061470720 | bytes 217736080 | solution.py:281
  594.1 34.0 %reduce-scatter.10.cloned.1.call-done = bf16[384,1024]{1,0:T(8,128)(2,1)} async-done(((bf16[1536,1024]{1,0:T(8,128)(2,1)}), bf16[384,1024]{1,0:T(8,128)(2,1)}) %reduce-scatter.10.cloned.1.call-update) | async-done | bytes 786448 | tf_op jit(solution)/shard_map/reduce_scatter | solution.py:289
  635.1 55.6 %reduce-scatter.12.cloned.1.call-done = bf16[384,1024]{1,0:T(8,128)(2,1)} async-done(((bf16[1536,1024]{1,0:T(8,128)(2,1)}), bf16[384,1024]{1,0:T(8,128)(2,1)}) %reduce-scatter.12.cloned.1.call-update) | async-done | bytes 786448 | tf_op jit(solution)/shard_map/reduce_scatter | solution.py:292
  717.7 27.6 %reduce-scatter.14.cloned.1.call-done = bf16[128,2048]{1,0:T(8,128)(2,1)} async-done(((bf16[1024,2048]{1,0:T(8,128)(2,1)}), bf16[128,2048]{1,0:T(8,128)(2,1)}) %reduce-scatter.14.cloned.1.call-update) | async-done | bytes 524304 | tf_op jit(solution)/shard_map/reduce_scatter | solution.py:330
  745.3 55.1 %reduce-scatter.20.cloned.1.call-done = bf16[256,1024]{1,0:T(8,128)(2,1)} async-done(((bf16[2048,1024]{1,0:T(8,128)(2,1)}), bf16[256,1024]{1,0:T(8,128)(2,1)}) %reduce-scatter.20.cloned.1.call-update) | async-done | bytes 524304 | tf_op jit(solution)/shard_map/reduce_scatter | solution.py:339
  800.4 44.4 %reduce-scatter.16.cloned.1.call-done = bf16[128,1024]{1,0:T(8,128)(2,1)} async-done(((bf16[1024,1024]{1,0:T(8,128)(2,1)}), bf16[128,1024]{1,0:T(8,128)(2,1)}) %reduce-scatter.16.cloned.1.call-update) | async-done | bytes 262160 | tf_op jit(solution)/shard_map/reduce_scatter | solution.py:333
  844.7 44.7 %reduce-scatter.18.cloned.1.call-done = bf16[128,1024]{1,0:T(8,128)(2,1)} async-done(((bf16[1024,1024]{1,0:T(8,128)(2,1)}), bf16[128,1024]{1,0:T(8,128)(2,1)}) %reduce-scatter.18.cloned.1.call-update) | async-done | bytes 262160 | tf_op jit(solution)/shard_map/reduce_scatter | solution.py:336
  889.5 65.0 %reduce-scatter.22.cloned.1.call-done = bf16[128,3072]{1,0:T(8,128)(2,1)} async-done(((bf16[1024,3072]{1,0:T(8,128)(2,1)}), bf16[128,3072]{1,0:T(8,128)(2,1)}) %reduce-scatter.22.cloned.1.call-update) | async-done | bytes 786448 | tf_op jit(solution)/shard_map/reduce_scatter | solution.py:345
  954.5 65.4 %reduce-scatter.24.cloned.1.call-done = bf16[128,3072]{1,0:T(8,128)(2,1)} async-done(((bf16[1024,3072]{1,0:T(8,128)(2,1)}), bf16[128,3072]{1,0:T(8,128)(2,1)}) %reduce-scatter.24.cloned.1.call-update) | async-done | bytes 786448 | tf_op jit(solution)/shard_map/reduce_scatter | solution.py:348
  1019.9 65.0 %reduce-scatter.26.cloned.1.call-done = bf16[384,1024]{1,0:T(8,128)(2,1)} async-done(((bf16[3072,1024]{1,0:T(8,128)(2,1)}), bf16[384,1024]{1,0:T(8,128)(2,1)}) %reduce-scatter.26.cloned.1.call-update) | async-done | bytes 786448 | tf_op jit(solution)/shard_map/reduce_scatter | solution.py:351
  1101.1 13.5 %all-reduce.3 = (bf16[1024]{0:T(1024)(128)(2,1)S(1)}, bf16[1024]{0:T(1024)(128)(2,1)S(1)}) all-reduce(bf16[1024]{0:T(1024)(128)(2,1)S(1)} %get-tuple-element.448, bf16[1024]{0:T(1024)(128)(2,1)S(1)} %copy-done.49), channel_id=4, replica_groups=mesh['dp'=8,'ctx'=4] {'dp'}, use_global_device_ids=true, to_apply=%region_22.23.clone | all-reduce | flops 2048 | bytes 8192
  1114.7 12.4 all-reduce.4
  1128.2 40.7 %all-reduce.2 = (f32[128]{0:T(128)}, f32[128]{0:T(128)}) all-reduce(f32[128]{0:T(128)S(1)} %get-tuple-element.442, f32[128]{0:T(128)S(1)} %get-tuple-element.446), channel_id=1, replica_groups=mesh['dp'=8,'ctx'=4] {'dp','ctx'}, use_global_device_ids=true, to_apply=%region_33.34 | all-reduce | flops 256 | bytes 2048 | tf_op jit(solution)/shard_map/psum | solution.py:321
  1171.9 66.0 %all-reduce.8.cloned.1.call-done = (bf16[128,2048]{1,0:T(8,128)(2,1)}, bf16[128,1024]{1,0:T(8,128)(2,1)}, bf16[128,1024]{1,0:T(8,128)(2,1)}, bf16[256,1024]{1,0:...) async-done(((bf16[128,2048]{1,0:T(8,128)(2,1)}, bf16[128,1024]{1,0:T(8,128)(2,1)}, bf16[128,1024]{1,0:T(8,128)(2,1)}, ...) | async-done | bytes 3932176 | tf_op jit(solution)/shard_map/psum | solution.py:368
  (358 shorter events, 327.1 us)
Async XLA Ops:
  7.2 33.4 %all-gather.12.cloned.1.call-start = ((), (), s32[]{:S(2)}) async-start(), calls=%async_computation.9 | async-start | bytes 2359296 | tf_op jit(solution)/shard_map/all_gather | solution.py:111
  7.9 62.4 %all-gather.16.cloned.1.call-start = ((), (), s32[]{:S(2)}) async-start(), calls=%async_computation.11 | async-start | bytes 2359296 | tf_op jit(solution)/shard_map/all_gather | solution.py:110
  8.7 100.3 %all-gather.20.cloned.1.call-start = ((), (), s32[]{:S(2)}) async-start(), calls=%async_computation.13 | async-start | bytes 4718592 | tf_op jit(solution)/shard_map/all_gather | solution.py:109
  9.4 165.1 %all-gather.14.cloned.1.call-start = ((), (), s32[]{:S(2)}) async-start(), calls=%async_computation.10 | async-start | bytes 3932160 | tf_op jit(solution)/shard_map/all_gather | solution.py:141
  19.8 95.7 %copy-start.40 = (f32[8,1,128]{2,1,0:T(1,128)}, f32[8,1,128]{2,1,0:T(1,128)S(1)}, u32[]{:S(2)}) copy-start(f32[8,1,128]{2,1,0:T(1,128)S(1)} %convert_element_type.258) | copy-start | bytes 12292
  21.2 94.3 %copy-start.42 = (f32[384]{0:T(512)}, f32[384]{0:T(512)S(1)}, u32[]{:S(2)}) copy-start(f32[384]{0:T(512)S(1)} %add_rsqrt_fusion.3) | copy-start | bytes 4612
  44.3 194.4 %all-gather.18.cloned.1.call-start = ((), (), s32[]{:S(2)}) async-start(), calls=%async_computation.12 | async-start | bytes 3932160 | tf_op jit(solution)/shard_map/all_gather | solution.py:140
  44.4 30.6 %copy-start.46 = (f32[128]{0:T(128)}, f32[128]{0:T(128)S(1)}, u32[]{:S(2)}) copy-start(f32[128]{0:T(128)S(1)} %convert_element_type.214) | copy-start | bytes 1540
  44.7 28.5 %copy-start.7 = (bf16[1,384,1024]{2,1,0:T(8,128)(2,1)S(1)}, bf16[1,384,1024]{2,1,0:T(8,128)(2,1)}, u32[]{:S(2)}) copy-start(bf16[1,384,1024]{2,1,0:T(8,128)(2,1)} %param.20) | copy-start | bytes 2359300
  45.5 75.6 %copy-start.15 = (f32[384,128]{0,1:T(8,128)}, f32[384,128]{0,1:T(8,128)S(1)}, u32[]{:S(2)}) copy-start(f32[384,128]{0,1:T(8,128)S(1)} %get-tuple-element.551) | copy-start | bytes 589828
  45.5 75.6 %copy-start.17 = (f32[384,128]{0,1:T(8,128)}, f32[384,128]{0,1:T(8,128)S(1)}, u32[]{:S(2)}) copy-start(f32[384,128]{0,1:T(8,128)S(1)} %get-tuple-element.550) | copy-start | bytes 589828
  77.4 248.1 %all-gather.22.cloned.1.call-start = ((), (), s32[]{:S(2)}) async-start(), calls=%async_computation.14 | async-start | bytes 4718592 | tf_op jit(solution)/shard_map/all_gather | solution.py:112
  78.0 253.4 %all-gather.24.cloned.1.call-start = ((), (), s32[]{:S(2)}) async-start(), calls=%async_computation.15 | async-start | bytes 7077888 | tf_op jit(solution)/shard_map/all_gather | solution.py:197
  78.8 292.0 %all-gather.26.cloned.1.call-start = ((), (), s32[]{:S(2)}) async-start(), calls=%async_computation.16 | async-start | bytes 7077888 | tf_op jit(solution)/shard_map/all_gather | solution.py:198
  79.5 338.7 %all-gather.28.cloned.1.call-start = ((), (), s32[]{:S(2)}) async-start(), calls=%async_computation.17 | async-start | bytes 7077888 | tf_op jit(solution)/shard_map/all_gather | solution.py:199
  80.2 547.8 %reduce-scatter.10.cloned.1.call-start = ((), (), s32[]{:S(2)}) async-start(), calls=%async_computation.18 | async-start | bytes 3932160 | tf_op jit(solution)/shard_map/reduce_scatter | solution.py:289
  80.5 40.6 %copy-start.44 = (f32[128]{0:T(128)}, f32[128]{0:T(128)S(1)}, u32[]{:S(2)}) copy-start(f32[128]{0:T(128)S(1)} %convert_element_type.217) | copy-start | bytes 1540
  331.4 39.3 %copy-start.26 = (bf16[384,1024]{1,0:T(8,128)(2,1)}, bf16[384,1024]{1,0:T(8,128)(2,1)S(1)}, u32[]{:S(2)}) copy-start(bf16[384,1024]{1,0:T(8,128)(2,1)S(1)} %multiply_convert_fusion.3) | copy-start | bytes 2359300
  339.3 78.9 %copy-start.31 = (bf16[1,384,1024]{2,1,0:T(8,128)(2,1)S(1)}, bf16[1,384,1024]{2,1,0:T(8,128)(2,1)}, u32[]{:S(2)}) copy-start(bf16[1,384,1024]{2,1,0:T(8,128)(2,1)} %param.33) | copy-start | bytes 2359300
  567.6 123.1 %reduce-scatter.12.cloned.1.call-start = ((), (), s32[]{:S(2)}) async-start(), calls=%async_computation.19 | async-start | bytes 3932160 | tf_op jit(solution)/shard_map/reduce_scatter | solution.py:292
  574.1 171.2 %reduce-scatter.14.cloned.1.call-start = ((), (), s32[]{:S(2)}) async-start(), calls=%async_computation.20 | async-start | bytes 4718592 | tf_op jit(solution)/shard_map/reduce_scatter | solution.py:330
  586.6 213.7 %reduce-scatter.20.cloned.1.call-start = ((), (), s32[]{:S(2)}) async-start(), calls=%async_computation.23 | async-start | bytes 4718592 | tf_op jit(solution)/shard_map/reduce_scatter | solution.py:339
  593.8 251.0 %reduce-scatter.16.cloned.1.call-start = ((), (), s32[]{:S(2)}) async-start(), calls=%async_computation.21 | async-start | bytes 2359296 | tf_op jit(solution)/shard_map/reduce_scatter | solution.py:333
  635.0 59.6 %copy-start.27 = (bf16[384,1024]{1,0:T(8,128)(2,1)S(1)}, bf16[384,1024]{1,0:T(8,128)(2,1)}, u32[]{:S(2)}) copy-start(bf16[384,1024]{1,0:T(8,128)(2,1)} %copy-done.26) | copy-start | bytes 2359300
  635.0 254.5 %reduce-scatter.18.cloned.1.call-start = ((), (), s32[]{:S(2)}) async-start(), calls=%async_computation.22 | async-start | bytes 2359296 | tf_op jit(solution)/shard_map/reduce_scatter | solution.py:336
  694.6 259.9 %reduce-scatter.22.cloned.1.call-start = ((), (), s32[]{:S(2)}) async-start(), calls=%async_computation.24 | async-start | bytes 7077888 | tf_op jit(solution)/shard_map/reduce_scatter | solution.py:345
  701.7 318.1 %reduce-scatter.24.cloned.1.call-start = ((), (), s32[]{:S(2)}) async-start(), calls=%async_computation.25 | async-start | bytes 7077888 | tf_op jit(solution)/shard_map/reduce_scatter | solution.py:348
  709.2 375.7 %reduce-scatter.26.cloned.1.call-start = ((), (), s32[]{:S(2)}) async-start(), calls=%async_computation.26 | async-start | bytes 7077888 | tf_op jit(solution)/shard_map/reduce_scatter | solution.py:351
  717.4 367.5 %copy-start.55 = (u32[32]{0:T(128)S(1)}, u32[32]{0:T(128)}, u32[]{:S(2)}) copy-start(u32[32]{0:T(128)} %constant.138) | copy-start | bytes 388
  717.4 368.8 %copy-start.25 = (bf16[384,16,128]{0,2,1:T(8,128)(2,1)S(1)}, bf16[384,16,128]{0,2,1:T(8,128)(2,1)}, u32[]{:S(2)}) copy-start(bf16[384,16,128]{0,2,1:T(8,128)(2,1)} %copy-done.24) | copy-start | bytes 4718596
  717.4 520.5 %all-reduce.8.cloned.1.call-start = ((), (), s32[]{:S(2)}) async-start(), calls=%async_computation.27 | async-start | bytes 7864320 | tf_op jit(solution)/shard_map/psum | solution.py:368
  1098.6 70.4 %copy-start.11 = (f32[384,1024]{1,0:T(8,128)S(1)}, f32[384,1024]{1,0:T(8,128)}, u32[]{:S(2)}) copy-start(f32[384,1024]{1,0:T(8,128)} %copy-done.9) | copy-start | bytes 4718596
  (63 other events, 248.7 us)
Sparse Core Ops, SparseCore 0:
  9.9 30.5 all-gather.11
  42.4 27.8 all-gather.15
  72.2 36.7 all-gather.19
  111.0 63.4 all-gather.13
  176.5 62.1 all-gather.17
  240.4 35.3 all-gather.21
  277.7 45.5 all-gather.23
  325.2 45.5 all-gather.25
  372.6 45.5 all-gather.27
  567.7 60.2 reduce-scatter.9
  630.3 60.2 reduce-scatter.11
  693.9 51.3 reduce-scatter.13
  749.0 51.3 reduce-scatter.19
  803.5 41.1 reduce-scatter.15
  848.2 41.2 reduce-scatter.17
  892.7 61.7 reduce-scatter.21
  958.1 61.7 reduce-scatter.23
  1023.1 61.7 reduce-scatter.25
  1088.1 149.8 all-reduce.7
where the time goes:
time: 1260 us; the launch traced here: 1250 us
  waiting for transfers between devices  771 us (61%)
  matrix products  226 us (18%)
  local copies, waits for them, and re-layouts  93.7 us (7%)
  blocking collectives  86.2 us (7%)
  other arithmetic  59 us (5%)
  between operations  15.8 us (1%)
    psum x1, waiting for transfers between devices, on_device(): lax.psum(part_query.astype(jnp.bfloat16), 'ctx').astype(jnp.float32)  66 us
    reduce_scatter x1, waiting for transfers between devices, on_device(): lax.psum_scatter(grad_up.astype(jnp.bfloat16), 'dp', scatter_dimension=0,...  65.4 us
    reduce_scatter x1, waiting for transfers between devices, on_device(): lax.psum_scatter(grad_gate.astype(jnp.bfloat16), 'dp', scatter_dimension=...  65 us
    reduce_scatter x1, waiting for transfers between devices, on_device(): lax.psum_scatter(grad_down.astype(jnp.bfloat16), 'dp', scatter_dimension=...  65 us
    all_gather x1, waiting for transfers between devices, on_device(): lax.all_gather(keys_low, 'ctx', axis=0, tiled=True)  59.8 us
    reduce_scatter x1, waiting for transfers between devices, on_device(): lax.psum_scatter(value_sums.astype(jnp.bfloat16), 'ctx', scatter_dimensio...  55.6 us
    reduce_scatter x1, waiting for transfers between devices, on_device(): lax.psum_scatter(grad_wout.astype(jnp.bfloat16), 'dp', scatter_dimension=...  55.1 us
    all_gather x1, waiting for transfers between devices, on_device(): lax.all_gather(values_low, 'ctx', axis=0, tiled=True)  48.8 us
  transfers between devices with their start and end apart: 19, of which 17 were waited for; matrix products, arithmetic and copies ran while one was open for 16% of the time, Pallas kernels for 0%

commit v1 on v0

v1 whole, which is shorter than its diff:
```python
import functools
import math

import jax
import jax.numpy as jnp
from jax import lax
from jax.experimental import pallas as pl
from jax.experimental.pallas import tpu as pltpu
from jax.sharding import PartitionSpec as P

HEADS = 16
KV_HEADS = 8
HEAD_DIM = 128
GROUPS = HEADS // KV_HEADS

EPSILON = 1e-06
ROPE_BASE = 1000000.0
MASKED = -1e30
SCALE = HEAD_DIM ** (-0.5)

F32 = jnp.float32
BF16 = jnp.bfloat16
MIB = 1 << 20
VMEM_MIB = 32
LARGE = 1 << 18


ORDER = []


def shape(dims, dtype):
    return jax.ShapeDtypeStruct(dims, dtype)


ANY = pl.BlockSpec(memory_space=pl.ANY)
IN_VMEM = pl.BlockSpec(memory_space=pltpu.VMEM)


def in_hbm(spec, array):
    return spec is not IN_VMEM and spec is not ANY and math.prod(array.shape) * 2 >= LARGE


def call(
    name, body, args, in_specs, out_specs, out_shape, grid=(1,), scratch=(), prefetch=(), aliases=None,
    after=(),
):
    waits = list(ORDER) + list(after)
    taken = len(prefetch) + len(args)
    args = [
        pltpu.with_memory_space_constraint(a, pltpu.HBM) if in_hbm(s, a) else a
        for a, s in zip(args, in_specs)
    ]
    out_shape = [
        pltpu.HBM(o.shape, o.dtype) if in_hbm(s, o) else o for o, s in zip(out_shape, out_specs)
    ]

    def without(*refs):
        body(*refs[:taken], *refs[taken + len(waits) :])

    results = pl.pallas_call(
        without,
        grid_spec=pltpu.PrefetchScalarGridSpec(
            num_scalar_prefetch=len(prefetch),
            grid=grid,
            in_specs=list(in_specs) + [pl.BlockSpec(memory_space=pl.ANY)] * len(waits),
            out_specs=out_specs,
            scratch_shapes=list(scratch),
        ),
        out_shape=out_shape,
        input_output_aliases={len(prefetch) + i: o for i, o in (aliases or {}).items()},
        compiler_params=pltpu.CompilerParams(vmem_limit_bytes=VMEM_MIB * MIB),
        cost_estimate=pl.CostEstimate(flops=0, bytes_accessed=0, transcendentals=0),
        name=name,
    )(*prefetch, *args, *waits)
    ORDER[:] = [min(results, key=lambda r: r.size)]
    return results


def whole(dims):
    return pl.BlockSpec(dims, lambda *_: (0,) * len(dims))


def mm(a, b):
    return lax.dot_general(a, b, (((1,), (0,)), ((), ())), preferred_element_type=F32)


def mm_nt(a, b):
    return lax.dot_general(a, b, (((1,), (1,)), ((), ())), preferred_element_type=F32)


def mm_tn(a, b):
    return lax.dot_general(a, b, (((0,), (0,)), ((), ())), preferred_element_type=F32)


def mean_last(v):
    return jnp.sum(v, axis=-1, keepdims=True) * (1.0 / v.shape[-1])


def factor_of(v):
    return lax.rsqrt(mean_last(v * v) + EPSILON)


def norm_back(v, gain, incoming):
    f = factor_of(v)
    weighted = incoming * gain
    inner = mean_last(weighted * v)
    return f * weighted - v * (f * f * f * inner), incoming * v * f


def stream_index(row_ids, stretch_rows, ctx_size):
    slab_index = row_ids // (2 * stretch_rows)
    within = row_ids % (2 * stretch_rows)
    mirrored = (2 * ctx_size - 1 - slab_index) * stretch_rows + within - stretch_rows
    return jnp.where(within < stretch_rows, slab_index * stretch_rows + within, mirrored)


def opening_of(stream, starts):
    started = starts[None, :] <= stream[:, None]
    return jnp.max(jnp.where(started, starts[None, :], 0), axis=1)


def rotary(positions):
    half_dim = HEAD_DIM // 2
    inverse = jnp.exp(
        jnp.arange(half_dim, dtype=F32) * (-2.0 * math.log(ROPE_BASE) / HEAD_DIM)
    )
    angles = positions.astype(F32)[:, None] * inverse[None, :]
    cos_half, sin_half = jnp.cos(angles), jnp.sin(angles)
    return (
        jnp.concatenate([cos_half, cos_half], axis=1),
        jnp.concatenate([-sin_half, sin_half], axis=1),
    )


def copies(name, sources, plan, out_shape, prefetch=(), after=()):
    count = len(sources)
    first = len(prefetch)

    def body(*refs):
        ins = refs[first : first + count]
        for source, target in plan(refs[:first], ins, refs[first + count :]):
            target[...] = source[...]

    return call(
        name, body, sources, [IN_VMEM] * count, [IN_VMEM] * len(out_shape), out_shape,
        prefetch=prefetch, after=after,
    )


def touch(after):
    def body(out_ref):
        out_ref[...] = jnp.zeros_like(out_ref)

    call("touch", body, [], [], [IN_VMEM], [shape((8, HEAD_DIM), F32)], after=after)


def norm_own(tokens, gain):
    def body(t_ref, g_ref, out_ref):
        x = t_ref[...].astype(F32)
        out_ref[...] = (x * factor_of(x) * g_ref[...]).astype(BF16)

    return call(
        "norm_own", body, [tokens, gain], [IN_VMEM] * 2, [IN_VMEM], [shape(tokens.shape, BF16)]
    )[0]


def norm_pack(own, from_left, from_right, gain, places, ctx_at):
    count = len(from_left) + 1
    rows, width = own.shape
    half = rows // 2

    def body(places_ref, at_ref, gain_ref, *refs):
        blocks, pack_ref = refs[:-1], refs[-1]
        step = pl.program_id(0)
        me = at_ref[0]

        def write(ref):
            x = ref[...].astype(F32)
            low = (x * factor_of(x) * gain_ref[...]).astype(BF16)
            pack_ref[...] = low.reshape(2, 1, half, width)

        @pl.when(step == 0)
        def _():
            write(blocks[0])

        for s in range(1, count):

            @pl.when((step == s) & (me >= s))
            def _():
                write(blocks[s])

            @pl.when((step == s) & (me < s))
            def _():
                write(blocks[count - 1 + count - s])

    blocks = [own] + from_left + from_right
    return call(
        "norm_pack", body, [gain] + blocks,
        [whole((1, width))] + [IN_VMEM] * len(blocks),
        [pl.BlockSpec((2, 1, half, width), lambda k, at, me: (0, at[k], 0, 0))],
        [shape((2, count, half, width), BF16)],
        grid=(count,), prefetch=[places, ctx_at],
    )[0]


def head_norm_rope(raw, gain, cos, sin):
    normed = raw * factor_of(raw) * gain
    return normed * cos + pltpu.roll(normed, HEAD_DIM // 2, 1) * sin


def project_queries(x, weights, gain, cos, sin):
    rows, width = x.shape
    step_cols = 2 * HEAD_DIM
    cols = HEADS * HEAD_DIM

    def body(x_ref, w_ref, g_ref, c_ref, s_ref, raw_ref, rot_ref):
        raw = mm(x_ref[...], w_ref[...])
        raw_ref[...] = raw
        for h in range(2):
            part = raw[:, h * HEAD_DIM : (h + 1) * HEAD_DIM]
            turned = head_norm_rope(part, g_ref[...], c_ref[...], s_ref[...])
            rot_ref[:, h * HEAD_DIM : (h + 1) * HEAD_DIM] = turned.astype(BF16)

    col = pl.BlockSpec((rows, step_cols), lambda j: (0, j))
    return call(
        "project_queries", body, [x, weights, gain, cos, sin],
        [
            whole((rows, width)),
            pl.BlockSpec((width, step_cols), lambda j: (0, j)),
            whole((1, HEAD_DIM)),
            whole((rows, HEAD_DIM)),
            whole((rows, HEAD_DIM)),
        ],
        [col, col],
        [shape((rows, cols), F32), shape((rows, cols), BF16)],
        grid=(cols // step_cols,),
    )


def project_keys_values(x, weights, gain, cos, sin):
    rows, width = x.shape
    step_cols = 2 * HEAD_DIM
    cols = KV_HEADS * HEAD_DIM
    key_at = HEADS * HEAD_DIM // step_cols
    value_at = key_at + cols // step_cols

    def body(x_ref, wk_ref, wv_ref, g_ref, c_ref, s_ref, raw_ref, rot_ref, val_ref):
        raw = mm(x_ref[...], wk_ref[...])
        raw_ref[...] = raw
        for h in range(2):
            part = raw[:, h * HEAD_DIM : (h + 1) * HEAD_DIM]
            turned = head_norm_rope(part, g_ref[...], c_ref[...], s_ref[...])
            rot_ref[:, h * HEAD_DIM : (h + 1) * HEAD_DIM] = turned.astype(BF16)
        val_ref[...] = mm(x_ref[...], wv_ref[...]).astype(BF16)

    col = pl.BlockSpec((rows, step_cols), lambda j: (0, j))
    return call(
        "project_keys_values", body, [x, weights, weights, gain, cos, sin],
        [
            whole((rows, width)),
            pl.BlockSpec((width, step_cols), lambda j: (0, key_at + j)),
            pl.BlockSpec((width, step_cols), lambda j: (0, value_at + j)),
            whole((1, HEAD_DIM)),
            whole((rows, HEAD_DIM)),
            whole((rows, HEAD_DIM)),
        ],
        [col, col, col],
        [shape((rows, cols), F32), shape((rows, cols), BF16), shape((rows, cols), BF16)],
        grid=(cols // step_cols,),
    )


def attend(queries, keys, values, q_low, q_high, k_stream):
    rows = queries.shape[0]
    half = rows // 2
    pack = keys.shape[0]
    pair = GROUPS * HEAD_DIM

    def body(q_ref, k_ref, v_ref, lo_ref, hi_ref, ks_ref, att_ref, mix_ref, lse_ref, bias):
        @pl.when(pl.program_id(0) == 0)
        def _():
            ks = ks_ref[...]
            ok = (ks >= lo_ref[...]) & (ks <= hi_ref[...])
            bias[...] = jnp.where(ok, 0.0, MASKED)

        for part in range(2):
            here = slice(part * half, (part + 1) * half)
            seen = pack // 2 if part == 0 else pack
            q2 = jnp.concatenate(
                [q_ref[here, j * HEAD_DIM : (j + 1) * HEAD_DIM] for j in range(GROUPS)], axis=0
            )
            scores = mm_nt(q2, k_ref[:seen, :]) * SCALE
            scores = (scores.reshape(GROUPS, half, seen) + bias[here, :seen][None]).reshape(
                GROUPS * half, seen
            )
            top = jnp.max(scores, axis=-1, keepdims=True)
            shifted = jnp.exp(scores - top)
            total = jnp.sum(shifted, axis=-1, keepdims=True)
            out = mm(shifted.astype(BF16), v_ref[:seen, :]) * (1.0 / total)
            for j in range(GROUPS):
                piece = out[j * half : (j + 1) * half]
                att_ref[here, j * HEAD_DIM : (j + 1) * HEAD_DIM] = piece
                mix_ref[here, j * HEAD_DIM : (j + 1) * HEAD_DIM] = piece.astype(BF16)
            lse = jnp.broadcast_to(top + jnp.log(total), (GROUPS * half, HEAD_DIM)).T
            lse_ref[0, :, part * GROUPS * half : (part + 1) * GROUPS * half] = lse[:8]

    col = pl.BlockSpec((rows, pair), lambda g: (0, g))
    key = pl.BlockSpec((pack, HEAD_DIM), lambda g: (0, g))
    return call(
        "attend", body, [queries, keys, values, q_low, q_high, k_stream],
        [col, key, key, whole((rows, 1)), whole((rows, 1)), whole((1, pack))],
        [col, col, pl.BlockSpec((1, 8, GROUPS * rows), lambda g: (g, 0, 0))],
        [
            shape((rows, HEADS * HEAD_DIM), F32),
            shape((rows, HEADS * HEAD_DIM), BF16),
            shape((KV_HEADS, 8, GROUPS * rows), F32),
        ],
        grid=(KV_HEADS,),
        scratch=[pltpu.VMEM((rows, pack), F32)],
    )


def project_out(mixed, stack, tokens, gain):
    rows, inner = mixed.shape
    count, _, width = stack.shape
    unit = width // count
    block = 256
    steps = width // block

    def body(m_ref, a_ref, b_ref, t_ref, g_ref, mid_ref, low_ref, acc):
        j = pl.program_id(0)
        w = jnp.concatenate([a_ref[...], b_ref[...]], axis=1).reshape(inner, block)
        acc[j] = t_ref[...].astype(F32) + mm(m_ref[...], w)

        @pl.when(j == steps - 1)
        def _():
            mid = jnp.concatenate([acc[i] for i in range(steps)], axis=1)
            mid_ref[...] = mid
            low_ref[...] = (mid * factor_of(mid) * g_ref[...]).astype(BF16)

    return call(
        "project_out", body, [mixed, stack, stack, tokens, gain],
        [
            whole((rows, inner)),
            pl.BlockSpec((count, unit, block), lambda j: (0, 9, j)),
            pl.BlockSpec((count, unit, block), lambda j: (0, 10, j)),
            pl.BlockSpec((rows, block), lambda j: (0, j)),
            whole((1, width)),
        ],
        [whole((rows, width)), whole((rows, width))],
        [shape((rows, width), F32), shape((rows, width), BF16)],
        grid=(steps,),
        scratch=[pltpu.VMEM((steps, rows, block), F32)],
    )


def gate_up(x, stack):
    rows, width = x.shape
    count = stack.shape[0]
    unit = width // count
    block = 256
    per = width // block
    hidden = 3 * width

    def body(x_ref, g_ref, u_ref, h_ref, dg_ref, du_ref):
        g = mm(x_ref[...], g_ref[...].reshape(width, block))
        u = mm(x_ref[...], u_ref[...].reshape(width, block))
        s = 1.0 / (1.0 + jnp.exp(-g))
        act = g * s
        h_ref[...] = (act * u).astype(BF16)
        dg_ref[...] = (u * s * (1.0 + g * (1.0 - s))).astype(BF16)
        du_ref[...] = act.astype(BF16)

    col = pl.BlockSpec((rows, block), lambda j: (0, j))
    return call(
        "gate_up", body, [x, stack, stack],
        [
            whole((rows, width)),
            pl.BlockSpec((count, unit, block), lambda j: (0, 3 + j // per, j % per)),
            pl.BlockSpec((count, unit, block), lambda j: (0, 6 + j // per, j % per)),
        ],
        [col, col, col],
        [shape((rows, hidden), BF16)] * 3,
        grid=(hidden // block,),
    )


def down_both(hidden, slope_gate, slope_up, grad, stack, middle):
    rows, inner = hidden.shape
    count, _, width = stack.shape
    unit = width // count
    block = 384
    per = block // (3 * unit)
    steps = inner // block

    def body(h_ref, sg_ref, su_ref, dy_ref, w_ref, mid_ref, out_ref, both_ref, acc):
        j = pl.program_id(0)
        w = w_ref[...].reshape(block, width)
        dh = mm_nt(dy_ref[...], w)
        both_ref[0] = (dh * sg_ref[...].astype(F32)).astype(BF16)
        both_ref[1] = (dh * su_ref[...].astype(F32)).astype(BF16)

        @pl.when(j == 0)
        def _():
            acc[...] = mid_ref[...]

        acc[...] += mm(h_ref[...], w)

        @pl.when(j == steps - 1)
        def _():
            out_ref[...] = acc[...].astype(BF16)

    col = pl.BlockSpec((rows, block), lambda j: (0, j))
    return call(
        "down_both", body, [hidden, slope_gate, slope_up, grad, stack, middle],
        [
            col,
            col,
            col,
            whole((rows, width)),
            pl.BlockSpec((per, 3 * unit, width), lambda j: (j, 0, 0)),
            whole((rows, width)),
        ],
        [whole((rows, width)), pl.BlockSpec((2, rows, block), lambda j: (0, 0, j))],
        [shape((rows, width), BF16), shape((2, rows, inner), BF16)],
        grid=(steps,),
        scratch=[pltpu.VMEM((rows, width), F32)],
    )


def mlp_back(d_both, stack, middle, gain, grad):
    _, rows, inner = d_both.shape
    count, _, width = stack.shape
    unit = width // count
    steps = inner // width

    def body(both_ref, g_ref, u_ref, mid_ref, gain_ref, dy_ref, gm_ref, gb_ref, gg_ref, acc):
        j = pl.program_id(0)
        part = mm_nt(both_ref[0], g_ref[...].reshape(width, width))
        part += mm_nt(both_ref[1], u_ref[...].reshape(width, width))

        @pl.when(j == 0)
        def _():
            acc[...] = part

        @pl.when(j > 0)
        def _():
            acc[...] += part

        @pl.when(j == steps - 1)
        def _():
            back, terms = norm_back(mid_ref[...], gain_ref[...], acc[...])
            total = dy_ref[...].astype(F32) + back
            gm_ref[...] = total
            gb_ref[...] = total.astype(BF16)
            gg_ref[...] = jnp.sum(terms, axis=0, keepdims=True)

    return call(
        "mlp_back", body, [d_both, stack, stack, middle, gain, grad],
        [
            pl.BlockSpec((2, rows, width), lambda j: (0, 0, j)),
            pl.BlockSpec((count, unit, width), lambda j: (0, 3 + j, 0)),
            pl.BlockSpec((count, unit, width), lambda j: (0, 6 + j, 0)),
            whole((rows, width)),
            whole((1, width)),
            whole((rows, width)),
        ],
        [whole((rows, width)), whole((rows, width)), whole((1, width))],
        [shape((rows, width), F32), shape((rows, width), BF16), shape((1, width), F32)],
        grid=(steps,),
        scratch=[pltpu.VMEM((rows, width), F32)],
    )


def mixed_back(grad_branch, stack):
    rows, width = grad_branch.shape
    count = stack.shape[0]
    unit = width // count
    block = 256
    per = block // (2 * unit)
    cols = HEADS * HEAD_DIM

    def body(gb_ref, a_ref, b_ref, out_ref):
        w = jnp.concatenate([a_ref[...], b_ref[...]], axis=1).reshape(block, width)
        out_ref[...] = mm_nt(gb_ref[...], w).astype(BF16)

    return call(
        "mixed_back", body, [grad_branch, stack, stack],
        [
            whole((rows, width)),
            pl.BlockSpec((per, unit, width), lambda j: (j, 9, 0)),
            pl.BlockSpec((per, unit, width), lambda j: (j, 10, 0)),
        ],
        [pl.BlockSpec((rows, block), lambda j: (0, j))],
        [shape((rows, cols), BF16)],
        grid=(cols // block,),
    )[0]


def attend_back(
    queries, grad_mixed, attended, keys, values, lse, q_low, q_high, k_stream,
    query_raw, key_raw, query_gain, key_gain, cos_own, sin_own, cos_pack, sin_pack,
    first_head, heads, earlier=(),
):
    rows = queries.shape[0]
    half = rows // 2
    pack = keys.shape[0]
    pair = GROUPS * HEAD_DIM
    wide = GROUPS * rows
    chunk = 256

    def stacked(ref):
        return jnp.concatenate(
            [
                ref[part * half : (part + 1) * half, j * HEAD_DIM : (j + 1) * HEAD_DIM]
                for part in range(2)
                for j in range(GROUPS)
            ],
            axis=0,
        )

    def unrotate(e, cos, sin):
        return e * cos - pltpu.roll(e, HEAD_DIM // 2, 1) * sin

    def body(
        q_ref, do_ref, att_ref, k_ref, v_ref, lse_ref, lo_ref, hi_ref, ks_ref,
        qr_ref, kr_ref, qg_ref, kg_ref, co_ref, so_ref, cp_ref, sp_ref,
        *rest,
    ):
        dq_ref, pair_ref, qgg_ref, kgg_ref, bias, dq_acc = rest[len(earlier) :]

        @pl.when(pl.program_id(0) == 0)
        def _():
            ks = ks_ref[...]
            ok = (ks >= lo_ref[...]) & (ks <= hi_ref[...])
            bias[...] = jnp.where(ok, 0.0, MASKED)
            qgg_ref[...] = jnp.zeros_like(qgg_ref)
            kgg_ref[...] = jnp.zeros_like(kgg_ref)

        q_all = stacked(q_ref)
        do_all = stacked(do_ref)
        delta = jnp.sum((do_all.astype(F32) * stacked(att_ref)).T, axis=0, keepdims=True)
        lse_row = lse_ref[0, 0:1, :]
        k_sum = jnp.zeros((1, HEAD_DIM), F32)
        for at in range(pack // chunk):
            here = slice(at * chunk, (at + 1) * chunk)
            first = 0 if at * chunk < pack // 2 else GROUPS * half
            kk, vv = k_ref[here, :], v_ref[here, :]
            qq, dd = q_all[first:], do_all[first:]
            scores = mm_nt(kk, qq) * SCALE + (bias[here, first:] - lse_row[:, first:])
            probs = jnp.exp(scores)
            d_probs = mm_nt(vv, dd)
            d_scores = (probs * (d_probs - delta[:, first:])).astype(BF16)
            pair_ref[1, here, :] = mm(probs.astype(BF16), dd).astype(BF16)
            dk = mm(d_scores, qq) * SCALE
            dq = mm_tn(d_scores, kk)
            if at == 0:
                dq_acc[...] = dq
            else:
                dq_acc[first:, :] += dq
            dk = unrotate(dk, cp_ref[here, :], sp_ref[here, :])
            dk, terms = norm_back(kr_ref[here, :], kg_ref[...], dk)
            pair_ref[0, here, :] = dk.astype(BF16)
            k_sum += jnp.sum(terms, axis=0, keepdims=True)
        kgg_ref[...] += k_sum
        for j in range(GROUPS):
            cols = slice(j * HEAD_DIM, (j + 1) * HEAD_DIM)
            dq = jnp.concatenate(
                [
                    dq_acc[(part * GROUPS + j) * half : (part * GROUPS + j + 1) * half, :]
                    for part in range(2)
                ],
                axis=0,
            ) * SCALE
            dq = unrotate(dq, co_ref[...], so_ref[...])
            dq, terms = norm_back(qr_ref[:, cols], qg_ref[...], dq)
            dq_ref[:, cols] = dq.astype(BF16)
            qgg_ref[...] += jnp.sum(terms, axis=0, keepdims=True)

    col = pl.BlockSpec((rows, pair), lambda g: (0, first_head + g))
    key = pl.BlockSpec((pack, HEAD_DIM), lambda g: (0, first_head + g))
    gain = whole((1, HEAD_DIM))
    return call(
        "attend_back", body,
        [
            queries, grad_mixed, attended, keys, values, lse, q_low, q_high, k_stream,
            query_raw, key_raw, query_gain, key_gain, cos_own, sin_own, cos_pack, sin_pack,
            *earlier,
        ],
        [
            col, col, col, key, key,
            pl.BlockSpec((1, 8, wide), lambda g: (first_head + g, 0, 0)),
            whole((1, wide)), whole((1, wide)), whole((pack, 1)),
            col, key, gain, gain,
            whole((rows, HEAD_DIM)), whole((rows, HEAD_DIM)),
            whole((pack, HEAD_DIM)), whole((pack, HEAD_DIM)),
        ]
        + [ANY] * len(earlier),
        [col, pl.BlockSpec((2, pack, HEAD_DIM), lambda g: (0, 0, first_head + g)), gain, gain],
        [
            shape((rows, HEADS * HEAD_DIM), BF16),
            shape((2, pack, KV_HEADS * HEAD_DIM), BF16),
            shape((1, HEAD_DIM), F32),
            shape((1, HEAD_DIM), F32),
        ],
        grid=(heads,),
        scratch=[pltpu.VMEM((pack, wide), F32), pltpu.VMEM((wide, HEAD_DIM), F32)],
        aliases={17 + i: i for i in range(len(earlier))},
    )


def normed_back_pack(d_pair, weights, ctx_size):
    _, pack, cols = d_pair.shape
    half = pack // (2 * ctx_size)
    width = weights.shape[0]

    def body(pair_ref, wk_ref, wv_ref, out_ref):
        part = mm_nt(pair_ref[0].reshape(2 * half, cols), wk_ref[...])
        part += mm_nt(pair_ref[1].reshape(2 * half, cols), wv_ref[...])
        out_ref[...] = part.astype(BF16)

    return call(
        "normed_back_pack", body, [d_pair.reshape(2, 2, ctx_size, half, cols), weights, weights],
        [
            pl.BlockSpec((2, 2, 1, half, cols), lambda d: (0, 0, d, 0, 0)),
            pl.BlockSpec((width, cols), lambda d: (0, 2)),
            pl.BlockSpec((width, cols), lambda d: (0, 3)),
        ],
        [pl.BlockSpec((2 * half, width), lambda d: (d, 0))],
        [shape((pack, width), BF16)],
        grid=(ctx_size,),
    )[0]


def normed_back_own(d_queries, weights):
    rows, cols = d_queries.shape
    width = weights.shape[0]
    block = 1024

    def body(dq_ref, w_ref, out_ref):
        part = mm_nt(dq_ref[...], w_ref[...])

        @pl.when(pl.program_id(0) == 0)
        def _():
            out_ref[...] = part

        @pl.when(pl.program_id(0) > 0)
        def _():
            out_ref[...] += part

    return call(
        "normed_back_own", body, [d_queries, weights],
        [
            pl.BlockSpec((rows, block), lambda j: (0, j)),
            pl.BlockSpec((width, block), lambda j: (0, j)),
        ],
        [whole((rows, width))],
        [shape((rows, width), F32)],
        grid=(cols // block,),
    )[0]


def input_back(d_own, d_pack, tokens, gain, grad_middle):
    rows, width = tokens.shape

    def body(a_ref, b_ref, t_ref, gain_ref, gm_ref, out_ref, gg_ref):
        incoming = a_ref[...] + b_ref[...].astype(F32)
        back, terms = norm_back(t_ref[...].astype(F32), gain_ref[...], incoming)
        out_ref[...] = (gm_ref[...] + back).astype(BF16)
        gg_ref[...] = jnp.sum(terms, axis=0, keepdims=True)

    full = whole((rows, width))
    return call(
        "input_back", body, [d_own, d_pack, tokens, gain, grad_middle],
        [full, full, full, whole((1, width)), full],
        [full, whole((1, width))],
        [shape((rows, width), BF16), shape((1, width), F32)],
        grid=(1,),
    )


def weight_grad(left, right, owners=None, cols=None, block=512):
    tokens, rows = left.shape
    count = 1 if owners is None else owners.shape[0]
    unit = rows // count
    deep = right.ndim == 3
    first, each = cols or (0, right.shape[-1])
    width = each * (right.shape[0] if deep else 1)

    def body(*refs):
        if owners is not None:
            own_ref, refs = refs[0], refs[1:]
        l_ref, r_ref, refs = refs[0], refs[1], refs[2:]
        outs, scratch = refs[: -1 if owners is None else -2], refs[-1 if owners is None else -2 :]

        @pl.when(pl.program_id(0) == 0)
        def _():
            scratch[0][...] = l_ref[...].T
            for k in range(count if owners is not None else 0):
                at = pl.multiple_of(own_ref[k] * unit, unit)
                scratch[1][k * unit : (k + 1) * unit, :] = scratch[0][pl.ds(at, unit), :]

        full = mm(scratch[-1][...], r_ref[0] if deep else r_ref[...]).astype(BF16)
        if owners is None:
            outs[0][...] = full
        else:
            full = full.reshape(count, unit, block)
            outs[0][...] = full[: count // 2]
            outs[1][...] = full[count // 2 :]

    per, start = each // block, first // block
    if deep:
        right_spec = pl.BlockSpec((1, tokens, block), lambda j, *_: (j // per, 0, start + j % per))
    else:
        right_spec = pl.BlockSpec((tokens, block), lambda j, *_: (0, start + j))
    if owners is None:
        out = [pl.BlockSpec((rows, block), lambda j: (0, j))]
        out_shape = [shape((rows, width), BF16)]
    else:
        out = [pl.BlockSpec((count // 2, unit, block), lambda j, own: (0, 0, j))] * 2
        out_shape = [shape((count // 2, unit, width), BF16)] * 2
    return call(
        "weight_grad", body, [left, right], [whole((tokens, rows)), right_spec], out, out_shape,
        grid=(width // block,),
        scratch=[pltpu.VMEM((rows, tokens), BF16)] * (1 if owners is None else 2),
        prefetch=() if owners is None else [owners],
    )


def fold(items, steps=1):
    arrays = []

    def slot(term):
        for i, known in enumerate(arrays):
            if known is term:
                return i
        arrays.append(term)
        return len(arrays) - 1

    laid = [([slot(t) for t in terms], rows, bit) for terms, rows, bit in items]
    in_specs = []
    for a in arrays:
        in_specs.append(
            IN_VMEM if steps == 1 else pl.BlockSpec(a.shape[:2] + (a.shape[2] // steps,), lambda j: (0, 0, j))
        )
    out_specs, out_shape = [], []
    for slots, (_, rows), bit in laid:
        many, _, cols = arrays[slots[0]].shape
        dims = (many, rows, cols) if bit is None else (many // 2, rows, cols)
        for _ in range(1 if bit is None else 2):
            out_specs.append(
                IN_VMEM if steps == 1 else pl.BlockSpec(dims[:2] + (cols // steps,), lambda j: (0, 0, j))
            )
            out_shape.append(shape(dims, BF16))

    def body(*refs):
        ins, outs = refs[: len(arrays)], list(refs[len(arrays) :])
        for slots, (first, rows), bit in laid:
            here = slice(first, first + rows)
            many = arrays[slots[0]].shape[0]

            def total(k):
                value = ins[slots[0]][k, here, :].astype(F32)
                for at in slots[1:]:
                    value = value + ins[at][k, here, :].astype(F32)
                return value.astype(BF16)

            if bit is None:
                out = outs.pop(0)
                for k in range(many):
                    out[k] = total(k)
                continue
            sent, kept = outs.pop(0), outs.pop(0)
            places = [0, 0]
            for k in range(many):
                with_bit = (k >> bit) & 1
                (sent if with_bit else kept)[places[with_bit]] = total(k)
                places[with_bit] += 1

    return call("fold", body, arrays, in_specs, out_specs, out_shape, grid=(steps,))


def choose(first, second, dims, odd):
    arrays = [a for a, _ in first + second]
    views = [v for _, v in first + second]

    def body(odd_ref, *refs):
        ins, (sent, kept) = refs[: len(arrays)], refs[len(arrays) :]

        def total(begin, end):
            value = ins[begin][views[begin]].astype(F32)
            for at in range(begin + 1, end):
                value = value + ins[at][views[at]].astype(F32)
            return value.astype(BF16)

        @pl.when(odd_ref[0] == 1)
        def _():
            sent[...] = total(0, len(first))
            kept[...] = total(len(first), len(arrays))

        @pl.when(odd_ref[0] == 0)
        def _():
            kept[...] = total(0, len(first))
            sent[...] = total(len(first), len(arrays))

    return call(
        "choose", body, arrays, [IN_VMEM] * len(arrays), [IN_VMEM] * 2, [shape(dims, BF16)] * 2,
        prefetch=[odd],
    )


def place(sums, odd, out_dims, cuts):
    arrays = [a for pair in sums for a in pair]

    def body(odd_ref, *refs):
        ins, outs = refs[: len(arrays)], refs[len(arrays) :]

        def write(swapped):
            for which, half, source, at, target in cuts:
                outs[at][target] = ins[2 * which + (half ^ swapped)][source].astype(F32)

        @pl.when(odd_ref[0] == 1)
        def _():
            write(1)

        @pl.when(odd_ref[0] == 0)
        def _():
            write(0)

    return call(
        "place", body, arrays, [IN_VMEM] * len(arrays), [whole(d) for d in out_dims],
        [shape(d, F32) for d in out_dims], prefetch=[odd],
    )


def swap(x, axis, bit):
    size = lax.axis_size(axis)
    return lax.ppermute(x, axis, [(i, i ^ bit) for i in range(size)])


def bits_of(size):
    return [1 << b for b in range(size.bit_length() - 1)]


def gather_pieces(own, cut):
    rest = bits_of(lax.axis_size("dp"))[1:]
    spans = [slice(0, cut), slice(cut, own.shape[1])]
    everything = slice(0, own.shape[1])
    held = {0: [(everything, own)]}
    for bit in rest:
        held[bit] = [(everything, swap(own, "dp", bit))]
    first = [held[bit][0][1] for bit in rest]
    for at in range(1 << len(rest)):
        at = 2 * at
        if at in held:
            continue
        held[at] = []
        for span, order in zip(spans, (rest, rest[::-1])):
            last = [bit for bit in order if at & bit][-1]
            before = held[at ^ last]
            source = before[0][1][:, span] if len(before) == 1 else before[spans.index(span)][1]
            held[at].append((span, swap(source, "dp", last)))
    for at in sorted(held):
        held[at | 1] = [(span, swap(piece, "dp", 1)) for span, piece in held[at]]
    return held, first


class Sum:
    def __init__(self, kept, sent, halves, odd):
        self.rest = bits_of(lax.axis_size("dp"))[1:]
        self.order = [list(range(len(self.rest))), list(range(len(self.rest)))[::-1]]
        self.left = [list(range(len(self.rest))), list(range(len(self.rest)))]
        self.odd = odd
        arrived = [swap(s, "dp", 1) for s in sent]
        if len(kept) == 1:
            kept, arrived = kept * 2, arrived * 2
        self.terms = [[k, a] for k, a in zip(kept, arrived)]
        self.rows = halves
        self.stage = 0

    def over_dp(self, steps=1):
        bits = [order[self.stage] for order in self.order]
        items = [
            (terms, rows, left.index(bit))
            for terms, rows, left, bit in zip(self.terms, self.rows, self.left, bits)
        ]
        sent0, kept0, sent1, kept1 = fold(items, steps)
        self.terms = [
            [kept, swap(sent, "dp", self.rest[bit])]
            for kept, sent, bit in zip((kept0, kept1), (sent0, sent1), bits)
        ]
        self.rows = [(0, k.shape[1]) for k in (kept0, kept1)]
        for left, bit in zip(self.left, bits):
            left.remove(bit)
        self.stage += 1

    def to_ctx(self):
        first, second = [[(t, 0) for t in terms] for terms in self.terms]
        self.begin_ctx(first, second, first[0][0].shape[1:])

    def begin_ctx(self, first, second, dims):
        sent, kept = choose(first, second, dims, self.odd)
        self.total, self.next = [kept, swap(sent, "ctx", 1)], bits_of(lax.axis_size("ctx"))[1:]

    def over_ctx(self):
        a, b = [t[None] for t in self.total]
        total = fold([([a, b], (0, a.shape[1]), None)])[0][0]
        if self.next:
            self.total = [total, swap(total, "ctx", self.next.pop(0))]
        else:
            self.total = [total, swap(total, "ctx", 1)]


def sum_everywhere(x):
    for axis in ("dp", "ctx"):
        for bit in bits_of(lax.axis_size(axis)):
            x = x + swap(x, axis, bit)
    return x


def on_device(
    tokens, doc_starts, attn_gain, w_query, w_key, w_value, w_out,
    query_gain, key_gain, mlp_gain, w_gate, w_up, w_down, cotangent,
):
    ORDER.clear()
    rows, width = tokens.shape[1], tokens.shape[2]
    stretch = rows // 2
    ctx_size = lax.axis_size("ctx")
    dp_size = lax.axis_size("dp")
    ctx_at = lax.axis_index("ctx")
    dp_at = lax.axis_index("dp")
    pack_rows = rows * ctx_size
    unit = width // dp_size
    inner = HEADS * HEAD_DIM
    own_tokens = tokens[0]
    grad_out = cotangent[0]
    starts = doc_starts[0]
    odd = (ctx_at % 2).astype(jnp.int32)[None]
    dp_bits = bits_of(dp_size)

    gains = jnp.concatenate(
        [attn_gain[:, None], mlp_gain[:, None], jnp.zeros((unit, HEAD_DIM - 2), BF16)], axis=1
    )

    def packing(_, ins, outs):
        at = 0
        for ref in ins:
            yield ref.at[:, :], outs[0].at[:, pl.ds(at, ref.shape[1])]
            at += ref.shape[1]

    def stacking(_, ins, outs):
        down, gate, up, out = ins
        stack_ref = outs[0]
        yield down.at[:, :], stack_ref.at[pl.ds(0, 3 * unit)]
        for i in range(3):
            cols = pl.ds(i * width, width)
            yield gate.at[:, cols], stack_ref.at[pl.ds((3 + i) * unit, unit)]
            yield up.at[:, cols], stack_ref.at[pl.ds((6 + i) * unit, unit)]
        yield out.at[:, :], stack_ref.at[pl.ds(9 * unit, 2 * unit)]

    attn_cols = inner + 2 * width + HEAD_DIM
    own_attn = copies(
        "pack_attn", [w_query, w_key, w_value, gains], packing, [shape((unit, attn_cols), BF16)]
    )[0]
    pieces, first_pieces = gather_pieces(own_attn, inner)
    from_left, from_right = [], []
    for step in range(1, ctx_size):
        block = from_left[-1] if from_left else own_tokens
        from_left.append(
            lax.ppermute(block, "ctx", [(i, i + 1) for i in range(step - 1, ctx_size - 1)])
        )
        block = from_right[-1] if from_right else own_tokens
        from_right.append(
            lax.ppermute(block, "ctx", [(i + 1, i) for i in range(ctx_size - step)])
        )
    stack_in = copies(
        "pack_stack", [w_down, w_gate, w_up, w_out], stacking, [shape((11 * unit, width), BF16)]
    )[0]
    stack = lax.all_gather(stack_in, "dp", axis=0)
    touch([from_left[0], from_right[0]])
    touch(first_pieces)
    touch([from_left[1], from_right[1]])

    place_at = jnp.arange(pack_rows, dtype=jnp.int32)
    in_half = place_at % (pack_rows // 2)
    part, device, row = place_at // (pack_rows // 2), in_half // stretch, place_at % stretch
    key_stream = stream_index(device * rows + part * stretch + row, stretch, ctx_size)
    query_stream = stream_index(
        ctx_at * rows + jnp.arange(rows, dtype=jnp.int32), stretch, ctx_size
    )
    key_open = opening_of(key_stream, starts)
    query_open = opening_of(query_stream, starts)
    cos_pack, sin_pack = rotary(key_stream - key_open)
    cos_own, sin_own = rotary(query_stream - query_open)

    def doubled(v):
        return jnp.concatenate([v[:stretch]] * GROUPS + [v[stretch:]] * GROUPS)[None, :]

    owners = (dp_at ^ jnp.arange(dp_size, dtype=jnp.int32)).astype(jnp.int32)
    listed = [(k, span, piece) for k in range(dp_size) for span, piece in pieces[k]]

    def assembling(prefetch, ins, outs):
        for (k, span, _), ref in zip(listed, ins):
            at = pl.multiple_of(prefetch[0][k] * unit, unit)
            target = outs[0].at[pl.ds(at, unit), pl.ds(span.start, span.stop - span.start)]
            yield ref.at[:, :], target

    attn_w = copies(
        "assemble_weights", [piece for _, _, piece in listed], assembling,
        [shape((width, attn_cols), BF16)], prefetch=[owners],
    )[0]
    gain_rows = attn_w[:, inner + 2 * width :][:, :2].astype(F32).T
    gain_attn, gain_mlp = gain_rows[0:1], gain_rows[1:2]
    gain_query = query_gain.astype(F32)[None, :]
    gain_key = key_gain.astype(F32)[None, :]

    normed = norm_own(own_tokens, gain_attn)
    query_raw, queries = project_queries(normed, attn_w, gain_query, cos_own, sin_own)
    places = ((ctx_at - jnp.arange(ctx_size, dtype=jnp.int32)) % ctx_size).astype(jnp.int32)
    normed_pack = norm_pack(
        own_tokens, from_left, from_right, gain_attn, places, ctx_at.astype(jnp.int32)[None]
    ).reshape(pack_rows, width)
    key_raw, keys, values = project_keys_values(normed_pack, attn_w, gain_key, cos_pack, sin_pack)
    attended, mixed, lse = attend(
        queries, keys, values, query_open[:, None], query_stream[:, None], key_stream[None, :]
    )
    middle, normed_mid = project_out(mixed, stack, own_tokens, gain_mlp)
    hidden, slope_gate, slope_up = gate_up(normed_mid, stack)

    order = [2 * k for k in range(dp_size // 2)] + [2 * k + 1 for k in range(dp_size // 2)]
    owners = (dp_at ^ jnp.array(order, jnp.int32)).astype(jnp.int32)
    everything = slice(None)
    ctx_steps = len(bits_of(ctx_size))

    def two_rows(total, half):
        cuts = [(0, k, everything, 0, slice(k * half, (k + 1) * half)) for k in range(2)]
        return place([total.total], odd, [(2 * half, width)], cuts)[0]

    def halves_of(pair):
        half = pair[0].shape[1] // 2
        return Sum(pair[:1], pair[1:], [(0, half), (half, half)], odd), half

    later_dp, later_ctx = len(dp_bits) - 2, ctx_steps - 1
    down, down_half = halves_of(weight_grad(hidden, grad_out, owners, block=256))
    output, d_both = down_both(hidden, slope_gate, slope_up, grad_out, stack, middle)
    down.over_dp()
    wide_grad = weight_grad(normed_mid, d_both)[0]
    wide_grad = lax.psum_scatter(wide_grad, "dp", scatter_dimension=0, tiled=True)
    grad_middle, grad_branch, mlp_part = mlp_back(d_both, stack, middle, gain_mlp, grad_out)
    for _ in range(later_dp):
        down.over_dp()
    grad_mixed = mixed_back(grad_branch, stack)
    out, out_half = halves_of(weight_grad(mixed, grad_branch, owners, block=256))
    back_args = (
        queries, grad_mixed, attended, keys, values, lse,
        doubled(query_open), doubled(query_stream), key_stream[:, None],
        query_raw, key_raw, gain_query, gain_key, cos_own, sin_own, cos_pack, sin_pack,
    )
    quarter = KV_HEADS // 4
    gain_parts = []

    def attend_quarter(at, early):
        results = attend_back(*back_args, at * quarter, quarter, early)
        gain_parts.append(results[2:])
        return results[:2]

    def attention_grads(at):
        query = weight_grad(normed, d_query, owners, (at * inner // 2, inner // 2))
        pair = weight_grad(normed_pack, d_pair, owners, (at * width // 2, width // 2))
        return Sum([query[0], pair[0]], [query[1], pair[1]], [(0, unit), (0, unit)], odd)

    early = attend_quarter(0, ())
    down.to_ctx()
    out.over_dp()
    d_query, d_pair = attend_quarter(1, early)
    down.over_ctx()
    for _ in range(later_dp):
        out.over_dp()
    attn_one = attention_grads(0)
    early = attend_quarter(2, (d_query, d_pair))
    for _ in range(later_ctx):
        down.over_ctx()
    out.to_ctx()
    attn_one.over_dp()
    d_query, d_pair = attend_quarter(3, early)
    d_normed = normed_back_pack(d_pair, attn_w, ctx_size)
    d_normed = lax.psum_scatter(d_normed, "ctx", scatter_dimension=0, tiled=True)
    for _ in range(later_dp):
        attn_one.over_dp()
    out.over_ctx()
    attn_two = attention_grads(1)
    down_grad = two_rows(down, down_half)
    wide = Sum([], [], None, odd)
    wide.begin_ctx(
        [(wide_grad, (everything, slice(0, 3 * width)))],
        [(wide_grad, (everything, slice(3 * width, 6 * width)))],
        (unit, 3 * width),
    )
    attn_one.to_ctx()
    attn_two.over_dp()
    d_own = normed_back_own(d_query, attn_w)
    for _ in range(later_ctx):
        out.over_ctx()
    for _ in range(later_dp):
        attn_two.over_dp()
    wide.over_ctx()
    attn_one.over_ctx()
    w_out_grad = two_rows(out, out_half)
    attn_two.to_ctx()
    for _ in range(later_ctx):
        wide.over_ctx()
        attn_one.over_ctx()
    attn_two.over_ctx()
    input_grad, attn_part = input_back(d_own, d_normed, own_tokens, gain_attn, grad_middle)
    gate_grad, up_grad = place(
        [wide.total], odd, [(unit, 3 * width)] * 2, [(0, k, everything, k, everything) for k in range(2)]
    )
    for _ in range(ctx_steps - 1):
        attn_two.over_ctx()
    cuts = []
    for at in range(2):
        near, far = slice(0, width // 2), slice(width // 2, width)
        cuts.append((at, 0, everything, 0, (everything, slice(at * inner // 2, (at + 1) * inner // 2))))
        cuts.append((at, 1, (everything, near), 1, (everything, (near, far)[at])))
        cuts.append((at, 1, (everything, far), 2, (everything, (near, far)[at])))
    query_grad, key_grad, value_grad = place(
        [attn_one.total, attn_two.total], odd, [(unit, inner), (unit, width), (unit, width)], cuts
    )
    query_part, key_part = [sum(parts[1:], parts[0]) for parts in zip(*gain_parts)]

    parts = [attn_part, mlp_part, query_part, key_part]
    small = sum_everywhere(jnp.concatenate(parts, axis=1).reshape(-1, HEAD_DIM)).reshape(-1)
    attn_gain_grad = lax.dynamic_slice(small, (dp_at * unit,), (unit,))
    mlp_gain_grad = lax.dynamic_slice(small, (width + dp_at * unit,), (unit,))
    query_gain_grad = small[2 * width : 2 * width + HEAD_DIM]
    key_gain_grad = small[2 * width + HEAD_DIM :]
    return (
        output[None], input_grad[None], attn_gain_grad, query_grad, key_grad, value_grad, w_out_grad,
        query_gain_grad, key_gain_grad, mlp_gain_grad, gate_grad, up_grad, down_grad,
    )


def solution(mesh):
    in_specs = (
        P("dp", "ctx", None),
        P("dp", None),
        P("dp"),
        P("dp", None),
        P("dp", None),
        P("dp", None),
        P("dp", None),
        P(),
        P(),
        P("dp"),
        P("dp", None),
        P("dp", None),
        P("dp", None),
        P("dp", "ctx", None),
    )
    out_specs = (
        P("dp", "ctx", None),
        P("dp", "ctx", None),
        P("dp"),
        P("dp", None),
        P("dp", None),
        P("dp", None),
        P("dp", None),
        P(),
        P(),
        P("dp"),
        P("dp", None),
        P("dp", None),
        P("dp", None),
    )
    return jax.shard_map(
        on_device, mesh=mesh, in_specs=in_specs, out_specs=out_specs, check_vma=False
    )
```

time: 1260 us -> 588 us (0.47)
  waiting for transfers between devices: 771 us -> 156 us
  Pallas kernels: 0 us -> 265 us
  matrix products: 226 us -> 0 us
  blocking collectives: 86.2 us -> 0 us
  starting transfers between devices: 1.4 us -> 79 us
  other arithmetic: 59 us -> 11.1 us
  local copies, waits for them, and re-layouts: 93.7 us -> 54.4 us
    reduce_scatter x9 -> x2, waiting for transfers between devices: 457 us -> 0.02 us  [the longest x1 0.02 us: on_device(): lax.psum_scatter(d_normed, 'ctx', scatter_dimension=0, tiled=True)]
    pallas_call x0 -> x57, Pallas kernels: none -> 265 us  [call(): pl.pallas_call(without, grid_spec=pltpu.PrefetchScalarGridSpec(num_scalar...]
    all_gather x9 -> x1, waiting for transfers between devices: 244 us -> 0.01 us  [on_device(): stack = lax.all_gather(stack_in, 'dp', axis=0)]
    dot_general x42 -> x0, matrix products: 226 us -> none  [the longest x6 32.5 us: scores_of(): jnp.einsum('tgjd,kgd->gjtk', queries, key_block, preferred_element_type=j...]
    ppermute x0 -> x57, waiting for transfers between devices: none -> 156 us  [the longest x51 149 us: swap(): return lax.ppermute(x, axis, [(i, i ^ bit) for i in range(size)])]
    ppermute x0 -> x57, starting transfers between devices: none -> 78.9 us  [the longest x51 65.4 us: swap(): return lax.ppermute(x, axis, [(i, i ^ bit) for i in range(size)])]
    psum x1 -> x0, waiting for transfers between devices: 66 us -> none  [on_device(): lax.psum(part_query.astype(jnp.bfloat16), 'ctx').astype(jnp.float32)]
    psum x2 -> x0, blocking collectives: 53.2 us -> none  [the longest x1 40.7 us: on_device(): lax.psum((jnp.sum(query_terms, axis=(0, 1)), jnp.sum(key_gain_terms, axis...]
  transfers between devices with their start and end apart: 19 -> 60, of which waited for: 17 -> 22; matrix products, arithmetic and copies ran while one was open for 16% -> 2% of each run, Pallas kernels for 0% -> 37%
where the time goes in v1:
time: 588 us; the launch traced here: 581 us
  Pallas kernels  265 us (45%)
  waiting for transfers between devices  156 us (27%)
  starting transfers between devices  79 us (13%)
  local copies, waits for them, and re-layouts  54.4 us (9%)
  between operations  15 us (3%)
  other arithmetic  11.1 us (2%)
    pallas_call x57, Pallas kernels, call(): pl.pallas_call(without, grid_spec=pltpu.PrefetchScalarGridSpec(num_scalar...  265 us
    ppermute x51, waiting for transfers between devices, swap(): return lax.ppermute(x, axis, [(i, i ^ bit) for i in range(size)])  149 us
    ppermute x51, starting transfers between devices, swap(): return lax.ppermute(x, axis, [(i, i ^ bit) for i in range(size)])  65.4 us
    unnamed x163, local copies, waits for them, and re-layouts  49.4 us
  transfers between devices with their start and end apart: 60, of which 22 were waited for; matrix products, arithmetic and copies ran while one was open for 2% of the time, Pallas kernels for 37%

profile of v1, /device:TPU:0, one launch (start us, length us, event | category | flops | bytes accessed | tf_op | source)
XLA Modules:
  0.0 580.7 jit_solution(14140921514340529258)
XLA Ops:
  18.4 6.5 %collective-permute-start.9 = (bf16[384,1024]{1,0:T(8,128)(2,1)S(1)}, bf16[384,1024]{1,0:T(8,128)(2,1)}, u32[]{:S(2)}, u32[]{:S(2)}) collective-permute-start(bf16[384,1024]{1,0:T(8,128)(2,1)S(1)} %bitcast.56), channel_id=1, source_target_pairs={{0,1},{1,2},{2,3},{4,5},{5,6},{6,7},{8,9},{9,10},{10,11},{12,13},{... | collective-permute-start | bytes 2359304 | tf_op jit(solution)/shard_map/ppermute | solution.py:970
  33.1 7.7 %collective-permute-done.9.refs_1_.refs_4_ = bf16[384,1024]{1,0:T(8,128)(2,1)} collective-permute-done((bf16[384,1024]{1,0:T(8,128)(2,1)S(1)}, bf16[384,1024]{1,0:T(8,128)(2,1)}, u32[]{:S(2)}, u32[]{:S(2)}) %collective-permute-start.9) | collective-permute-done | bytes 786464 | tf_op jit(solution)/shard_map/ppermute | solution.py:970
  42.3 28.7 %collective-permute-done.1.refs_1_.refs_3_ = bf16[128,4224]{1,0:T(8,128)(2,1)} collective-permute-done((bf16[128,4224]{1,0:T(8,128)(2,1)S(1)}, bf16[128,4224]{1,0:T(8,128)(2,1)}, u32[]{:S(2)}, u32[]{:S(2)}) %collective-permute-start.1) | collective-permute-done | bytes 1081376 | tf_op jit(solution)/shard_map/ppermute | solution.py:838
  78.2 15.5 %collective-permute-done.5.refs_7_ = bf16[128,2048]{1,0:T(8,128)(2,1)S(1)} collective-permute-done((bf16[128,2048]{1,0:T(8,128)(2,1)S(1)}, bf16[128,2048]{1,0:T(8,128)(2,1)S(1)}, u32[]{:S(2)}, u32[]{:S(2)}) %collective-permute-start.5) | collective-permute-done | bytes 524320 | tf_op jit(solution)/shard_map/ppermute | solution.py:838
  112.8 9.6 %project_queries.1 = (f32[384,2048]{1,0:T(8,128)}, bf16[384,2048]{1,0:T(8,128)(2,1)}) custom-call(bf16[384,1024]{1,0:T(8,128)(2,1)} %copy-done.7, bf16[1024,4224]{1,0:T(8,128)(2,1)} %copy-done, f32[1,128]{1,0:T(1,128)S(1)} %bitcast_convert_fusion.1.refs_2_.refs_11_, f32[384,128]{1,0:T(8,128)S(1)} %get-tuple-element.221.refs_3_.refs_13_, ...), custom_call_target="tpu_custom_call" | custom-call | tf_op jit(solution)/shard_map/project_queries/pallas_call | solution.py:60
  124.4 5.7 norm_pack.1.refs_6_
  130.1 28.4 %project_keys_values.1 = (f32[1536,1024]{1,0:T(8,128)}, bf16[1536,1024]{1,0:T(8,128)(2,1)}, bf16[1536,1024]{1,0:T(8,128)(2,1)}) custom-call(bf16[1536,1024]{1,0:T(8,128)(2,1)} %bitcast.100, bf16[1024,4224]{1,0:T(8,128)(2,1)} %copy-done, bf16[1024,4224]{1,0:T(8,128)(2,1)} %copy-done, f32[1,128]{1,0:T(1,128)S(1)} %copy-done.50, ...), custom_call_target="tpu_custom_call" | custom-call | tf_op jit(solution)/shard_map/project_keys_values/pallas_call | solution.py:60
  161.3 19.9 %attend.1 = (f32[384,2048]{1,0:T(8,128)}, bf16[384,2048]{1,0:T(8,128)(2,1)}, f32[8,8,768]{2,1,0:T(8,128)S(1)}) custom-call(bf16[384,2048]{1,0:T(8,128)(2,1)} %get-tuple-element.108.refs_0_, bf16[1536,1024]{1,0:T(8,128)(2,1)} %get-tuple-element.110.refs_1_.refs_3_, bf16[1536,1024]{1,0:T(8,128)(2,1)} %get-tuple-element.111.refs_2_.refs_4_, ...), custom_call_target="tpu_custom_call" | custom-call | tf_op jit(solution)/shard_map/attend/pallas_call | solution.py:60
  181.3 6.7 %project_out.1 = (f32[384,1024]{1,0:T(8,128)}, bf16[384,1024]{1,0:T(8,128)(2,1)}) custom-call(bf16[384,2048]{1,0:T(8,128)(2,1)} %get-tuple-element.113.refs_0_.refs_1_, bf16[8,1408,1024]{2,1,0:T(8,128)(2,1)} %bitcast.90, bf16[8,1408,1024]{2,1,0:T(8,128)(2,1)} %bitcast.91, bf16[384,1024]{1,0:T(8,128)(2,1)} %bitcast.53, ...), custom_call_target="tpu_custom_call" | custom-call | tf_op jit(solution)/shard_map/project_out/pallas_call | solution.py:60
  189.3 14.9 %gate_up.1 = (bf16[384,3072]{1,0:T(8,128)(2,1)}, bf16[384,3072]{1,0:T(8,128)(2,1)}, bf16[384,3072]{1,0:T(8,128)(2,1)}) custom-call(bf16[384,1024]{1,0:T(8,128)(2,1)} %get-tuple-element.115.refs_0_, bf16[8,1408,1024]{2,1,0:T(8,128)(2,1)} %bitcast.92, bf16[8,1408,1024]{2,1,0:T(8,128)(2,1)} %bitcast.93, f32[384,1024]{1,0:T(8,128)S(1)} %copy-done.8), custom_call_target="tpu_custom_call" | custom-call | tf_op jit(solution)/shard_map/gate_up/pallas_call | solution.py:60
  204.2 8.7 %weight_grad.7 = (bf16[4,384,1024]{2,1,0:T(8,128)(2,1)}, bf16[4,384,1024]{2,1,0:T(8,128)(2,1)}) custom-call(s32[8]{0:T(128)S(1)} %get-tuple-element.220.refs_0_, bf16[384,3072]{1,0:T(8,128)(2,1)} %get-tuple-element.117.refs_1_.refs_3_.refs_0_, bf16[384,1024]{1,0:T(8,128)(2,1)} %bitcast.103, bf16[384,3072]{1,0:T(8,128)(2,1)} %get-tuple-element.117.refs_1_.refs_3_.refs_0_), custom_call_target="tpu_custom_call" | custom-call | tf_op jit(solution)/shard_map/weight_grad/pallas_call | solution.py:60
  214.8 14.7 %down_both.1 = (bf16[384,1024]{1,0:T(8,128)(2,1)}, bf16[2,384,3072]{2,1,0:T(8,128)(2,1)}) custom-call(bf16[384,3072]{1,0:T(8,128)(2,1)} %get-tuple-element.117.refs_1_.refs_3_.refs_0_, bf16[384,3072]{1,0:T(8,128)(2,1)} %get-tuple-element.118.refs_1_, bf16[384,3072]{1,0:T(8,128)(2,1)} %get-tuple-element.119.refs_2_, bf16[384,1024]{1,0:T(8,128)(2,1)} %bitcast.104, ...), custom_call_target="tpu_custom_call" | custom-call | tf_op jit(solution)/shard_map/down_both/pallas_call | solution.py:60
  233.0 14.6 %weight_grad.8.refs_6_ = bf16[1024,6144]{1,0:T(8,128)(2,1)} custom-call(bf16[384,1024]{1,0:T(8,128)(2,1)} %get-tuple-element.115.refs_0_, bf16[2,384,3072]{2,1,0:T(8,128)(2,1)} %get-tuple-element.122.refs_1_.refs_0_, bf16[2,192,1024]{2,1,0:T(8,128)(2,1)S(1)} %get-tuple-element.124.refs_2_), custom_call_target="tpu_custom_call" | custom-call | tf_op jit(solution)/shard_map/weight_grad/pallas_call | solution.py:60
  249.9 5.5 copy-done.3
  255.4 15.8 %mlp_back.1 = (f32[384,1024]{1,0:T(8,128)}, bf16[384,1024]{1,0:T(8,128)(2,1)}, f32[1,1024]{1,0:T(1,128)S(1)}) custom-call(bf16[2,384,3072]{2,1,0:T(8,128)(2,1)} %get-tuple-element.122.refs_1_.refs_0_, bf16[8,1408,1024]{2,1,0:T(8,128)(2,1)} %bitcast.95, bf16[8,1408,1024]{2,1,0:T(8,128)(2,1)} %bitcast.96, f32[384,1024]{1,0:T(8,128)} %get-tuple-element.116.refs_3_.refs_5_, ...), custom_call_target="tpu_custom_call" | custom-call | tf_op jit(solution)/shard_map/mlp_back/pallas_call | solution.py:60
  272.3 7.8 %mixed_back.1.refs_3_.refs_1_ = bf16[384,2048]{1,0:T(8,128)(2,1)} custom-call(bf16[384,1024]{1,0:T(8,128)(2,1)} %get-tuple-element.125.refs_0_.refs_2_, bf16[8,1408,1024]{2,1,0:T(8,128)(2,1)} %bitcast.97, bf16[8,1408,1024]{2,1,0:T(8,128)(2,1)} %bitcast.98, bf16[1,192,1024]{2,1,0:T(8,128)(2,1)S(1)} %get-tuple-element.130.refs_3_), custom_call_target="tpu_custom_call" | custom-call | tf_op jit(solution)/shard_map/mixed_back/pallas_call | solution.py:60
  281.5 6.8 %weight_grad.9 = (bf16[4,256,1024]{2,1,0:T(8,128)(2,1)}, bf16[4,256,1024]{2,1,0:T(8,128)(2,1)}) custom-call(s32[8]{0:T(128)S(1)} %get-tuple-element.220.refs_0_, bf16[384,2048]{1,0:T(8,128)(2,1)} %get-tuple-element.113.refs_0_.refs_1_, bf16[384,1024]{1,0:T(8,128)(2,1)} %get-tuple-element.125.refs_0_.refs_2_, bf16[384,2048]{1,0:T(8,128)(2,1)S(1)} %copy-done.5), custom_call_target="tpu_custom_call" | custom-call | tf_op jit(solution)/shard_map/weight_grad/pallas_call | solution.py:60
  292.9 11.5 %attend_back.4 = (bf16[384,2048]{1,0:T(8,128)(2,1)}, bf16[2,1536,1024]{2,1,0:T(8,128)(2,1)}, f32[1,128]{1,0:T(1,128)S(1)}, f32[1,128]{1,0:T(1,128)S(1)}) custom-call(bf16[384,2048]{1,0:T(8,128)(2,1)} %get-tuple-element.108.refs_0_, bf16[384,2048]{1,0:T(8,128)(2,1)} %mixed_back.1.refs_3_.refs_1_, f32[384,2048]{1,0:T(8,128)} %get-tuple-element.131.refs_2_, ...), custom_call_target="tpu_custom_call" | custom-call | tf_op jit(solution)/shard_map/attend_back/pallas_call | solution.py:60
  317.8 11.3 %attend_back.5 = (bf16[384,2048]{1,0:T(8,128)(2,1)}, bf16[2,1536,1024]{2,1,0:T(8,128)(2,1)}, f32[1,128]{1,0:T(1,128)S(1)}, f32[1,128]{1,0:T(1,128)S(1)}) custom-call(bf16[384,2048]{1,0:T(8,128)(2,1)} %get-tuple-element.108.refs_0_, bf16[384,2048]{1,0:T(8,128)(2,1)} %mixed_back.1.refs_3_.refs_1_, ...), custom_call_target="tpu_custom_call", output_to_operand_aliasing={{0}: (17, {}), {1}: (18, {})} | custom-call | tf_op jit(solution)/shard_map/attend_back/pallas_call | solution.py:60
  338.5 8.5 %weight_grad.11 = (bf16[4,128,1024]{2,1,0:T(8,128)(2,1)}, bf16[4,128,1024]{2,1,0:T(8,128)(2,1)}) custom-call(s32[8]{0:T(128)S(1)} %get-tuple-element.220.refs_0_, bf16[1536,1024]{1,0:T(8,128)(2,1)} %bitcast.101, bf16[2,1536,1024]{2,1,0:T(8,128)(2,1)} %get-tuple-element.143.refs_2_.refs_18_, bf16[4,128,1024]{2,1,0:T(8,128)(2,1)S(1)} %copy-done.22), custom_call_target="tpu_custom_call" | custom-call | tf_op jit(solution)/shard_map/weight_grad/pallas_call | solution.py:60
  353.5 11.4 %attend_back.6 = (bf16[384,2048]{1,0:T(8,128)(2,1)}, bf16[2,1536,1024]{2,1,0:T(8,128)(2,1)}, f32[1,128]{1,0:T(1,128)S(1)}, f32[1,128]{1,0:T(1,128)S(1)}) custom-call(bf16[384,2048]{1,0:T(8,128)(2,1)} %get-tuple-element.108.refs_0_, bf16[384,2048]{1,0:T(8,128)(2,1)} %mixed_back.1.refs_3_.refs_1_, ...), custom_call_target="tpu_custom_call", output_to_operand_aliasing={{0}: (17, {}), {1}: (18, {})} | custom-call | tf_op jit(solution)/shard_map/attend_back/pallas_call | solution.py:60
  369.1 11.9 %attend_back.7 = (bf16[384,2048]{1,0:T(8,128)(2,1)}, bf16[2,1536,1024]{2,1,0:T(8,128)(2,1)}, f32[1,128]{1,0:T(1,128)S(1)}, f32[1,128]{1,0:T(1,128)S(1)}) custom-call(bf16[384,2048]{1,0:T(8,128)(2,1)} %get-tuple-element.108.refs_0_, bf16[384,2048]{1,0:T(8,128)(2,1)} %mixed_back.1.refs_3_.refs_1_, ...), custom_call_target="tpu_custom_call", output_to_operand_aliasing={{0}: (17, {}), {1}: (18, {})} | custom-call | tf_op jit(solution)/shard_map/attend_back/pallas_call | solution.py:60
  381.7 11.0 %normed_back_pack.1.refs_4_ = bf16[1536,1024]{1,0:T(8,128)(2,1)} custom-call(bf16[2,2,4,192,1024]{4,3,2,1,0:T(8,128)(2,1)} %bitcast.99, bf16[1024,4224]{1,0:T(8,128)(2,1)} %copy-done, bf16[1024,4224]{1,0:T(8,128)(2,1)} %copy-done, f32[1,128]{1,0:T(1,128)S(1)} %get-tuple-element.168.refs_3_), custom_call_target="tpu_custom_call" | custom-call | tf_op jit(solution)/shard_map/normed_back_pack/pallas_call | solution.py:60
  395.6 10.4 %collective-permute-done.30.refs_1_ = bf16[2,128,1024]{2,1,0:T(8,128)(2,1)S(1)} collective-permute-done((bf16[2,128,1024]{2,1,0:T(8,128)(2,1)}, bf16[2,128,1024]{2,1,0:T(8,128)(2,1)S(1)}, u32[]{:S(2)}, u32[]{:S(2)}) %collective-permute-start.30) | collective-permute-done | bytes 524320 | tf_op jit(solution)/shard_map/ppermute | solution.py:838
  415.9 8.5 %weight_grad.13 = (bf16[4,128,1024]{2,1,0:T(8,128)(2,1)}, bf16[4,128,1024]{2,1,0:T(8,128)(2,1)}) custom-call(s32[8]{0:T(128)S(1)} %get-tuple-element.220.refs_0_, bf16[1536,1024]{1,0:T(8,128)(2,1)} %bitcast.102, bf16[2,1536,1024]{2,1,0:T(8,128)(2,1)} %get-tuple-element.167.refs_2_, bf16[4,128,1024]{2,1,0:T(8,128)(2,1)S(1)} %copy-done.20), custom_call_target="tpu_custom_call" | custom-call | tf_op jit(solution)/shard_map/weight_grad/pallas_call | solution.py:60
  428.3 25.5 %collective-permute-done.36.refs_2_ = bf16[192,1024]{1,0:T(8,128)(2,1)S(1)} collective-permute-done((bf16[192,1024]{1,0:T(8,128)(2,1)S(1)}, bf16[192,1024]{1,0:T(8,128)(2,1)S(1)}, u32[]{:S(2)}, u32[]{:S(2)}) %collective-permute-start.36) | collective-permute-done | bytes 393248 | tf_op jit(solution)/shard_map/ppermute | solution.py:838
  466.8 5.2 normed_back_own.1.refs_2_.refs_0_
  472.0 10.7 %collective-permute-done.39 = bf16[128,1024]{1,0:T(8,128)(2,1)S(1)} collective-permute-done((bf16[128,1024]{1,0:T(8,128)(2,1)S(1)}, bf16[128,1024]{1,0:T(8,128)(2,1)S(1)}, u32[]{:S(2)}, u32[]{:S(2)}) %collective-permute-start.39) | collective-permute-done | bytes 262176 | tf_op jit(solution)/shard_map/ppermute | solution.py:838
  491.8 19.9 %collective-permute-done.43 = bf16[128,1024]{1,0:T(8,128)(2,1)S(1)} collective-permute-done((bf16[128,1024]{1,0:T(8,128)(2,1)S(1)}, bf16[128,1024]{1,0:T(8,128)(2,1)S(1)}, u32[]{:S(2)}, u32[]{:S(2)}) %collective-permute-start.43) | collective-permute-done | bytes 262176 | tf_op jit(solution)/shard_map/ppermute | solution.py:838
  511.7 4.6 collective-permute-start.46
  522.3 6.7 %collective-permute-done.47 = bf16[128,3072]{1,0:T(8,128)(2,1)S(1)} collective-permute-done((bf16[128,3072]{1,0:T(8,128)(2,1)S(1)}, bf16[128,3072]{1,0:T(8,128)(2,1)S(1)}, u32[]{:S(2)}, u32[]{:S(2)}) %collective-permute-start.47) | collective-permute-done | bytes 786464 | tf_op jit(solution)/shard_map/ppermute | solution.py:838
  556.8 5.7 collective-permute-start.53
  (355 shorter events, 185.7 us)
Async XLA Ops:
  7.2 174.1 %all-gather.3.cloned.1.call-start = ((), (), s32[]{:S(2)}) async-start(), calls=%async_computation.4 | async-start | bytes 25952256 | tf_op jit(solution)/shard_map/all_gather | solution.py:979
  16.0 440.2 %reduce-scatter.3.cloned.1.call-start = ((), (), s32[]{:S(2)}) async-start(), calls=%async_computation.2 | async-start | bytes 14155776 | tf_op jit(solution)/shard_map/reduce_scatter | solution.py:1048
  17.1 56.7 %collective-permute-start.10 = (bf16[384,1024]{1,0:T(8,128)(2,1)S(1)}, bf16[384,1024]{1,0:T(8,128)(2,1)}, u32[]{:S(2)}, u32[]{:S(2)}) collective-permute-start(bf16[384,1024]{1,0:T(8,128)(2,1)S(1)} %bitcast.55), channel_id=1, source_target_pairs={{1,0},{2,1},{3,2},{5,4},{6,5},{7,6},{9,8},{10,9},{11,10},{13,12},{... | collective-permute-start | bytes 2359304 | tf_op jit(solution)/shard_map/ppermute | solution.py:974
  18.4 22.3 %collective-permute-start.9 = (bf16[384,1024]{1,0:T(8,128)(2,1)S(1)}, bf16[384,1024]{1,0:T(8,128)(2,1)}, u32[]{:S(2)}, u32[]{:S(2)}) collective-permute-start(bf16[384,1024]{1,0:T(8,128)(2,1)S(1)} %bitcast.56), channel_id=1, source_target_pairs={{0,1},{1,2},{2,3},{4,5},{5,6},{6,7},{8,9},{9,10},{10,11},{12,13},{... | collective-permute-start | bytes 2359304 | tf_op jit(solution)/shard_map/ppermute | solution.py:970
  24.8 46.1 %collective-permute-start.1 = (bf16[128,4224]{1,0:T(8,128)(2,1)S(1)}, bf16[128,4224]{1,0:T(8,128)(2,1)}, u32[]{:S(2)}, u32[]{:S(2)}) collective-permute-start(bf16[128,4224]{1,0:T(8,128)(2,1)S(1)} %pack_attn.1.refs_4_.refs_1_), channel_id=1, source_target_pairs={{0,8},{4,12},{8,0},{12,4},{16,24},{20,28},{24,16},{28,20},{1,9},{5... | collective-permute-start | bytes 3244040 | tf_op jit(solution)/shard_map/ppermute | solution.py:838
  26.8 48.3 %collective-permute-start.3 = (bf16[128,4224]{1,0:T(8,128)(2,1)S(1)}, bf16[128,4224]{1,0:T(8,128)(2,1)S(1)}, u32[]{:S(2)}, u32[]{:S(2)}) collective-permute-start(bf16[128,4224]{1,0:T(8,128)(2,1)S(1)} %pack_attn.1.refs_4_.refs_1_), channel_id=1, source_target_pairs={{0,16},{4,20},{8,24},{12,28},{16,0},{20,4},{24,8},{28,12},{1,17},{... | collective-permute-start | bytes 3244040 | tf_op jit(solution)/shard_map/ppermute | solution.py:838
  28.3 49.3 %collective-permute-start = (bf16[128,4224]{1,0:T(8,128)(2,1)S(1)}, bf16[128,4224]{1,0:T(8,128)(2,1)}, u32[]{:S(2)}, u32[]{:S(2)}) collective-permute-start(bf16[128,4224]{1,0:T(8,128)(2,1)S(1)} %pack_attn.1.refs_4_.refs_1_), channel_id=1, source_target_pairs={{0,4},{4,0},{8,12},{12,8},{16,20},{20,16},{24,28},{28,24},{1,5},{5... | collective-permute-start | bytes 3244040 | tf_op jit(solution)/shard_map/ppermute | solution.py:838
  40.7 37.0 %collective-permute-start.11 = (bf16[384,1024]{1,0:T(8,128)(2,1)}, bf16[384,1024]{1,0:T(8,128)(2,1)}, u32[]{:S(2)}, u32[]{:S(2)}) collective-permute-start(bf16[384,1024]{1,0:T(8,128)(2,1)} %collective-permute-done.9.refs_1_.refs_4_), channel_id=1, source_target_pairs={{1,2},{2,3},{5,6},{6,7},{9,10},{10,11},{13,14},{14,15},{17,18},{18... | collective-permute-start | bytes 2359304 | tf_op jit(solution)/shard_map/ppermute | solution.py:970
  72.0 21.6 %collective-permute-start.5 = (bf16[128,2048]{1,0:T(8,128)(2,1)S(1)}, bf16[128,2048]{1,0:T(8,128)(2,1)S(1)}, u32[]{:S(2)}, u32[]{:S(2)}) collective-permute-start(bf16[128,2048]{1,0:T(8,128)(2,1)S(1)} %slice.56), channel_id=1, source_target_pairs={{0,16},{4,20},{8,24},{12,28},{16,0},{20,4},{24,8},{28,12},{1,17},{... | collective-permute-start | bytes 1572872 | tf_op jit(solution)/shard_map/ppermute | solution.py:838
  73.8 22.2 %collective-permute-start.12 = (bf16[384,1024]{1,0:T(8,128)(2,1)}, bf16[384,1024]{1,0:T(8,128)(2,1)}, u32[]{:S(2)}, u32[]{:S(2)}) collective-permute-start(bf16[384,1024]{1,0:T(8,128)(2,1)} %collective-permute-done.10.refs_2_.refs_7_), channel_id=1, source_target_pairs={{1,0},{2,1},{5,4},{6,5},{9,8},{10,9},{13,12},{14,13},{17,16},{18,1... | collective-permute-start | bytes 2359304 | tf_op jit(solution)/shard_map/ppermute | solution.py:974
  77.6 24.2 %collective-permute-start.2 = (bf16[128,4224]{1,0:T(8,128)(2,1)}, bf16[128,4224]{1,0:T(8,128)(2,1)S(1)}, u32[]{:S(2)}, u32[]{:S(2)}) collective-permute-start(bf16[128,4224]{1,0:T(8,128)(2,1)} %collective-permute-done.1.refs_1_.refs_3_), channel_id=1, source_target_pairs={{0,4},{4,0},{8,12},{12,8},{16,20},{20,16},{24,28},{28,24},{1,5},{5... | collective-permute-start | bytes 3244040 | tf_op jit(solution)/shard_map/ppermute | solution.py:838
  77.7 24.1 %collective-permute-start.4 = (bf16[128,4224]{1,0:T(8,128)(2,1)S(1)}, bf16[128,4224]{1,0:T(8,128)(2,1)S(1)}, u32[]{:S(2)}, u32[]{:S(2)}) collective-permute-start(bf16[128,4224]{1,0:T(8,128)(2,1)S(1)} %collective-permute-done.3.refs_2_.refs_5_), channel_id=1, source_target_pairs={{0,4},{4,0},{8,12},{12,8},{16,20},{20,16},{24,28},{28,24},{1,5},{5... | collective-permute-start | bytes 3244040 | tf_op jit(solution)/shard_map/ppermute | solution.py:838
  96.0 26.4 %collective-permute-start.13 = (bf16[384,1024]{1,0:T(8,128)(2,1)}, bf16[384,1024]{1,0:T(8,128)(2,1)}, u32[]{:S(2)}, u32[]{:S(2)}) collective-permute-start(bf16[384,1024]{1,0:T(8,128)(2,1)} %collective-permute-done.11.refs_1_.refs_5_), channel_id=1, source_target_pairs={{2,3},{6,7},{10,11},{14,15},{18,19},{22,23},{26,27},{30,31}} | collective-permute-start | bytes 2359304 | tf_op jit(solution)/shard_map/ppermute | solution.py:970
  97.5 24.9 %collective-permute-start.14 = (bf16[384,1024]{1,0:T(8,128)(2,1)}, bf16[384,1024]{1,0:T(8,128)(2,1)}, u32[]{:S(2)}, u32[]{:S(2)}) collective-permute-start(bf16[384,1024]{1,0:T(8,128)(2,1)} %collective-permute-done.12.refs_2_.refs_8_), channel_id=1, source_target_pairs={{1,0},{5,4},{9,8},{13,12},{17,16},{21,20},{25,24},{29,28}} | collective-permute-start | bytes 2359304 | tf_op jit(solution)/shard_map/ppermute | solution.py:974
  247.7 290.1 %reduce-scatter.5.cloned.1.call-start = ((), (), s32[]{:S(2)}) async-start(), calls=%async_computation.3 | async-start | bytes 3932160 | tf_op jit(solution)/shard_map/reduce_scatter | solution.py:1087
  247.7 23.5 %collective-permute-start.16 = (bf16[2,192,1024]{2,1,0:T(8,128)(2,1)S(1)}, bf16[2,192,1024]{2,1,0:T(8,128)(2,1)S(1)}, u32[]{:S(2)}, u32[]{:S(2)}) collective-permute-start(bf16[2,192,1024]{2,1,0:T(8,128)(2,1)S(1)} %get-tuple-element.124.refs_2_), channel_id=1, source_target_pairs={{0,8},{4,12},{8,0},{12,4},{16,24},{20,28},{24,16},{28,20},{1,9},{5... | collective-permute-start | bytes 2359304 | tf_op jit(solution)/shard_map/ppermute | solution.py:838
  247.9 23.2 %collective-permute-start.17 = (bf16[2,192,1024]{2,1,0:T(8,128)(2,1)}, bf16[2,192,1024]{2,1,0:T(8,128)(2,1)S(1)}, u32[]{:S(2)}, u32[]{:S(2)}) collective-permute-start(bf16[2,192,1024]{2,1,0:T(8,128)(2,1)} %get-tuple-element.128), channel_id=1, source_target_pairs={{0,16},{4,20},{8,24},{12,28},{16,0},{20,4},{24,8},{28,12},{1,17},{... | collective-permute-start | bytes 2359304 | tf_op jit(solution)/shard_map/ppermute | solution.py:838
  424.4 36.1 %collective-permute-start.33 = (bf16[4,128,1024]{2,1,0:T(8,128)(2,1)}, bf16[4,128,1024]{2,1,0:T(8,128)(2,1)S(1)}, u32[]{:S(2)}, u32[]{:S(2)}) collective-permute-start(bf16[4,128,1024]{2,1,0:T(8,128)(2,1)} %get-tuple-element.173), channel_id=1, source_target_pairs={{0,4},{4,0},{8,12},{12,8},{16,20},{20,16},{24,28},{28,24},{1,5},{5... | collective-permute-start | bytes 3145736 | tf_op jit(solution)/shard_map/ppermute | solution.py:838
  424.5 36.0 %collective-permute-start.32 = (bf16[4,128,1024]{2,1,0:T(8,128)(2,1)}, bf16[4,128,1024]{2,1,0:T(8,128)(2,1)S(1)}, u32[]{:S(2)}, u32[]{:S(2)}) collective-permute-start(bf16[4,128,1024]{2,1,0:T(8,128)(2,1)} %get-tuple-element.171), channel_id=1, source_target_pairs={{0,4},{4,0},{8,12},{12,8},{16,20},{20,16},{24,28},{28,24},{1,5},{5... | collective-permute-start | bytes 3145736 | tf_op jit(solution)/shard_map/ppermute | solution.py:838
  425.0 28.7 %collective-permute-start.36 = (bf16[192,1024]{1,0:T(8,128)(2,1)S(1)}, bf16[192,1024]{1,0:T(8,128)(2,1)S(1)}, u32[]{:S(2)}, u32[]{:S(2)}) collective-permute-start(bf16[192,1024]{1,0:T(8,128)(2,1)S(1)} %bitcast.63), channel_id=1, source_target_pairs={{0,1},{1,0},{2,3},{3,2},{4,5},{5,4},{6,7},{7,6},{8,9},{9,8},{10,11... | collective-permute-start | bytes 1179656 | tf_op jit(solution)/shard_map/ppermute | solution.py:838
  426.2 33.1 %collective-permute-start.34 = (bf16[1,128,1024]{2,1,0:T(8,128)(2,1)}, bf16[1,128,1024]{2,1,0:T(8,128)(2,1)S(1)}, u32[]{:S(2)}, u32[]{:S(2)}) collective-permute-start(bf16[1,128,1024]{2,1,0:T(8,128)(2,1)} %get-tuple-element.169.refs_2_), channel_id=1, source_target_pairs={{0,16},{4,20},{8,24},{12,28},{16,0},{20,4},{24,8},{28,12},{1,17},{... | collective-permute-start | bytes 786440 | tf_op jit(solution)/shard_map/ppermute | solution.py:838
  427.2 32.1 %collective-permute-start.35 = (bf16[1,128,1024]{2,1,0:T(8,128)(2,1)}, bf16[1,128,1024]{2,1,0:T(8,128)(2,1)S(1)}, u32[]{:S(2)}, u32[]{:S(2)}) collective-permute-start(bf16[1,128,1024]{2,1,0:T(8,128)(2,1)} %get-tuple-element.176), channel_id=1, source_target_pairs={{0,8},{4,12},{8,0},{12,4},{16,24},{20,28},{24,16},{28,20},{1,9},{5... | collective-permute-start | bytes 786440 | tf_op jit(solution)/shard_map/ppermute | solution.py:838
  459.2 25.2 %collective-permute-start.44 = (bf16[128,3072]{1,0:T(8,128)(2,1)S(1)}, bf16[128,3072]{1,0:T(8,128)(2,1)S(1)}, u32[]{:S(2)}, u32[]{:S(2)}) collective-permute-start(bf16[128,3072]{1,0:T(8,128)(2,1)S(1)} %get-tuple-element.177.refs_5_), channel_id=1, source_target_pairs={{0,1},{1,0},{2,3},{3,2},{4,5},{5,4},{6,7},{7,6},{8,9},{9,8},{10,11... | collective-permute-start | bytes 2359304 | tf_op jit(solution)/shard_map/ppermute | solution.py:838
  461.3 22.9 %collective-permute-start.37 = (bf16[2,128,1024]{2,1,0:T(8,128)(2,1)S(1)}, bf16[2,128,1024]{2,1,0:T(8,128)(2,1)S(1)}, u32[]{:S(2)}, u32[]{:S(2)}) collective-permute-start(bf16[2,128,1024]{2,1,0:T(8,128)(2,1)S(1)} %get-tuple-element.179.refs_2_), channel_id=1, source_target_pairs={{0,8},{4,12},{8,0},{12,4},{16,24},{20,28},{24,16},{28,20},{1,9},{5... | collective-permute-start | bytes 1572872 | tf_op jit(solution)/shard_map/ppermute | solution.py:838
  462.1 22.1 %collective-permute-start.38 = (bf16[2,128,1024]{2,1,0:T(8,128)(2,1)S(1)}, bf16[2,128,1024]{2,1,0:T(8,128)(2,1)S(1)}, u32[]{:S(2)}, u32[]{:S(2)}) collective-permute-start(bf16[2,128,1024]{2,1,0:T(8,128)(2,1)S(1)} %get-tuple-element.183), channel_id=1, source_target_pairs={{0,16},{4,20},{8,24},{12,28},{16,0},{20,4},{24,8},{28,12},{1,17},{... | collective-permute-start | bytes 1572872 | tf_op jit(solution)/shard_map/ppermute | solution.py:838
  484.6 44.4 %collective-permute-start.47 = (bf16[128,3072]{1,0:T(8,128)(2,1)S(1)}, bf16[128,3072]{1,0:T(8,128)(2,1)S(1)}, u32[]{:S(2)}, u32[]{:S(2)}) collective-permute-start(bf16[128,3072]{1,0:T(8,128)(2,1)S(1)} %bitcast.61), channel_id=1, source_target_pairs={{0,2},{1,3},{2,0},{3,1},{4,6},{5,7},{6,4},{7,5},{8,10},{9,11},{10,... | collective-permute-start | bytes 2359304 | tf_op jit(solution)/shard_map/ppermute | solution.py:838
  488.1 23.6 %collective-permute-start.43 = (bf16[128,1024]{1,0:T(8,128)(2,1)S(1)}, bf16[128,1024]{1,0:T(8,128)(2,1)S(1)}, u32[]{:S(2)}, u32[]{:S(2)}) collective-permute-start(bf16[128,1024]{1,0:T(8,128)(2,1)S(1)} %get-tuple-element.178.refs_4_), channel_id=1, source_target_pairs={{0,1},{1,0},{2,3},{3,2},{4,5},{5,4},{6,7},{7,6},{8,9},{9,8},{10,11... | collective-permute-start | bytes 786440 | tf_op jit(solution)/shard_map/ppermute | solution.py:838
  489.2 28.1 %collective-permute-start.42 = (bf16[128,1024]{1,0:T(8,128)(2,1)S(1)}, bf16[128,1024]{1,0:T(8,128)(2,1)S(1)}, u32[]{:S(2)}, u32[]{:S(2)}) collective-permute-start(bf16[128,1024]{1,0:T(8,128)(2,1)S(1)} %bitcast.68), channel_id=1, source_target_pairs={{0,1},{1,0},{2,3},{3,2},{4,5},{5,4},{6,7},{7,6},{8,9},{9,8},{10,11... | collective-permute-start | bytes 786440 | tf_op jit(solution)/shard_map/ppermute | solution.py:838
  490.1 28.2 %collective-permute-start.40 = (bf16[1,128,1024]{2,1,0:T(8,128)(2,1)S(1)}, bf16[1,128,1024]{2,1,0:T(8,128)(2,1)S(1)}, u32[]{:S(2)}, u32[]{:S(2)}) collective-permute-start(bf16[1,128,1024]{2,1,0:T(8,128)(2,1)S(1)} %get-tuple-element.185.refs_2_), channel_id=1, source_target_pairs={{0,16},{4,20},{8,24},{12,28},{16,0},{20,4},{24,8},{28,12},{1,17},{... | collective-permute-start | bytes 786440 | tf_op jit(solution)/shard_map/ppermute | solution.py:838
  491.2 27.1 %collective-permute-start.41 = (bf16[1,128,1024]{2,1,0:T(8,128)(2,1)S(1)}, bf16[1,128,1024]{2,1,0:T(8,128)(2,1)S(1)}, u32[]{:S(2)}, u32[]{:S(2)}) collective-permute-start(bf16[1,128,1024]{2,1,0:T(8,128)(2,1)S(1)} %get-tuple-element.187), channel_id=1, source_target_pairs={{0,8},{4,12},{8,0},{12,4},{16,24},{20,28},{24,16},{28,20},{1,9},{5... | collective-permute-start | bytes 786440 | tf_op jit(solution)/shard_map/ppermute | solution.py:838
  511.7 22.2 %collective-permute-start.46 = (bf16[128,1024]{1,0:T(8,128)(2,1)S(1)}, bf16[128,1024]{1,0:T(8,128)(2,1)S(1)}, u32[]{:S(2)}, u32[]{:S(2)}) collective-permute-start(bf16[128,1024]{1,0:T(8,128)(2,1)S(1)} %bitcast.73), channel_id=1, source_target_pairs={{0,2},{1,3},{2,0},{3,1},{4,6},{5,7},{6,4},{7,5},{8,10},{9,11},{10,... | collective-permute-start | bytes 786440 | tf_op jit(solution)/shard_map/ppermute | solution.py:838
  529.2 33.3 %collective-permute-start.55 = (bf16[128,3072]{1,0:T(8,128)(2,1)S(1)}, bf16[128,3072]{1,0:T(8,128)(2,1)S(1)}, u32[]{:S(2)}, u32[]{:S(2)}) collective-permute-start(bf16[128,3072]{1,0:T(8,128)(2,1)S(1)} %bitcast.59), channel_id=1, source_target_pairs={{0,1},{1,0},{2,3},{3,2},{4,5},{5,4},{6,7},{7,6},{8,9},{9,8},{10,11... | collective-permute-start | bytes 2359304 | tf_op jit(solution)/shard_map/ppermute | solution.py:838
  (109 other events, 1343.2 us)
Sparse Core Ops, SparseCore 0:
  16.1 147.8 all-gather.2
  247.8 114.5 reduce-scatter.2
  392.8 70.0 reduce-scatter.4

commit v2 on v1

v2 whole, which is shorter than its diff:
```python
import functools
import math

import jax
import jax.numpy as jnp
from jax import lax
from jax.experimental import pallas as pl
from jax.experimental.pallas import tpu as pltpu
from jax.sharding import PartitionSpec as P

HEADS = 16
KV_HEADS = 8
HEAD_DIM = 128
GROUPS = HEADS // KV_HEADS

EPSILON = 1e-06
ROPE_BASE = 1000000.0
MASKED = -1e30
SCALE = HEAD_DIM ** (-0.5)

F32 = jnp.float32
BF16 = jnp.bfloat16
MIB = 1 << 20
VMEM_MIB = 20
LARGE = 1 << 18


ORDER = []


def shape(dims, dtype):
    return jax.ShapeDtypeStruct(dims, dtype)


ANY = pl.BlockSpec(memory_space=pl.ANY)
IN_VMEM = pl.BlockSpec(memory_space=pltpu.VMEM)
IN_HBM = pl.BlockSpec(memory_space=pltpu.HBM)


def in_hbm(spec, array):
    return spec not in (IN_VMEM, ANY, IN_HBM) and math.prod(array.shape) * 2 >= LARGE


def call(
    name, body, args, in_specs, out_specs, out_shape, grid=(1,), scratch=(), prefetch=(), aliases=None,
    after=(), vmem=VMEM_MIB,
):
    waits = list(ORDER) + list(after)
    wait_specs = [IN_VMEM] * len(ORDER) + [ANY] * len(after)
    taken = len(prefetch) + len(args)
    token = taken + len(waits) + len(out_shape)
    args = [
        pltpu.with_memory_space_constraint(a, pltpu.HBM) if in_hbm(s, a) else a
        for a, s in zip(args, in_specs)
    ]
    out_shape = [
        pltpu.HBM(o.shape, o.dtype) if in_hbm(s, o) else o for o, s in zip(out_shape, out_specs)
    ]

    def without(*refs):
        refs[token][...] = jnp.zeros_like(refs[token])
        body(*refs[:taken], *refs[taken + len(waits) : token], *refs[token + 1 :])

    results = pl.pallas_call(
        without,
        grid_spec=pltpu.PrefetchScalarGridSpec(
            num_scalar_prefetch=len(prefetch),
            grid=grid,
            in_specs=list(in_specs) + wait_specs,
            out_specs=list(out_specs) + [IN_VMEM],
            scratch_shapes=list(scratch),
        ),
        out_shape=out_shape + [shape((8, HEAD_DIM), F32)],
        input_output_aliases={len(prefetch) + i: o for i, o in (aliases or {}).items()},
        compiler_params=pltpu.CompilerParams(vmem_limit_bytes=vmem * MIB),
        cost_estimate=pl.CostEstimate(flops=0, bytes_accessed=0, transcendentals=0),
        name=name,
    )(*prefetch, *args, *waits)
    ORDER[:] = [results[-1]]
    return results[:-1]


def whole(dims):
    return pl.BlockSpec(dims, lambda *_: (0,) * len(dims))


def mm(a, b):
    return lax.dot_general(a, b, (((1,), (0,)), ((), ())), preferred_element_type=F32)


def mm_nt(a, b):
    return lax.dot_general(a, b, (((1,), (1,)), ((), ())), preferred_element_type=F32)


def mm_tn(a, b):
    return lax.dot_general(a, b, (((0,), (0,)), ((), ())), preferred_element_type=F32)


def mean_last(v):
    return jnp.sum(v, axis=-1, keepdims=True) * (1.0 / v.shape[-1])


def factor_of(v):
    return lax.rsqrt(mean_last(v * v) + EPSILON)


def norm_back(v, gain, incoming):
    f = factor_of(v)
    weighted = incoming * gain
    inner = mean_last(weighted * v)
    return f * weighted - v * (f * f * f * inner), incoming * v * f


def stream_index(row_ids, stretch_rows, ctx_size):
    slab_index = row_ids // (2 * stretch_rows)
    within = row_ids % (2 * stretch_rows)
    mirrored = (2 * ctx_size - 1 - slab_index) * stretch_rows + within - stretch_rows
    return jnp.where(within < stretch_rows, slab_index * stretch_rows + within, mirrored)


def opening_of(stream, starts):
    started = starts[None, :] <= stream[:, None]
    return jnp.max(jnp.where(started, starts[None, :], 0), axis=1)


def rotary(positions):
    half_dim = HEAD_DIM // 2
    inverse = jnp.exp(
        jnp.arange(half_dim, dtype=F32) * (-2.0 * math.log(ROPE_BASE) / HEAD_DIM)
    )
    angles = positions.astype(F32)[:, None] * inverse[None, :]
    cos_half, sin_half = jnp.cos(angles), jnp.sin(angles)
    return (
        jnp.concatenate([cos_half, cos_half], axis=1),
        jnp.concatenate([-sin_half, sin_half], axis=1),
    )


def copies(name, sources, plan, out_shape, prefetch=(), after=(), in_specs=None, out_specs=None):
    count = len(sources)
    first = len(prefetch)

    def body(*refs):
        ins = refs[first : first + count]
        for source, target in plan(refs[:first], ins, refs[first + count :]):
            target[...] = source[...]

    return call(
        name, body, sources, in_specs or [IN_VMEM] * count, out_specs or [IN_VMEM] * len(out_shape), out_shape,
        prefetch=prefetch, after=after,
    )


def touch(after):
    call("touch", lambda *_: None, [], [], [], [], after=after, vmem=4)


def norm_own(tokens, gain):
    def body(t_ref, g_ref, out_ref):
        x = t_ref[...].astype(F32)
        out_ref[...] = (x * factor_of(x) * g_ref[...]).astype(BF16)

    return call(
        "norm_own", body, [tokens, gain], [IN_VMEM] * 2, [IN_VMEM], [shape(tokens.shape, BF16)]
    )[0]


def norm_pack(own, from_left, from_right, gain, places, ctx_at):
    count = len(from_left) + 1
    rows, width = own.shape
    half = rows // 2

    def body(places_ref, at_ref, gain_ref, *refs):
        blocks, pack_ref = refs[:-1], refs[-1]
        step = pl.program_id(0)
        me = at_ref[0]

        def write(ref):
            x = ref[...].astype(F32)
            low = (x * factor_of(x) * gain_ref[...]).astype(BF16)
            pack_ref[...] = low.reshape(2, 1, half, width)

        @pl.when(step == 0)
        def _():
            write(blocks[0])

        for s in range(1, count):

            @pl.when((step == s) & (me >= s))
            def _():
                write(blocks[s])

            @pl.when((step == s) & (me < s))
            def _():
                write(blocks[count - 1 + count - s])

    blocks = [own] + from_left + from_right
    return call(
        "norm_pack", body, [gain] + blocks,
        [whole((1, width))] + [IN_VMEM] * len(blocks),
        [pl.BlockSpec((2, 1, half, width), lambda k, at, me: (0, at[k], 0, 0))],
        [shape((2, count, half, width), BF16)],
        grid=(count,), prefetch=[places, ctx_at],
    )[0]


def lane_sums(v):
    cols = v.shape[-1]
    head = lax.broadcasted_iota(jnp.int32, (cols, cols), 0) // HEAD_DIM
    same = (head == lax.broadcasted_iota(jnp.int32, (cols, cols), 1) // HEAD_DIM).astype(BF16)
    high = v.astype(BF16)
    low = (v - high.astype(F32)).astype(BF16)
    return mm(high, same) + mm(low, same)


def head_factors(raw):
    return lax.rsqrt(lane_sums(raw * raw) * (1.0 / HEAD_DIM) + EPSILON)


def turn(v):
    parts = [
        pltpu.roll(v[:, at : at + HEAD_DIM], HEAD_DIM // 2, 1) for at in range(0, v.shape[1], HEAD_DIM)
    ]
    return parts[0] if len(parts) == 1 else jnp.concatenate(parts, axis=1)


def rotated(v, cos, sin):
    return v * cos + turn(v) * sin


def rope(raw, gain, cos, sin):
    return rotated(raw * head_factors(raw) * gain, cos, sin)


def twice(ref):
    return jnp.concatenate([ref[...]] * 2, axis=1)


def project_queries(x, weights, gain, cos, sin):
    rows, width = x.shape
    cols = HEADS * HEAD_DIM
    block = 2 * HEAD_DIM
    each = 2 * block
    col = pl.BlockSpec((rows, each), lambda j: (0, j))

    def body(x_ref, w_ref, g_ref, c_ref, s_ref, raw_ref, rot_ref, fac_ref):
        g, c, s = twice(g_ref), twice(c_ref), twice(s_ref)
        for j in range(each // block):
            at = slice(j * block, (j + 1) * block)
            raw = mm(x_ref[...], w_ref[:, at])
            raw_ref[:, at] = raw.astype(BF16)
            factors = head_factors(raw)
            rot_ref[:, at] = rotated(raw * factors * g, c, s).astype(BF16)
            for h in range(2):
                fac_ref[2 * j + h] = factors[:, h * HEAD_DIM : (h + 1) * HEAD_DIM].T[:8]

    return call(
        "project_queries", body, [x, weights, gain, cos, sin],
        [IN_VMEM, pl.BlockSpec((width, each), lambda j: (0, j))] + [IN_VMEM] * 3,
        [col, col, pl.BlockSpec((each // HEAD_DIM, 8, rows), lambda j: (j, 0, 0))],
        [shape((rows, cols), BF16), shape((rows, cols), BF16), shape((HEADS, 8, rows), F32)],
        grid=(cols // each,),
    )


def project_keys_values(x, weights, gain, cos, sin):
    rows, width = x.shape
    block = 2 * HEAD_DIM
    cols = KV_HEADS * HEAD_DIM
    inner = HEADS * HEAD_DIM
    part = 256

    def body(x_ref, wk_ref, wv_ref, g_ref, c_ref, s_ref, raw_ref, rot_ref, val_ref):
        wk, wv = wk_ref[...], wv_ref[...]
        g = twice(g_ref)
        for i in range(rows // part):
            here = slice(i * part, (i + 1) * part)
            raw = mm(x_ref[here, :], wk)
            raw_ref[here, :] = raw.astype(BF16)
            val_ref[here, :] = mm(x_ref[here, :], wv).astype(BF16)
            c, s = [jnp.concatenate([r[here, :]] * 2, axis=1) for r in (c_ref, s_ref)]
            rot_ref[here, :] = rope(raw, g, c, s).astype(BF16)

    col = pl.BlockSpec((rows, block), lambda j: (0, j))
    return call(
        "project_keys_values", body, [x, weights, weights, gain, cos, sin],
        [
            IN_VMEM,
            pl.BlockSpec((width, block), lambda j: (0, inner // block + j)),
            pl.BlockSpec((width, block), lambda j: (0, (inner + cols) // block + j)),
        ]
        + [IN_VMEM] * 3,
        [col, col, col], [shape((rows, cols), BF16)] * 3, grid=(cols // block,),
    )


LOG2E = 1.4426950408889634


def attend(queries, keys, values, q_low, q_high, k_stream):
    rows = queries.shape[0]
    half = rows // 2
    pack = keys.shape[0]
    pair = GROUPS * HEAD_DIM

    def body(q_ref, k_ref, v_ref, lo_ref, hi_ref, ks_ref, mix_ref, lse_ref, bias):
        @pl.when(pl.program_id(0) == 0)
        def _():
            ks = ks_ref[...]
            ok = (ks >= lo_ref[...]) & (ks <= hi_ref[...])
            bias[...] = jnp.where(ok, 0.0, MASKED)

        v_ones = jnp.concatenate([v_ref[...], jnp.ones((pack, HEAD_DIM), BF16)], axis=1)
        for part in range(2):
            here = slice(part * half, (part + 1) * half)
            seen = pack // 2 if part == 0 else pack
            for j in range(GROUPS):
                cols = slice(j * HEAD_DIM, (j + 1) * HEAD_DIM)
                scores = mm_nt(q_ref[here, cols], k_ref[:seen, :]) * (SCALE * LOG2E) + bias[here, :seen]
                both = mm(jnp.exp2(scores).astype(BF16), v_ones[:seen])
                total = both[:, HEAD_DIM:]
                mix_ref[here, cols] = (both[:, :HEAD_DIM] * (1.0 / total)).astype(BF16)
                lse_ref[j, :, here] = jnp.log2(total).T[:8]

    col = pl.BlockSpec((rows, pair), lambda g: (0, g))
    key = pl.BlockSpec((pack, HEAD_DIM), lambda g: (0, g))
    return call(
        "attend", body, [queries, keys, values, q_low, q_high, k_stream],
        [col, key, key, whole((rows, 1)), whole((rows, 1)), whole((1, pack))],
        [col, pl.BlockSpec((GROUPS, 8, rows), lambda g: (g, 0, 0))],
        [shape((rows, HEADS * HEAD_DIM), BF16), shape((HEADS, 8, rows), F32)],
        grid=(KV_HEADS,),
        scratch=[pltpu.VMEM((rows, pack), F32)],
    )


def high_low(v):
    high = v.astype(BF16)
    return high, (v - high.astype(F32)).astype(BF16)


def feed_forward(mixed, tokens, grad, gain, stack):
    rows, inner = mixed.shape
    count, _, width = stack.shape
    unit = width // count
    hidden = 3 * width
    block = 256

    def body(
        mixed_hbm, tok_hbm, dy_hbm, gain_ref, stack_ref,
        out_ref, low_ref, h_ref, both_ref, mid_ref,
        w, acc, mixed_ref, tok_ref, dy_ref, sems,
    ):
        def move(first, many, sem):
            here = (slice(None), pl.ds(first * unit, many * unit))
            return pltpu.make_async_copy(stack_ref.at[here], w.at[here], sems.at[sem])

        loads = [
            pltpu.make_async_copy(a, b, sems.at[8 + i])
            for i, (a, b) in enumerate(((mixed_hbm, mixed_ref), (tok_hbm, tok_ref), (dy_hbm, dy_ref)))
        ]
        out_copy = move(9, 2, 0)
        gate_copies = [move(3 + i, 1, 1 + i) for i in range(3)]
        up_copies = [move(6 + i, 1, 4 + i) for i in range(3)]
        down_copy = move(0, 3, 7)
        loads[0].start()
        out_copy.start()
        loads[1].start()
        loads[2].start()
        for a, b in zip(gate_copies, up_copies):
            a.start()
            b.start()
        down_copy.start()

        for load in loads:
            load.wait()
        out_copy.wait()
        for j in range(width // block):
            cols = slice(j * block, (j + 1) * block)
            part = w[:, 9 * unit : 11 * unit, cols].reshape(inner, block)
            mid_ref[:, cols] = tok_ref[:, cols].astype(F32) + mm(mixed_ref[...], part)
        x = mid_ref[...]
        low_ref[...] = (x * factor_of(x) * gain_ref[...]).astype(BF16)

        for i in range(3):
            gate_copies[i].wait()
            up_copies[i].wait()
            for j in range(width // block):
                cols = slice(j * block, (j + 1) * block)
                to = slice(i * width + j * block, i * width + (j + 1) * block)
                g = mm(low_ref[...], w[:, (3 + i) * unit : (4 + i) * unit, cols].reshape(width, block))
                u = mm(low_ref[...], w[:, (6 + i) * unit : (7 + i) * unit, cols].reshape(width, block))
                s = 1.0 / (1.0 + jnp.exp(-g))
                act = g * s
                h_ref[:, to] = (act * u).astype(BF16)
                both_ref[0, :, to] = (u * (s + act * (1.0 - s))).astype(BF16)
                both_ref[1, :, to] = act.astype(BF16)

        down_copy.wait()
        wide = 384
        owners = wide // (3 * unit)
        acc[...] = mid_ref[...]
        for j in range(hidden // wide):
            cols = slice(j * wide, (j + 1) * wide)
            part = w[j * owners : (j + 1) * owners, 0 : 3 * unit, :].reshape(wide, width)
            dh = mm_nt(dy_ref[...], part)
            both_ref[0, :, cols] = (both_ref[0, :, cols].astype(F32) * dh).astype(BF16)
            both_ref[1, :, cols] = (both_ref[1, :, cols].astype(F32) * dh).astype(BF16)
            acc[...] += mm(h_ref[:, cols], part)
        out_ref[...] = acc[...].astype(BF16)

    full = (rows, width)
    return call(
        "feed_forward", body, [mixed, tokens, grad, gain, stack],
        [IN_HBM, IN_HBM, IN_HBM, whole((1, width)), IN_HBM],
        [whole(full), IN_VMEM, IN_VMEM, IN_VMEM, IN_VMEM],
        [
            shape(full, BF16), shape(full, BF16), shape((rows, hidden), BF16),
            shape((2, rows, hidden), BF16), shape(full, F32),
        ],
        scratch=[
            pltpu.VMEM(stack.shape, BF16),
            pltpu.VMEM(full, F32),
            pltpu.VMEM((rows, inner), BF16),
            pltpu.VMEM(full, BF16),
            pltpu.VMEM(full, BF16),
            pltpu.SemaphoreType.DMA((11,)),
        ],
        vmem=40,
    )


def branch_back(both, middle, grad, gain, mixed, lse, factors, stack):
    _, rows, hidden = both.shape
    count, _, width = stack.shape
    unit = width // count
    inner = mixed.shape[1]
    block = 256

    def body(
        both_ref, mid_ref, dy_ref, gain_ref, mixed_ref, lse_ref, fac_ref, stack_ref,
        gm_ref, gb_ref, gg_ref, dm_ref, parcel_ref,
        w, acc, deltas, sems,
    ):
        owners_in = block // unit
        steps = width // block
        copies_in = []
        for b in range(steps):
            here = (pl.ds(b * owners_in, owners_in), pl.ds(3 * unit, 6 * unit))
            to = (pl.ds(b * owners_in, owners_in), pl.ds(0, 6 * unit))
            copies_in.append(pltpu.make_async_copy(stack_ref.at[here], w.at[to], sems.at[b]))
        here, to = (slice(None), pl.ds(9 * unit, 2 * unit)), (slice(None), pl.ds(6 * unit, 2 * unit))
        out_copy = pltpu.make_async_copy(stack_ref.at[here], w.at[to], sems.at[steps])
        for copy in copies_in + [out_copy]:
            copy.start()

        for b in range(steps):
            copies_in[b].wait()
            at = slice(b * owners_in, (b + 1) * owners_in)
            total = None
            for i in range(6):
                part = w[at, i * unit : (i + 1) * unit, :].reshape(block, width)
                term = mm_nt(both_ref[i // 3, :, (i % 3) * width : (i % 3 + 1) * width], part)
                total = term if total is None else total + term
            acc[:, b * block : (b + 1) * block] = total

        back, terms = norm_back(mid_ref[...], gain_ref[...], acc[...])
        grad_mid = dy_ref[...].astype(F32) + back
        gm_ref[...] = grad_mid
        gb_ref[...] = grad_mid.astype(BF16)
        gg_ref[...] = jnp.sum(terms, axis=0, keepdims=True)

        out_copy.wait()
        owners_out = block // (2 * unit)
        for j in range(inner // block):
            cols = slice(j * block, (j + 1) * block)
            at = slice(j * owners_out, (j + 1) * owners_out)
            dm = mm_nt(gb_ref[...], w[at, 6 * unit : 8 * unit, :].reshape(block, width)).astype(BF16)
            dm_ref[:, cols] = dm
            terms = (dm.astype(F32) * mixed_ref[:, cols].astype(F32)).T
            for k in range(block // HEAD_DIM):
                head = j * (block // HEAD_DIM) + k
                deltas[head : head + 1, :] = jnp.sum(
                    terms[k * HEAD_DIM : (k + 1) * HEAD_DIM], axis=0, keepdims=True
                )
        parcel_ref[:rows, :] = gb_ref[...]
        parcel_ref[rows:, :] = jnp.zeros((3 * HEADS, width), BF16)
        for which, values in enumerate((lse_ref[:, 0, :], deltas[...], fac_ref[:, 0, :])):
            at = rows + which * HEADS
            for side, piece in enumerate(high_low(values)):
                parcel_ref[at : at + HEADS, side * rows : (side + 1) * rows] = piece

    full = (rows, width)
    return call(
        "branch_back", body, [both, middle, grad, gain, mixed, lse, factors, stack],
        [
            IN_VMEM, IN_VMEM, whole(full), whole((1, width)), whole((rows, inner)), whole(lse.shape),
            whole(factors.shape), IN_HBM,
        ],
        [whole(full), IN_VMEM, IN_VMEM, whole((rows, inner)), IN_VMEM],
        [
            shape(full, F32), shape(full, BF16), shape((1, width), F32), shape((rows, inner), BF16),
            shape((rows + 3 * HEADS, width), BF16),
        ],
        scratch=[
            pltpu.VMEM((count, 8 * unit, width), BF16),
            pltpu.VMEM(full, F32),
            pltpu.VMEM((HEADS, rows), F32),
            pltpu.SemaphoreType.DMA((width // block + 1,)),
        ],
        vmem=32,
    )


def head_norm_back(v, gain, incoming):
    f = head_factors(v)
    weighted = incoming * gain
    inner = lane_sums(weighted * v) * (1.0 / HEAD_DIM)
    return f * (weighted - v * (f * f * inner)), incoming * v * f


def query_back(
    queries, grad_mixed, mixed, keys, values, lse, q_low, q_high, k_stream, query_raw, gain, cos, sin,
    first, count, earlier=(),
):
    rows = queries.shape[0]
    half = rows // 2
    pack = keys.shape[0]
    pair = GROUPS * HEAD_DIM

    def body(
        q_ref, do_ref, mix_ref, k_ref, v_ref, lse_ref, lo_ref, hi_ref, ks_ref, raw_ref, g_ref, c_ref, s_ref,
        *rest,
    ):
        dq_ref, gg_ref, bias = rest[len(earlier) :]

        @pl.when(pl.program_id(0) == 0)
        def _():
            ks = ks_ref[...]
            ok = (ks >= lo_ref[...]) & (ks <= hi_ref[...])
            bias[...] = jnp.where(ok, 0.0, MASKED)
            gg_ref[...] = jnp.zeros_like(gg_ref)

        deltas = lane_sums(do_ref[...].astype(F32) * mix_ref[...].astype(F32))
        for j in range(GROUPS):
            cols = slice(j * HEAD_DIM, (j + 1) * HEAD_DIM)
            lse_col = jnp.broadcast_to(lse_ref[j, 0:1, :], (HEAD_DIM, rows)).T[:, :1]
            grads = []
            for part in range(2):
                here = slice(part * half, (part + 1) * half)
                seen = pack // 2 if part == 0 else pack
                scores = mm_nt(q_ref[here, cols], k_ref[:seen, :]) * (SCALE * LOG2E) + bias[here, :seen]
                probs = jnp.exp2(scores - lse_col[here])
                d_probs = mm_nt(do_ref[here, cols], v_ref[:seen, :])
                d_scores = (probs * (d_probs - deltas[here, cols][:, :1])).astype(BF16)
                grads.append(mm(d_scores, k_ref[:seen, :]))
            dq = jnp.concatenate(grads, axis=0) * SCALE
            dq = dq * c_ref[...] - turn(dq) * s_ref[...]
            dq, terms = head_norm_back(raw_ref[:, cols].astype(F32), g_ref[...], dq)
            dq_ref[:, cols] = dq.astype(BF16)
            gg_ref[...] += jnp.sum(terms, axis=0, keepdims=True)

    col = pl.BlockSpec((rows, pair), lambda g: (0, first + g))
    key = pl.BlockSpec((pack, HEAD_DIM), lambda g: (0, first + g))
    return call(
        "query_back", body,
        [queries, grad_mixed, mixed, keys, values, lse, q_low, q_high, k_stream, query_raw, gain, cos, sin, *earlier],
        [
            col, col, col, key, key,
            pl.BlockSpec((GROUPS, 8, rows), lambda g: (first + g, 0, 0)),
            whole((rows, 1)), whole((rows, 1)), whole((1, pack)),
            col, whole((1, HEAD_DIM)), whole((rows, HEAD_DIM)), whole((rows, HEAD_DIM)),
        ]
        + [ANY] * len(earlier),
        [col, whole((1, HEAD_DIM))],
        [shape((rows, HEADS * HEAD_DIM), BF16), shape((1, HEAD_DIM), F32)],
        grid=(count,),
        scratch=[pltpu.VMEM((rows, pack), F32)],
        aliases={13: 0} if earlier else None,
    )


def key_back(
    queries, grad_mixed, keys, values, far, q_low, q_high, k_stream, key_raw, gain, cos, sin,
    ctx_at, ctx_size, first, count, earlier=(),
):
    pack = queries.shape[0]
    rows = pack // ctx_size
    half = rows // 2
    pair = GROUPS * HEAD_DIM

    def body(
        at_ref, q_ref, do_ref, k_ref, v_ref, far_ref, lo_ref, hi_ref, ks_ref, raw_ref, g_ref,
        c_ref, s_ref, *rest,
    ):
        out_ref, gg_ref, bias, acc = rest[len(earlier) :]

        @pl.when(pl.program_id(0) == 0)
        def _():
            ks = ks_ref[...]
            ok = (ks >= lo_ref[...]) & (ks <= hi_ref[...])
            bias[...] = jnp.where(ok, 0.0, MASKED)
            gg_ref[...] = jnp.zeros_like(gg_ref)

        k_own = k_ref[...].reshape(rows, HEAD_DIM)
        v_own = v_ref[...].reshape(rows, HEAD_DIM)
        for j in range(GROUPS):
            cols = slice(j * HEAD_DIM, (j + 1) * HEAD_DIM)
            head = GROUPS * (first + pl.program_id(0)) + j
            lse, delta, factors = [far_ref[pl.ds(i * HEADS + head, 1), :] for i in range(3)]
            for late in range(2):
                there = slice(late * pack // 2, (late + 1) * pack // 2)
                here = slice(0, rows if late else half)
                qq, dd = q_ref[there, cols], do_ref[there, cols]
                factor = factors[:, there]
                scores = mm_nt(k_own[here], qq) * (factor * (SCALE * LOG2E)) + bias[here, there]
                probs = jnp.exp2(scores - lse[:, there])
                d_probs = mm_nt(v_own[here], dd)
                d_scores = (probs * factor * (d_probs - delta[:, there])).astype(BF16)
                dv = mm(probs.astype(BF16), dd)
                dk = mm(d_scores, qq)
                if j == 0 and late == 0:
                    acc[...] = jnp.zeros_like(acc)
                acc[0, here, :] += dk
                acc[1, here, :] += dv
        out_ref[1] = acc[1].astype(BF16)
        dk = acc[0] * SCALE
        dk = dk * c_ref[...] - turn(dk) * s_ref[...]
        dk, terms = head_norm_back(raw_ref[...].astype(F32).reshape(rows, HEAD_DIM), g_ref[...], dk)
        out_ref[0] = dk.astype(BF16)
        gg_ref[...] += jnp.sum(terms, axis=0, keepdims=True)

    col = pl.BlockSpec((pack, pair), lambda g, at: (0, first + g))
    key = pl.BlockSpec((2, 1, half, HEAD_DIM), lambda g, at: (0, at[0], 0, first + g))
    laid = (2, ctx_size, half, KV_HEADS * HEAD_DIM)
    return call(
        "key_back", body,
        [
            queries, grad_mixed, keys.reshape(laid), values.reshape(laid), far, q_low, q_high, k_stream, key_raw.reshape(laid), gain, cos, sin, *earlier,
        ],
        [
            col, col, key, key, whole(far.shape), whole((1, pack)), whole((1, pack)), whole((rows, 1)),
            key, whole((1, HEAD_DIM)), whole((rows, HEAD_DIM)), whole((rows, HEAD_DIM)),
        ]
        + [ANY] * len(earlier),
        [pl.BlockSpec((2, rows, HEAD_DIM), lambda g, at: (0, 0, first + g)), whole((1, HEAD_DIM))],
        [shape((2, rows, KV_HEADS * HEAD_DIM), BF16), shape((1, HEAD_DIM), F32)],
        grid=(count,),
        scratch=[pltpu.VMEM((rows, pack), F32), pltpu.VMEM((2, rows, HEAD_DIM), F32)],
        prefetch=[ctx_at], aliases={12: 0} if earlier else None,
    )


def all_queries(x, weights, gain, cos, sin):
    rows, width = x.shape
    cols = HEADS * HEAD_DIM
    block = 2 * HEAD_DIM
    part = 256

    def body(x_ref, w_ref, g_ref, c_ref, s_ref, rot_ref):
        g = twice(g_ref)
        for i in range(rows // part):
            here = slice(i * part, (i + 1) * part)
            raw = mm(x_ref[here, :], w_ref[...])
            c, s = [jnp.concatenate([r[here, :]] * 2, axis=1) for r in (c_ref, s_ref)]
            rot_ref[here, :] = rotated(raw * g, c, s).astype(BF16)

    return call(
        "all_queries", body, [x, weights, gain, cos, sin],
        [IN_VMEM, pl.BlockSpec((width, block), lambda j: (0, j)), IN_VMEM, IN_VMEM, IN_VMEM],
        [pl.BlockSpec((rows, block), lambda j: (0, j))], [shape((rows, cols), BF16)],
        grid=(cols // block,),
    )[0]


def all_grad_mixed(own, parcels, stack, places, ctx_at, rows):
    count = (len(parcels) + 1) // 2
    numbers = parcels[0].shape[0] - rows
    half = rows // 2
    inner = own.shape[1]
    _, _, width = stack.shape
    owners = stack.shape[0]
    unit = width // owners

    def body(places_ref, at_ref, own_ref, a_ref, b_ref, *refs):
        blocks, (out_ref, far_ref, turned) = refs[:-3], refs[-3:]
        step = pl.program_id(0)
        me = at_ref[0]

        def spread(ref):
            both = ref[rows:, :rows].astype(F32) + ref[rows:, rows : 2 * rows].astype(F32)
            far_ref[0, 0] = both[:, :half]
            far_ref[1, 0] = both[:, half:]

        @pl.when(step == 0)
        def _():
            spread(blocks[0])
            out_ref[...] = own_ref[...].reshape(2, 1, half, inner)
            turned[...] = jnp.concatenate([a_ref[...], b_ref[...]], axis=1).reshape(inner, width)

        def write(ref):
            spread(ref)
            for j in range(inner // 512):
                at = slice(j * 512, (j + 1) * 512)
                part = mm_nt(ref[:rows, :], turned[at, :]).astype(BF16)
                out_ref[:, :, :, at] = part.reshape(2, 1, half, 512)

        for s in range(1, count):

            @pl.when((step == s) & (me >= s))
            def _():
                write(blocks[s])

            @pl.when((step == s) & (me < s))
            def _():
                write(blocks[count - 1 + count - s])

    return call(
        "all_grad_mixed", body, [own, stack, stack, *parcels],
        [
            IN_VMEM,
            pl.BlockSpec((owners, unit, width), lambda *_: (0, 9, 0)),
            pl.BlockSpec((owners, unit, width), lambda *_: (0, 10, 0)),
        ]
        + [IN_VMEM] * len(parcels),
        [
            pl.BlockSpec((2, 1, half, inner), lambda k, at, me: (0, at[k], 0, 0)),
            pl.BlockSpec((2, 1, numbers, half), lambda k, at, me: (0, at[k], 0, 0)),
        ],
        [shape((2, count, half, inner), BF16), shape((2, count, numbers, half), F32)],
        grid=(count,), scratch=[pltpu.VMEM((inner, width), BF16)], prefetch=[places, ctx_at], vmem=32,
    )


def normed_back(d_queries, d_pair, weights):
    rows, inner = d_queries.shape
    cols = d_pair.shape[2]
    width = weights.shape[0]

    def body(dq_ref, pair_ref, wq_ref, wk_ref, wv_ref, out_ref):
        part = mm_nt(dq_ref[...], wq_ref[...])
        part += mm_nt(pair_ref[0], wk_ref[...])
        part += mm_nt(pair_ref[1], wv_ref[...])
        out_ref[...] = part

    block = 256
    return call(
        "normed_back", body, [d_queries, d_pair, weights, weights, weights],
        [
            IN_VMEM,
            IN_VMEM,
            pl.BlockSpec((block, inner), lambda j: (j, 0)),
            pl.BlockSpec((block, cols), lambda j: (j, inner // cols)),
            pl.BlockSpec((block, cols), lambda j: (j, inner // cols + 1)),
        ],
        [pl.BlockSpec((rows, block), lambda j: (0, j))],
        [shape((rows, width), F32)],
        grid=(width // block,),
    )[0]


def input_back(d_normed, tokens, gain, grad_middle):
    rows, width = tokens.shape

    def body(a_ref, t_ref, gain_ref, gm_ref, out_ref, gg_ref):
        back, terms = norm_back(t_ref[...].astype(F32), gain_ref[...], a_ref[...])
        out_ref[...] = (gm_ref[...] + back).astype(BF16)
        gg_ref[...] = jnp.sum(terms, axis=0, keepdims=True)

    return call(
        "input_back", body, [d_normed, tokens, gain, grad_middle],
        [IN_VMEM] * 4,
        [whole((rows, width)), IN_VMEM],
        [shape((rows, width), BF16), shape((1, width), F32)],
    )


def weight_grad(left, right, owners=None, cols=None, block=512, apart=False, beside=False):
    tokens, rows = left.shape
    count = 1 if owners is None else owners.shape[0]
    unit = rows // count
    deep = right.ndim == 3
    first, each = cols or (0, right.shape[-1])
    width = each * (right.shape[0] if deep else 1)
    steps = width // block
    split = owners is not None
    results = 2 * (right.shape[0] if apart else 1) if split else 1

    def body(*refs):
        if split:
            own_ref, refs = refs[0], refs[1:]
        l_ref, r_ref, refs = refs[0], refs[1], refs[2:]
        outs, scratch = refs[:results], refs[results:]

        @pl.when(pl.program_id(0) == 0)
        def _():
            scratch[0][...] = l_ref[...].T
            for k in range(count if split else 0):
                at = pl.multiple_of(own_ref[k] * unit, unit)
                scratch[1][k * unit : (k + 1) * unit, :] = scratch[0][pl.ds(at, unit), :]

        def block_at(j):
            if deep:
                per = each // block
                return r_ref[j // per, :, pl.ds(pl.multiple_of(first + (j % per) * block, block), block)]
            return r_ref[:, pl.ds(pl.multiple_of(first + j * block, block), block)]

        if not split:
            outs[0][...] = mm(scratch[0][...], block_at(pl.program_id(0))).astype(BF16)
            return
        per = each // block
        for j in range(steps):
            at = 2 * (j // per) if apart else 0
            to = slice((j % per) * block, (j % per + 1) * block) if apart else slice(j * block, (j + 1) * block)
            for side in range(2):
                here = slice(side * rows // 2, (side + 1) * rows // 2)
                part = mm(scratch[1][here, :], block_at(j)).astype(BF16)
                part = part.reshape(count // 2, unit, block)
                if beside:
                    outs[side][:, :, to] = part[:, : unit // 2]
                    outs[side][:, :, width + j * block : width + (j + 1) * block] = part[:, unit // 2 :]
                else:
                    outs[at + side][:, :, to] = part

    if split:
        out = [IN_VMEM] * results
        dims = (count // 2, unit // 2, 2 * width) if beside else (count // 2, unit, each if apart else width)
        out_shape = [shape(dims, BF16)] * results
    else:
        out = [pl.BlockSpec((rows, block), lambda j: (0, j))]
        out_shape = [shape((rows, width), BF16)]
    return call(
        "weight_grad", body, [left, right], [IN_VMEM] * 2, out, out_shape,
        grid=(1 if split else steps,),
        scratch=[pltpu.VMEM((rows, tokens), BF16)] * (1 + split),
        prefetch=[owners] if split else (),
    )


def fold(items, steps=1):
    arrays = []

    def slot(term):
        for i, known in enumerate(arrays):
            if known is term:
                return i
        arrays.append(term)
        return len(arrays) - 1

    laid = [([slot(t) for t in terms], rows, bit) for terms, rows, bit in items]
    in_specs = []
    for a in arrays:
        in_specs.append(
            IN_VMEM if steps == 1 else pl.BlockSpec(a.shape[:2] + (a.shape[2] // steps,), lambda j: (0, 0, j))
        )
    out_specs, out_shape = [], []
    for slots, (_, rows), bit in laid:
        many, _, cols = arrays[slots[0]].shape
        dims = (many, rows, cols) if bit is None else (many // 2, rows, cols)
        for _ in range(1 if bit is None else 2):
            out_specs.append(
                IN_VMEM if steps == 1 else pl.BlockSpec(dims[:2] + (cols // steps,), lambda j: (0, 0, j))
            )
            out_shape.append(shape(dims, BF16))

    def body(*refs):
        ins, outs = refs[: len(arrays)], list(refs[len(arrays) :])
        for slots, (first, rows), bit in laid:
            here = slice(first, first + rows)
            many = arrays[slots[0]].shape[0]

            def total(k):
                value = ins[slots[0]][k, here, :].astype(F32)
                for at in slots[1:]:
                    value = value + ins[at][k, here, :].astype(F32)
                return value.astype(BF16)

            if bit is None:
                out = outs.pop(0)
                for k in range(many):
                    out[k] = total(k)
                continue
            sent, kept = outs.pop(0), outs.pop(0)
            places = [0, 0]
            for k in range(many):
                with_bit = (k >> bit) & 1
                (sent if with_bit else kept)[places[with_bit]] = total(k)
                places[with_bit] += 1

    return call("fold", body, arrays, in_specs, out_specs, out_shape, grid=(steps,))


def choose(first, second, dims, odd):
    arrays = [a for a, _ in first + second]
    views = [v for _, v in first + second]

    def body(odd_ref, *refs):
        ins, (sent, kept) = refs[: len(arrays)], refs[len(arrays) :]

        def total(begin, end):
            value = ins[begin][views[begin]].astype(F32)
            for at in range(begin + 1, end):
                value = value + ins[at][views[at]].astype(F32)
            return value.astype(BF16)

        @pl.when(odd_ref[0] == 1)
        def _():
            sent[...] = total(0, len(first))
            kept[...] = total(len(first), len(arrays))

        @pl.when(odd_ref[0] == 0)
        def _():
            kept[...] = total(0, len(first))
            sent[...] = total(len(first), len(arrays))

    return call(
        "choose", body, arrays, [IN_VMEM] * len(arrays), [IN_VMEM] * 2, [shape(dims, BF16)] * 2,
        prefetch=[odd],
    )


def place(sums, odd, out_dims, cuts):
    arrays = [a for pair in sums for a in pair]

    def body(odd_ref, *refs):
        ins, outs = refs[: len(arrays)], refs[len(arrays) :]

        def write(swapped):
            for which, half, source, at, target in cuts:
                outs[at][target] = ins[2 * which + (half ^ swapped)][source].astype(F32)

        @pl.when(odd_ref[0] == 1)
        def _():
            write(1)

        @pl.when(odd_ref[0] == 0)
        def _():
            write(0)

    return call(
        "place", body, arrays, [IN_VMEM] * len(arrays), [whole(d) for d in out_dims],
        [shape(d, F32) for d in out_dims], prefetch=[odd],
    )


def swap(x, axis, bit):
    size = lax.axis_size(axis)
    return lax.ppermute(x, axis, [(i, i ^ bit) for i in range(size)])


def bits_of(size):
    return [1 << b for b in range(size.bit_length() - 1)]


def gather_pieces(own, cut):
    rest = bits_of(lax.axis_size("dp"))[1:]
    spans = [slice(0, cut), slice(cut, own.shape[1])]
    everything = slice(0, own.shape[1])
    held = {0: [(everything, own)]}
    for bit in rest:
        held[bit] = [(everything, swap(own, "dp", bit))]
    first = [held[bit][0][1] for bit in rest]
    for at in range(1 << len(rest)):
        at = 2 * at
        if at in held:
            continue
        held[at] = []
        for span, order in zip(spans, (rest, rest[::-1])):
            last = [bit for bit in order if at & bit][-1]
            before = held[at ^ last]
            source = before[0][1][:, span] if len(before) == 1 else before[spans.index(span)][1]
            held[at].append((span, swap(source, "dp", last)))
    for at in sorted(held):
        held[at | 1] = [(span, swap(piece, "dp", 1)) for span, piece in held[at]]
    return held, first


class Sum:
    def __init__(self, kept, sent, halves, odd):
        self.rest = bits_of(lax.axis_size("dp"))[1:]
        self.order = [list(range(len(self.rest))), list(range(len(self.rest)))[::-1]]
        self.left = [list(range(len(self.rest))), list(range(len(self.rest)))]
        self.odd = odd
        arrived = [swap(s, "dp", 1) for s in sent]
        if len(kept) == 1:
            kept, arrived = kept * 2, arrived * 2
        self.terms = [[k, a] for k, a in zip(kept, arrived)]
        self.rows = halves
        self.stage = 0

    def over_dp(self, steps=1):
        bits = [order[self.stage] for order in self.order]
        items = [
            (terms, rows, left.index(bit))
            for terms, rows, left, bit in zip(self.terms, self.rows, self.left, bits)
        ]
        sent0, kept0, sent1, kept1 = fold(items, steps)
        self.terms = [
            [kept, swap(sent, "dp", self.rest[bit])]
            for kept, sent, bit in zip((kept0, kept1), (sent0, sent1), bits)
        ]
        self.rows = [(0, k.shape[1]) for k in (kept0, kept1)]
        for left, bit in zip(self.left, bits):
            left.remove(bit)
        self.stage += 1

    def joined(self):
        dims = [terms[0].shape[1:] for terms in self.terms]
        arrays = [term for terms in self.terms for term in terms]
        many = len(self.terms[0])

        def body(*refs):
            at = 0
            for part, (rows, _) in enumerate(dims):
                value = refs[part * many][0].astype(F32)
                for k in range(1, many):
                    value = value + refs[part * many + k][0].astype(F32)
                refs[-1][at : at + rows, :] = value.astype(BF16)
                at += rows

        total = (sum(rows for rows, _ in dims), dims[0][1])
        return call(
            "joined", body, arrays, [IN_VMEM] * len(arrays), [IN_VMEM], [shape(total, BF16)]
        )[0]

    def to_ctx(self):
        first, second = [[(t, 0) for t in terms] for terms in self.terms]
        self.begin_ctx(first, second, first[0][0].shape[1:])

    def begin_ctx(self, first, second, dims):
        sent, kept = choose(first, second, dims, self.odd)
        self.total, self.next = [kept, swap(sent, "ctx", 1)], bits_of(lax.axis_size("ctx"))[1:]

    def over_ctx(self):
        a, b = [t[None] for t in self.total]
        total = fold([([a, b], (0, a.shape[1]), None)])[0][0]
        if self.next:
            self.total = [total, swap(total, "ctx", self.next.pop(0))]
        else:
            self.total = [total, swap(total, "ctx", 1)]


class Line:
    def __init__(self, total):
        size = lax.axis_size("ctx")
        middle = size // 2
        self.hops = [("add", [(k, k + 1), (size - 1 - k, size - 2 - k)]) for k in range(middle - 1)]
        self.hops.append(("add", [(middle - 1, middle), (middle, middle - 1)]))
        for k in reversed(range(middle - 1)):
            self.hops.append(("take", [(k + 1, k), (size - 2 - k, size - 1 - k)]))
        self.total = total
        self.send()

    def send(self):
        self.kind, pairs = self.hops.pop(0)
        self.takers = [b for _, b in pairs]
        self.came = lax.ppermute(self.total, "ctx", pairs)

    def taking(self):
        at = lax.axis_index("ctx")
        return sum((at == taker).astype(jnp.int32) for taker in self.takers)[None]

    def step(self):
        if self.kind == "add":
            rows = self.total.shape[0]
            self.total = fold([([self.total[None], self.came[None]], (0, rows), None)])[0][0]
        else:
            self.total = jnp.where(self.taking()[0] == 1, self.came, self.total)
        self.send()

    def finish(self):
        while self.hops:
            self.step()

    def place(self, out_dims, cuts):
        cuts = [(0, 0, source, at, target) for source, at, target in cuts]
        if self.kind == "add":
            self.total, self.came = fold([([self.total[None], self.came[None]], (0, self.total.shape[0]), None)])[0][0], self.total
            return place([(self.total, self.came)], jnp.zeros((1,), jnp.int32), out_dims, cuts)
        return place([(self.total, self.came)], self.taking(), out_dims, cuts)


class Relay:
    def __init__(self, block):
        self.size = lax.axis_size("ctx")
        self.from_left, self.from_right = [], []
        self.send(block, block)

    def send(self, right, left):
        step = len(self.from_left)
        self.from_left.append(lax.ppermute(right, "ctx", [(i, i + 1) for i in range(step, self.size - 1)]))
        self.from_right.append(
            lax.ppermute(left, "ctx", [(i + 1, i) for i in range(self.size - 1 - step)])
        )

    def step(self):
        came = [self.from_left[-1], self.from_right[-1]]
        self.send(
            *copies(
                "pass_on", came, lambda _, ins, outs: list(zip(ins, outs)),
                [shape(c.shape, c.dtype) for c in came],
            )
        )

    def finish(self):
        while len(self.from_left) < self.size - 1:
            self.step()


def sum_everywhere(x):
    for axis in ("dp", "ctx"):
        for bit in bits_of(lax.axis_size(axis)):
            x = x + swap(x, axis, bit)
    return x


def on_device(
    tokens, doc_starts, attn_gain, w_query, w_key, w_value, w_out,
    query_gain, key_gain, mlp_gain, w_gate, w_up, w_down, cotangent,
):
    ORDER.clear()
    rows, width = tokens.shape[1], tokens.shape[2]
    stretch = rows // 2
    ctx_size = lax.axis_size("ctx")
    dp_size = lax.axis_size("dp")
    ctx_at = lax.axis_index("ctx")
    dp_at = lax.axis_index("dp")
    pack_rows = rows * ctx_size
    unit = width // dp_size
    inner = HEADS * HEAD_DIM
    own_tokens = tokens[0]
    grad_out = cotangent[0]
    starts = doc_starts[0]
    odd = (ctx_at % 2).astype(jnp.int32)[None]
    dp_bits = bits_of(dp_size)

    gains = jnp.concatenate(
        [attn_gain[:, None], mlp_gain[:, None], jnp.zeros((unit, HEAD_DIM - 2), BF16)], axis=1
    )

    def packing(_, ins, outs):
        at = 0
        for ref in ins:
            yield ref.at[:, :], outs[0].at[:, pl.ds(at, ref.shape[1])]
            at += ref.shape[1]

    def stacking(_, ins, outs):
        down, gate, up, out = ins
        stack_ref = outs[0]
        yield down.at[:, :], stack_ref.at[pl.ds(0, 3 * unit)]
        for i in range(3):
            cols = pl.ds(i * width, width)
            yield gate.at[:, cols], stack_ref.at[pl.ds((3 + i) * unit, unit)]
            yield up.at[:, cols], stack_ref.at[pl.ds((6 + i) * unit, unit)]
        yield out.at[:, :], stack_ref.at[pl.ds(9 * unit, 2 * unit)]

    attn_cols = inner + 2 * width + HEAD_DIM
    own_attn = copies(
        "pack_attn", [w_query, w_key, w_value, gains], packing, [shape((unit, attn_cols), BF16)],
        in_specs=[whole(w.shape) for w in (w_query, w_key, w_value)] + [IN_VMEM],
    )[0]
    pieces, first_pieces = gather_pieces(own_attn, inner)
    gathered = Relay(own_tokens)
    stack_in = copies(
        "pack_stack", [w_down, w_gate, w_up, w_out], stacking, [shape((11 * unit, width), BF16)],
        in_specs=[whole(w.shape) for w in (w_down, w_gate, w_up, w_out)],
        out_specs=[whole((11 * unit, width))],
    )[0]
    stack = lax.all_gather(stack_in, "dp", axis=0)
    gathered.step()
    touch(first_pieces)
    gathered.finish()
    from_left, from_right = gathered.from_left, gathered.from_right

    place_at = jnp.arange(pack_rows, dtype=jnp.int32)
    in_half = place_at % (pack_rows // 2)
    part, device, row = place_at // (pack_rows // 2), in_half // stretch, place_at % stretch
    key_stream = stream_index(device * rows + part * stretch + row, stretch, ctx_size)
    query_stream = stream_index(
        ctx_at * rows + jnp.arange(rows, dtype=jnp.int32), stretch, ctx_size
    )
    key_open = opening_of(key_stream, starts)
    query_open = opening_of(query_stream, starts)
    cos_pack, sin_pack = rotary(key_stream - key_open)
    cos_own, sin_own = rotary(query_stream - query_open)

    owners = (dp_at ^ jnp.arange(dp_size, dtype=jnp.int32)).astype(jnp.int32)
    listed = [(k, span, piece) for k in range(dp_size) for span, piece in pieces[k]]

    def assembling(prefetch, ins, outs):
        for (k, span, _), ref in zip(listed, ins):
            at = pl.multiple_of(prefetch[0][k] * unit, unit)
            cols = pl.ds(span.start, span.stop - span.start)
            yield ref.at[:, :], outs[0].at[pl.ds(at, unit), cols]
            if span.stop == attn_cols:
                last = ref.shape[1] - HEAD_DIM
                yield ref.at[:, pl.ds(last, HEAD_DIM)], outs[1].at[pl.ds(at, unit), :]

    attn_w, gain_cols = copies(
        "assemble_weights", [piece for _, _, piece in listed], assembling,
        [shape((width, attn_cols), BF16), shape((width, HEAD_DIM), BF16)], prefetch=[owners],
        out_specs=[whole((width, attn_cols)), IN_VMEM],
    )
    gain_rows = gain_cols[:, :2].astype(F32).T
    gain_attn, gain_mlp = gain_rows[0:1], gain_rows[1:2]
    gain_query = query_gain.astype(F32)[None, :]
    gain_key = key_gain.astype(F32)[None, :]

    normed = norm_own(own_tokens, gain_attn)
    query_raw, queries, factors = project_queries(normed, attn_w, gain_query, cos_own, sin_own)
    places = ((ctx_at - jnp.arange(ctx_size, dtype=jnp.int32)) % ctx_size).astype(jnp.int32)
    normed_pack = norm_pack(
        own_tokens, from_left, from_right, gain_attn, places, ctx_at.astype(jnp.int32)[None]
    ).reshape(pack_rows, width)
    key_raw, keys, values = project_keys_values(normed_pack, attn_w, gain_key, cos_pack, sin_pack)
    mixed, lse = attend(
        queries, keys, values, query_open[:, None], query_stream[:, None], key_stream[None, :]
    )
    output, normed_mid, hidden, d_both, middle = feed_forward(
        mixed, own_tokens, grad_out, gain_mlp, stack
    )

    order = [2 * k for k in range(dp_size // 2)] + [2 * k + 1 for k in range(dp_size // 2)]
    owners = (dp_at ^ jnp.array(order, jnp.int32)).astype(jnp.int32)
    everything = slice(None)
    ctx_steps = len(bits_of(ctx_size))
    later_dp, later_ctx = len(dp_bits) - 2, ctx_steps - 1

    def two_rows(total, half, widths=(width,)):
        cuts, at = [], 0
        for which, each in enumerate(widths):
            for k in range(2):
                to = (slice(k * half, (k + 1) * half), everything)
                cuts.append((0, k, (everything, slice(at, at + each)), which, to))
            at += each
        return place([total.total], odd, [(2 * half, each) for each in widths], cuts)

    def halves_of(pair):
        half = pair[0].shape[1] // 2
        return Sum(pair[:1], pair[1:], [(0, half), (half, half)], odd), half

    half_heads = KV_HEADS // 2
    down, down_half = halves_of(weight_grad(hidden, grad_out, owners))
    wide_grad = weight_grad(normed_mid, d_both, block=1024)[0]
    wide_grad = lax.psum_scatter(wide_grad, "dp", scatter_dimension=0, tiled=True)
    down.over_dp()
    grad_middle, grad_branch, mlp_part, grad_mixed, parcel = branch_back(
        d_both, middle, grad_out, gain_mlp, mixed, lse, factors, stack
    )
    parcels = Relay(parcel)
    for _ in range(later_dp):
        down.over_dp()
    out_kept, out_sent = weight_grad(mixed, grad_branch, owners, beside=True)
    query_args = (
        queries, grad_mixed, mixed, keys, values, lse, query_open[:, None], query_stream[:, None],
        key_stream[None, :], query_raw, gain_query, cos_own, sin_own,
    )
    d_query, query_part = query_back(*query_args, 0, half_heads)
    parcels.step()
    down = Line(down.joined())
    d_query, query_more = query_back(*query_args, half_heads, half_heads, (d_query,))
    parcels.finish()
    down.step()
    query_kept, query_sent = weight_grad(normed, d_query, owners)
    outer = Sum([out_kept, query_kept], [out_sent, query_sent], [(0, unit), (0, unit)], odd)
    wide_grad = copies(
        "take", [wide_grad], lambda _, ins, outs: [(ins[0], outs[0])], [shape(wide_grad.shape, BF16)]
    )[0]
    wide = Line(wide_grad)
    every_query = all_queries(normed_pack, attn_w, gain_query, cos_pack, sin_pack)
    touch([parcels.from_left[-1], parcels.from_right[-1]])
    down.finish()
    outer.over_dp()
    parcels = [parcel] + parcels.from_left + parcels.from_right
    grad_mixed_pack, far = all_grad_mixed(
        grad_mixed, parcels, stack, places, ctx_at.astype(jnp.int32)[None], rows
    )
    grad_mixed_pack = grad_mixed_pack.reshape(pack_rows, inner)
    far = far.transpose(2, 0, 1, 3).reshape(3 * HEADS, pack_rows)
    key_args = (
        every_query, grad_mixed_pack, keys, values, far,
        key_open[None, :], key_stream[None, :], query_stream[:, None],
        key_raw, gain_key, cos_own, sin_own, ctx_at.astype(jnp.int32)[None], ctx_size,
    )
    wide.step()
    d_pair, key_part = key_back(*key_args, 0, half_heads)
    for _ in range(later_dp):
        outer.over_dp()
    down_grad = down.place([(2 * down_half, width)], [(everything, 0, everything)])[0]
    d_pair, key_more = key_back(*key_args, half_heads, half_heads, (d_pair,))
    query_part, key_part = query_part + query_more, key_part + key_more
    outer = Line(outer.joined())
    key_kept, key_sent, value_kept, value_sent = weight_grad(normed, d_pair, owners, apart=True)
    pair = Sum([key_kept, value_kept], [key_sent, value_sent], [(0, unit), (0, unit)], odd)
    wide.finish()
    d_normed = normed_back(d_query, d_pair, attn_w)
    pair.over_dp()
    input_grad, attn_part = input_back(d_normed, own_tokens, gain_attn, grad_middle)
    for _ in range(later_dp):
        pair.over_dp()
    outer.step()
    gate_grad, up_grad = wide.place(
        [(unit, 3 * width)] * 2,
        [((everything, slice(k * 3 * width, (k + 1) * 3 * width)), k, everything) for k in range(2)],
    )
    pair.to_ctx()
    outer.finish()
    pair.over_ctx()
    near, far_half = slice(0, width), slice(width, 2 * width)
    first, second = slice(0, unit), slice(unit, 2 * unit)
    w_out_grad, query_grad = outer.place(
        [(2 * unit, width), (unit, inner)],
        [
            ((first, near), 0, (first, everything)),
            ((first, far_half), 0, (second, everything)),
            ((second, everything), 1, everything),
        ],
    )
    for _ in range(later_ctx):
        pair.over_ctx()
    key_grad, value_grad = place(
        [pair.total], odd, [(unit, width)] * 2, [(0, k, everything, k, everything) for k in range(2)]
    )

    parts = [attn_part, mlp_part, query_part, key_part]
    small = sum_everywhere(jnp.concatenate(parts, axis=1).reshape(-1, HEAD_DIM)).reshape(-1)
    attn_gain_grad = lax.dynamic_slice(small, (dp_at * unit,), (unit,))
    mlp_gain_grad = lax.dynamic_slice(small, (width + dp_at * unit,), (unit,))
    query_gain_grad = small[2 * width : 2 * width + HEAD_DIM]
    key_gain_grad = small[2 * width + HEAD_DIM :]
    return (
        output[None], input_grad[None], attn_gain_grad, query_grad, key_grad, value_grad, w_out_grad,
        query_gain_grad, key_gain_grad, mlp_gain_grad, gate_grad, up_grad, down_grad,
    )


def solution(mesh):
    in_specs = (
        P("dp", "ctx", None),
        P("dp", None),
        P("dp"),
        P("dp", None),
        P("dp", None),
        P("dp", None),
        P("dp", None),
        P(),
        P(),
        P("dp"),
        P("dp", None),
        P("dp", None),
        P("dp", None),
        P("dp", "ctx", None),
    )
    out_specs = (
        P("dp", "ctx", None),
        P("dp", "ctx", None),
        P("dp"),
        P("dp", None),
        P("dp", None),
        P("dp", None),
        P("dp", None),
        P(),
        P(),
        P("dp"),
        P("dp", None),
        P("dp", None),
        P("dp", None),
    )
    return jax.shard_map(
        on_device, mesh=mesh, in_specs=in_specs, out_specs=out_specs, check_vma=False
    )
```

time: 588 us -> 536 us (0.912)
  local copies, waits for them, and re-layouts: 54.4 us -> 31.1 us
  Pallas kernels: 265 us -> 242 us
  starting transfers between devices: 79 us -> 91 us
  waiting for transfers between devices: 156 us -> 144 us
    ppermute x51 -> x34, waiting for transfers between devices: 149 us -> 94.8 us  [swap(): return lax.ppermute(x, axis, [(i, i ^ bit) for i in range(size)])]
    ppermute x6 -> x21, starting transfers between devices: 13.4 us -> 60.9 us  [the longest x9 38.2 us: send(): self.came = lax.ppermute(self.total, 'ctx', pairs)]
    ppermute x51 -> x34, starting transfers between devices: 65.4 us -> 30 us  [swap(): return lax.ppermute(x, axis, [(i, i ^ bit) for i in range(size)])]
    ppermute x6 -> x21, waiting for transfers between devices: 7.67 us -> 41.1 us  [the longest x9 26.6 us: send(): self.came = lax.ppermute(self.total, 'ctx', pairs)]
    unnamed x163 -> x124, local copies, waits for them, and re-layouts: 49.4 us -> 22 us
    pallas_call x57 -> x51, Pallas kernels: 265 us -> 242 us  [call(): pl.pallas_call(without, grid_spec=pltpu.PrefetchScalarGridSpec(num_scalar...]
  transfers between devices with their start and end apart: 60 -> 57, of which waited for: 22 -> 19; matrix products, arithmetic and copies ran while one was open for 2% -> 3% of each run, Pallas kernels for 37% -> 38%
where the time goes in v2:
time: 536 us; the launch traced here: 530 us
  Pallas kernels  242 us (45%)
  waiting for transfers between devices  144 us (27%)
  starting transfers between devices  91 us (17%)
  local copies, waits for them, and re-layouts  31.1 us (6%)
  between operations  15.3 us (3%)
  other arithmetic  7.42 us (1%)
    pallas_call x51, Pallas kernels, call(): pl.pallas_call(without, grid_spec=pltpu.PrefetchScalarGridSpec(num_scalar...  242 us
    ppermute x34, waiting for transfers between devices, swap(): return lax.ppermute(x, axis, [(i, i ^ bit) for i in range(size)])  94.8 us
    ppermute x9, starting transfers between devices, send(): self.came = lax.ppermute(self.total, 'ctx', pairs)  38.2 us
    ppermute x34, starting transfers between devices, swap(): return lax.ppermute(x, axis, [(i, i ^ bit) for i in range(size)])  30 us
    ppermute x9, waiting for transfers between devices, send(): self.came = lax.ppermute(self.total, 'ctx', pairs)  26.6 us
    unnamed x124, local copies, waits for them, and re-layouts  22 us
    ppermute x6, starting transfers between devices, send(): lax.ppermute(right, 'ctx', [(i, i + 1) for i in range(step, self.size - 1)])  14.8 us
    ppermute x6, waiting for transfers between devices, send(): lax.ppermute(left, 'ctx', [(i + 1, i) for i in range(self.size - 1 - step)])  13.3 us
  transfers between devices with their start and end apart: 57, of which 19 were waited for; matrix products, arithmetic and copies ran while one was open for 3% of the time, Pallas kernels for 38%

profile of v2, /device:TPU:0, one launch (start us, length us, event | category | flops | bytes accessed | tf_op | source)
XLA Modules:
  0.0 530.2 jit_solution(3463269022967850030)
XLA Ops:
  17.1 5.6 %collective-permute-start.9 = (bf16[384,1024]{1,0:T(8,128)(2,1)S(1)}, bf16[384,1024]{1,0:T(8,128)(2,1)S(1)}, u32[]{:S(2)}, u32[]{:S(2)}) collective-permute-start(bf16[384,1024]{1,0:T(8,128)(2,1)S(1)} %bitcast.55), channel_id=1, source_target_pairs={{0,1},{1,2},{2,3},{4,5},{5,6},{6,7},{8,9},{9,10},{10,11},{12,13},{... | collective-permute-start | bytes 2359304 | tf_op jit(solution)/shard_map/ppermute | solution.py:1091
  30.9 7.4 %collective-permute-done.10.refs_1_.refs_7_ = bf16[384,1024]{1,0:T(8,128)(2,1)S(1)} collective-permute-done((bf16[384,1024]{1,0:T(8,128)(2,1)S(1)}, bf16[384,1024]{1,0:T(8,128)(2,1)S(1)}, u32[]{:S(2)}, u32[]{:S(2)}) %collective-permute-start.10) | collective-permute-done | bytes 786464 | tf_op jit(solution)/shard_map/ppermute | solution.py:1093
  43.0 28.6 %collective-permute-done.1.refs_1_.refs_3_ = bf16[128,4224]{1,0:T(8,128)(2,1)} collective-permute-done((bf16[128,4224]{1,0:T(8,128)(2,1)}, bf16[128,4224]{1,0:T(8,128)(2,1)}, u32[]{:S(2)}, u32[]{:S(2)}) %collective-permute-start.1) | collective-permute-done | bytes 1081376 | tf_op jit(solution)/shard_map/ppermute | solution.py:948
  78.7 11.9 %collective-permute-done.5.refs_7_ = bf16[128,2048]{1,0:T(8,128)(2,1)} collective-permute-done((bf16[128,2048]{1,0:T(8,128)(2,1)}, bf16[128,2048]{1,0:T(8,128)(2,1)}, u32[]{:S(2)}, u32[]{:S(2)}) %collective-permute-start.5) | collective-permute-done | bytes 524320 | tf_op jit(solution)/shard_map/ppermute | solution.py:948
  100.8 6.8 %assemble_weights.1 = (bf16[1024,4224]{1,0:T(8,128)(2,1)}, bf16[1024,128]{1,0:T(8,128)(2,1)S(1)}, f32[8,128]{1,0:T(8,128)S(1)}) custom-call(s32[8]{0:T(128)S(1)} %iota_xor_fusion.refs_0_, bf16[128,4224]{1,0:T(8,128)(2,1)} %get-tuple-element.162.refs_1_, bf16[128,4224]{1,0:T(8,128)(2,1)} %collective-permute-done.refs_2_, ...), custom_call_target="tpu_custom_call" | custom-call | tf_op jit(solution)/shard_map/assemble_weights/pallas_call | solution.py:64
  109.6 9.0 %project_queries.1 = (bf16[384,2048]{1,0:T(8,128)(2,1)}, bf16[384,2048]{1,0:T(8,128)(2,1)}, f32[16,8,384]{2,1,0:T(8,128)S(1)}, f32[8,128]{1,0:T(8,128)S(1)}) custom-call(bf16[384,1024]{1,0:T(8,128)(2,1)S(1)} %get-tuple-element.171.refs_0_.refs_1_, bf16[1024,4224]{1,0:T(8,128)(2,1)} %get-tuple-element.172.refs_1_.refs_2_.refs_3_.refs_4_, ...), custom_call_target="tpu_custom_call" | custom-call | tf_op jit(solution)/shard_map/project_queries/pallas_call | solution.py:64
  120.9 5.0 norm_pack.1
  127.8 12.9 %project_keys_values.1 = (bf16[1536,1024]{1,0:T(8,128)(2,1)}, bf16[1536,1024]{1,0:T(8,128)(2,1)}, bf16[1536,1024]{1,0:T(8,128)(2,1)}, f32[8,128]{1,0:T(8,128)S(1)}) custom-call(bf16[1536,1024]{1,0:T(8,128)(2,1)S(1)} %bitcast.60, bf16[1024,4224]{1,0:T(8,128)(2,1)} %get-tuple-element.172.refs_1_.refs_2_.refs_3_.refs_4_, ...), custom_call_target="tpu_custom_call" | custom-call | tf_op jit(solution)/shard_map/project_keys_values/pallas_call | solution.py:64
  140.7 13.9 %attend.1 = (bf16[384,2048]{1,0:T(8,128)(2,1)}, f32[16,8,384]{2,1,0:T(8,128)S(1)}, f32[8,128]{1,0:T(8,128)S(1)}) custom-call(bf16[384,2048]{1,0:T(8,128)(2,1)} %get-tuple-element.174.refs_0_, bf16[1536,1024]{1,0:T(8,128)(2,1)} %get-tuple-element.180.refs_1_.refs_3_, bf16[1536,1024]{1,0:T(8,128)(2,1)} %get-tuple-element.181.refs_2_.refs_4_, ...), custom_call_target="tpu_custom_call" | custom-call | tf_op jit(solution)/shard_map/attend/pallas_call | solution.py:64
  154.6 5.5 %all-gather.3.cloned.1.call-done = bf16[11264,1024]{1,0:T(8,128)(2,1)} async-done(((bf16[1408,1024]{1,0:T(8,128)(2,1)}), bf16[11264,1024]{1,0:T(8,128)(2,1)}) %all-gather.3.cloned.1.call-update) | async-done | bytes 23068688 | tf_op jit(solution)/shard_map/all_gather | solution.py:1169
  161.5 18.3 %feed_forward.1 = (bf16[384,1024]{1,0:T(8,128)(2,1)}, bf16[384,1024]{1,0:T(8,128)(2,1)S(1)}, bf16[384,3072]{1,0:T(8,128)(2,1)S(1)}, bf16[2,384,3072]{2,1,0:T(8,1...) custom-call(bf16[384,2048]{1,0:T(8,128)(2,1)S(1)} %copy-done, bf16[384,1024]{1,0:T(8,128)(2,1)S(1)} %bitcast.58, ...), custom_call_target="tpu_custom_call" | custom-call | tf_op jit(solution)/shard_map/feed_forward/pallas_call | solution.py:64
  179.8 4.9 weight_grad.5
  186.4 9.5 %weight_grad.6 = (bf16[1024,6144]{1,0:T(8,128)(2,1)}, f32[8,128]{1,0:T(8,128)S(1)}) custom-call(bf16[384,1024]{1,0:T(8,128)(2,1)S(1)} %get-tuple-element.195.refs_0_, bf16[2,384,3072]{2,1,0:T(8,128)(2,1)S(1)} %get-tuple-element.187.refs_1_.refs_0_, f32[8,128]{1,0:T(8,128)S(1)} %get-tuple-element.196.refs_2_), custom_call_target="tpu_custom_call" | custom-call | tf_op jit(solution)/shard_map/weight_grad/pallas_call | solution.py:64
  198.4 5.6 %collective-permute-done.15.refs_1_ = bf16[4,384,1024]{2,1,0:T(8,128)(2,1)S(1)} collective-permute-done((bf16[4,384,1024]{2,1,0:T(8,128)(2,1)}, bf16[4,384,1024]{2,1,0:T(8,128)(2,1)S(1)}, u32[]{:S(2)}, u32[]{:S(2)}) %collective-permute-start.15) | collective-permute-done | bytes 3145760 | tf_op jit(solution)/shard_map/ppermute | solution.py:948
  210.5 19.5 %branch_back.1 = (f32[384,1024]{1,0:T(8,128)}, bf16[384,1024]{1,0:T(8,128)(2,1)S(1)}, f32[1,1024]{1,0:T(1,128)S(1)}, bf16[384,2048]{1,0:T(8,128)(2,1)}, bf16[432...) custom-call(bf16[2,384,3072]{2,1,0:T(8,128)(2,1)S(1)} %copy-done.3, f32[384,1024]{1,0:T(8,128)S(1)} %copy-done.40, ...), custom_call_target="tpu_custom_call" | custom-call | tf_op jit(solution)/shard_map/branch_back/pallas_call | solution.py:64
  231.3 4.6 collective-permute-start.20
  239.3 4.8 weight_grad.7
  244.1 13.6 %query_back.2 = (bf16[384,2048]{1,0:T(8,128)(2,1)}, f32[1,128]{1,0:T(1,128)S(1)}, f32[8,128]{1,0:T(8,128)S(1)}) custom-call(bf16[384,2048]{1,0:T(8,128)(2,1)} %get-tuple-element.174.refs_0_, bf16[384,2048]{1,0:T(8,128)(2,1)} %get-tuple-element.199.refs_1_.refs_2_, bf16[384,2048]{1,0:T(8,128)(2,1)} %get-tuple-element.183.refs_0_.refs_4_.refs_1_.refs_2_, ...), custom_call_target="tpu_custom_call" | custom-call | tf_op jit(solution)/shard_map/query_back/pallas_call | solution.py:64
  260.1 6.8 %collective-permute-start.22 = (bf16[384,1024]{1,0:T(8,128)(2,1)S(1)}, bf16[384,1024]{1,0:T(8,128)(2,1)S(1)}, u32[]{:S(2)}, u32[]{:S(2)}) collective-permute-start(bf16[384,1024]{1,0:T(8,128)(2,1)S(1)} %get-tuple-element.220), channel_id=1, source_target_pairs={{0,1},{3,2},{4,5},{7,6},{8,9},{11,10},{12,13},{15,14},{16,17},{19,... | collective-permute-start | bytes 2359304 | tf_op jit(solution)/shard_map/ppermute | solution.py:1057
  267.0 12.8 %query_back.3 = (bf16[384,2048]{1,0:T(8,128)(2,1)}, f32[1,128]{1,0:T(1,128)S(1)}, f32[8,128]{1,0:T(8,128)S(1)}) custom-call(bf16[384,2048]{1,0:T(8,128)(2,1)} %get-tuple-element.174.refs_0_, bf16[384,2048]{1,0:T(8,128)(2,1)} %get-tuple-element.199.refs_1_.refs_2_, ...), custom_call_target="tpu_custom_call", output_to_operand_aliasing={{0}: (13, {})} | custom-call | tf_op jit(solution)/shard_map/query_back/pallas_call | solution.py:64
  286.2 4.5 weight_grad.8
  301.8 4.6 collective-permute-start.30
  308.3 12.3 %all_queries.1 = (bf16[1536,2048]{1,0:T(8,128)(2,1)}, f32[8,128]{1,0:T(8,128)S(1)}) custom-call(bf16[1536,1024]{1,0:T(8,128)(2,1)S(1)} %bitcast.61, bf16[1024,4224]{1,0:T(8,128)(2,1)} %get-tuple-element.172.refs_1_.refs_2_.refs_3_.refs_4_, f32[1,128]{1,0:T(1,128)S(1)} %bitcast_convert_fusion.1.refs_2_.refs_10_, f32[1536,128]{1,0:T(8,128)S(1)} %copy-done.15, ...), custom_call_target="tpu_custom_call" | custom-call | tf_op jit(solution)/shard_map/all_queries/pallas_call | solution.py:64
  332.6 10.8 %all_grad_mixed.1 = (bf16[2,4,192,2048]{3,2,1,0:T(8,128)(2,1)}, f32[2,4,48,192]{3,2,1,0:T(8,128)S(1)}, f32[8,128]{1,0:T(8,128)S(1)}) custom-call(s32[4]{0:T(128)S(1)} %and_select_fusion.6.refs_0_, s32[1]{0:T(128)} %bitcast.6.refs_1_.refs_0_, bf16[384,2048]{1,0:T(8,128)(2,1)S(1)} %copy-done.4, bf16[8,1408,1024]{2,1,0:T(8,128)(2,1)} %bitcast.81, ...), custom_call_target="tpu_custom_call" | custom-call | tf_op jit(solution)/shard_map/all_grad_mixed/pallas_call | solution.py:64
  349.2 12.8 %key_back.2 = (bf16[2,384,1024]{2,1,0:T(8,128)(2,1)}, f32[1,128]{1,0:T(1,128)S(1)}, f32[8,128]{1,0:T(8,128)S(1)}) custom-call(s32[1]{0:T(128)} %bitcast.6.refs_1_.refs_0_, bf16[1536,2048]{1,0:T(8,128)(2,1)} %get-tuple-element.228.refs_1_, bf16[1536,2048]{1,0:T(8,128)(2,1)} %bitcast.87, bf16[2,4,192,1024]{3,2,1,0:T(8,128)(2,1)} %bitcast.83, ...), custom_call_target="tpu_custom_call" | custom-call | tf_op jit(solution)/shard_map/key_back/pallas_call | solution.py:64
  372.7 12.5 %key_back.3 = (bf16[2,384,1024]{2,1,0:T(8,128)(2,1)}, f32[1,128]{1,0:T(1,128)S(1)}, f32[8,128]{1,0:T(8,128)S(1)}) custom-call(s32[1]{0:T(128)} %bitcast.6.refs_1_.refs_0_, bf16[1536,2048]{1,0:T(8,128)(2,1)} %get-tuple-element.228.refs_1_, bf16[1536,2048]{1,0:T(8,128)(2,1)} %bitcast.88, ...), custom_call_target="tpu_custom_call", output_to_operand_aliasing={{0}: (13, {})} | custom-call | tf_op jit(solution)/shard_map/key_back/pallas_call | solution.py:64
  390.6 17.6 %collective-permute-start.44 = (bf16[256,2048]{1,0:T(8,128)(2,1)S(1)}, bf16[256,2048]{1,0:T(8,128)(2,1)S(1)}, u32[]{:S(2)}, u32[]{:S(2)}) collective-permute-start(bf16[256,2048]{1,0:T(8,128)(2,1)S(1)} %get-tuple-element.279), channel_id=1, source_target_pairs={{0,1},{3,2},{4,5},{7,6},{8,9},{11,10},{12,13},{15,14},{16,17},{19,... | collective-permute-start | bytes 3145736 | tf_op jit(solution)/shard_map/ppermute | solution.py:1057
  411.6 7.2 %normed_back.1 = (f32[384,1024]{1,0:T(8,128)}, f32[8,128]{1,0:T(8,128)S(1)}) custom-call(bf16[384,2048]{1,0:T(8,128)(2,1)S(1)} %copy-done.5, bf16[2,384,1024]{2,1,0:T(8,128)(2,1)S(1)} %copy-done.6, bf16[1024,4224]{1,0:T(8,128)(2,1)} %get-tuple-element.172.refs_1_.refs_2_.refs_3_.refs_4_, ...), custom_call_target="tpu_custom_call" | custom-call | tf_op jit(solution)/shard_map/normed_back/pallas_call | solution.py:64
  424.4 8.6 %collective-permute-done.45.refs_1_ = bf16[2,128,1024]{2,1,0:T(8,128)(2,1)S(1)} collective-permute-done((bf16[2,128,1024]{2,1,0:T(8,128)(2,1)S(1)}, bf16[2,128,1024]{2,1,0:T(8,128)(2,1)S(1)}, u32[]{:S(2)}, u32[]{:S(2)}) %collective-permute-start.45) | collective-permute-done | bytes 524320 | tf_op jit(solution)/shard_map/ppermute | solution.py:948
  438.0 26.6 %collective-permute-done.50.refs_2_ = bf16[128,6144]{1,0:T(8,128)(2,1)S(1)} collective-permute-done((bf16[128,6144]{1,0:T(8,128)(2,1)}, bf16[128,6144]{1,0:T(8,128)(2,1)S(1)}, u32[]{:S(2)}, u32[]{:S(2)}) %collective-permute-start.50) | collective-permute-done | bytes 1572896 | tf_op jit(solution)/shard_map/ppermute | solution.py:1057
  476.8 22.7 %collective-permute-done.52 = bf16[128,1024]{1,0:T(8,128)(2,1)S(1)} collective-permute-done((bf16[128,1024]{1,0:T(8,128)(2,1)S(1)}, bf16[128,1024]{1,0:T(8,128)(2,1)S(1)}, u32[]{:S(2)}, u32[]{:S(2)}) %collective-permute-start.52) | collective-permute-done | bytes 262176 | tf_op jit(solution)/shard_map/ppermute | solution.py:948
  517.2 4.9 collective-permute-done.54.refs_2_
  (301 shorter events, 163.1 us)
Async XLA Ops:
  7.2 152.9 %all-gather.3.cloned.1.call-start = ((), (), s32[]{:S(2)}) async-start(), calls=%async_computation.2 | async-start | bytes 25952256 | tf_op jit(solution)/shard_map/all_gather | solution.py:1169
  14.7 284.3 %reduce-scatter.2.cloned.1.call-start = ((), (), s32[]{:S(2)}) async-start(), calls=%async_computation.1 | async-start | bytes 14155776 | tf_op jit(solution)/shard_map/reduce_scatter | solution.py:1245
  22.7 50.9 %collective-permute-start.3 = (bf16[128,4224]{1,0:T(8,128)(2,1)}, bf16[128,4224]{1,0:T(8,128)(2,1)}, u32[]{:S(2)}, u32[]{:S(2)}) collective-permute-start(bf16[128,4224]{1,0:T(8,128)(2,1)} %get-tuple-element.162.refs_1_), channel_id=1, source_target_pairs={{0,16},{4,20},{8,24},{12,28},{16,0},{20,4},{24,8},{28,12},{1,17},{... | collective-permute-start | bytes 3244040 | tf_op jit(solution)/shard_map/ppermute | solution.py:948
  24.7 46.8 %collective-permute-start.1 = (bf16[128,4224]{1,0:T(8,128)(2,1)}, bf16[128,4224]{1,0:T(8,128)(2,1)}, u32[]{:S(2)}, u32[]{:S(2)}) collective-permute-start(bf16[128,4224]{1,0:T(8,128)(2,1)} %get-tuple-element.162.refs_1_), channel_id=1, source_target_pairs={{0,8},{4,12},{8,0},{12,4},{16,24},{20,28},{24,16},{28,20},{1,9},{5... | collective-permute-start | bytes 3244040 | tf_op jit(solution)/shard_map/ppermute | solution.py:948
  26.2 70.9 %collective-permute-start = (bf16[128,4224]{1,0:T(8,128)(2,1)}, bf16[128,4224]{1,0:T(8,128)(2,1)}, u32[]{:S(2)}, u32[]{:S(2)}) collective-permute-start(bf16[128,4224]{1,0:T(8,128)(2,1)} %get-tuple-element.162.refs_1_), channel_id=1, source_target_pairs={{0,4},{4,0},{8,12},{12,8},{16,20},{20,16},{24,28},{28,24},{1,5},{5... | collective-permute-start | bytes 3244040 | tf_op jit(solution)/shard_map/ppermute | solution.py:948
  40.9 36.5 %collective-permute-start.11 = (bf16[384,1024]{1,0:T(8,128)(2,1)}, bf16[384,1024]{1,0:T(8,128)(2,1)S(1)}, u32[]{:S(2)}, u32[]{:S(2)}) collective-permute-start(bf16[384,1024]{1,0:T(8,128)(2,1)} %get-tuple-element.165), channel_id=1, source_target_pairs={{1,2},{2,3},{5,6},{6,7},{9,10},{10,11},{13,14},{14,15},{17,18},{18... | collective-permute-start | bytes 2359304 | tf_op jit(solution)/shard_map/ppermute | solution.py:1091
  41.6 36.6 %collective-permute-start.12 = (bf16[384,1024]{1,0:T(8,128)(2,1)}, bf16[384,1024]{1,0:T(8,128)(2,1)}, u32[]{:S(2)}, u32[]{:S(2)}) collective-permute-start(bf16[384,1024]{1,0:T(8,128)(2,1)} %get-tuple-element.166), channel_id=1, source_target_pairs={{1,0},{2,1},{5,4},{6,5},{9,8},{10,9},{13,12},{14,13},{17,16},{18,1... | collective-permute-start | bytes 2359304 | tf_op jit(solution)/shard_map/ppermute | solution.py:1093
  206.7 29.2 %collective-permute-start.16 = (bf16[2,192,1024]{2,1,0:T(8,128)(2,1)S(1)}, bf16[2,192,1024]{2,1,0:T(8,128)(2,1)S(1)}, u32[]{:S(2)}, u32[]{:S(2)}) collective-permute-start(bf16[2,192,1024]{2,1,0:T(8,128)(2,1)S(1)} %get-tuple-element.203), channel_id=1, source_target_pairs={{0,8},{4,12},{8,0},{12,4},{16,24},{20,28},{24,16},{28,20},{1,9},{5... | collective-permute-start | bytes 2359304 | tf_op jit(solution)/shard_map/ppermute | solution.py:948
  208.3 27.6 %collective-permute-start.17 = (bf16[2,192,1024]{2,1,0:T(8,128)(2,1)S(1)}, bf16[2,192,1024]{2,1,0:T(8,128)(2,1)S(1)}, u32[]{:S(2)}, u32[]{:S(2)}) collective-permute-start(bf16[2,192,1024]{2,1,0:T(8,128)(2,1)S(1)} %get-tuple-element.205), channel_id=1, source_target_pairs={{0,16},{4,20},{8,24},{12,28},{16,0},{20,4},{24,8},{28,12},{1,17},{... | collective-permute-start | bytes 2359304 | tf_op jit(solution)/shard_map/ppermute | solution.py:948
  230.0 27.6 %collective-permute-start.21 = (bf16[432,1024]{1,0:T(8,128)(2,1)S(1)}, bf16[432,1024]{1,0:T(8,128)(2,1)S(1)}, u32[]{:S(2)}, u32[]{:S(2)}) collective-permute-start(bf16[432,1024]{1,0:T(8,128)(2,1)S(1)} %get-tuple-element.214.refs_5_), channel_id=1, source_target_pairs={{1,0},{2,1},{3,2},{5,4},{6,5},{7,6},{9,8},{10,9},{11,10},{13,12},{... | collective-permute-start | bytes 2654216 | tf_op jit(solution)/shard_map/ppermute | solution.py:1093
  231.3 26.4 %collective-permute-start.20 = (bf16[432,1024]{1,0:T(8,128)(2,1)S(1)}, bf16[432,1024]{1,0:T(8,128)(2,1)S(1)}, u32[]{:S(2)}, u32[]{:S(2)}) collective-permute-start(bf16[432,1024]{1,0:T(8,128)(2,1)S(1)} %get-tuple-element.214.refs_5_), channel_id=1, source_target_pairs={{0,1},{1,2},{2,3},{4,5},{5,6},{6,7},{8,9},{9,10},{10,11},{12,13},{... | collective-permute-start | bytes 2654216 | tf_op jit(solution)/shard_map/ppermute | solution.py:1091
  258.5 24.9 %collective-permute-start.24 = (bf16[432,1024]{1,0:T(8,128)(2,1)S(1)}, bf16[432,1024]{1,0:T(8,128)(2,1)S(1)}, u32[]{:S(2)}, u32[]{:S(2)}) collective-permute-start(bf16[432,1024]{1,0:T(8,128)(2,1)S(1)} %get-tuple-element.222), channel_id=1, source_target_pairs={{1,0},{2,1},{5,4},{6,5},{9,8},{10,9},{13,12},{14,13},{17,16},{18,1... | collective-permute-start | bytes 2654216 | tf_op jit(solution)/shard_map/ppermute | solution.py:1093
  260.1 24.6 %collective-permute-start.22 = (bf16[384,1024]{1,0:T(8,128)(2,1)S(1)}, bf16[384,1024]{1,0:T(8,128)(2,1)S(1)}, u32[]{:S(2)}, u32[]{:S(2)}) collective-permute-start(bf16[384,1024]{1,0:T(8,128)(2,1)S(1)} %get-tuple-element.220), channel_id=1, source_target_pairs={{0,1},{3,2},{4,5},{7,6},{8,9},{11,10},{12,13},{15,14},{16,17},{19,... | collective-permute-start | bytes 2359304 | tf_op jit(solution)/shard_map/ppermute | solution.py:1057
  266.9 56.3 %collective-permute-start.27 = (bf16[4,128,2048]{2,1,0:T(8,128)(2,1)}, bf16[4,128,2048]{2,1,0:T(8,128)(2,1)}, u32[]{:S(2)}, u32[]{:S(2)}) collective-permute-start(bf16[4,128,2048]{2,1,0:T(8,128)(2,1)} %get-tuple-element.232), channel_id=1, source_target_pairs={{0,4},{4,0},{8,12},{12,8},{16,20},{20,16},{24,28},{28,24},{1,5},{5... | collective-permute-start | bytes 6291464 | tf_op jit(solution)/shard_map/ppermute | solution.py:948
  292.1 31.1 %collective-permute-start.28 = (bf16[4,128,2048]{2,1,0:T(8,128)(2,1)}, bf16[4,128,2048]{2,1,0:T(8,128)(2,1)}, u32[]{:S(2)}, u32[]{:S(2)}) collective-permute-start(bf16[4,128,2048]{2,1,0:T(8,128)(2,1)} %get-tuple-element.234), channel_id=1, source_target_pairs={{0,4},{4,0},{8,12},{12,8},{16,20},{20,16},{24,28},{28,24},{1,5},{5... | collective-permute-start | bytes 6291464 | tf_op jit(solution)/shard_map/ppermute | solution.py:948
  293.7 26.9 %collective-permute-start.26 = (bf16[432,1024]{1,0:T(8,128)(2,1)}, bf16[432,1024]{1,0:T(8,128)(2,1)}, u32[]{:S(2)}, u32[]{:S(2)}) collective-permute-start(bf16[432,1024]{1,0:T(8,128)(2,1)} %get-tuple-element.230), channel_id=1, source_target_pairs={{1,0},{5,4},{9,8},{13,12},{17,16},{21,20},{25,24},{29,28}} | collective-permute-start | bytes 2654216 | tf_op jit(solution)/shard_map/ppermute | solution.py:1093
  294.9 25.6 %collective-permute-start.29 = (bf16[384,1024]{1,0:T(8,128)(2,1)}, bf16[384,1024]{1,0:T(8,128)(2,1)}, u32[]{:S(2)}, u32[]{:S(2)}) collective-permute-start(bf16[384,1024]{1,0:T(8,128)(2,1)} %bitcast.15), channel_id=1, source_target_pairs={{1,2},{2,1},{5,6},{6,5},{9,10},{10,9},{13,14},{14,13},{17,18},{18,... | collective-permute-start | bytes 2359304 | tf_op jit(solution)/shard_map/ppermute | solution.py:1057
  301.8 44.0 %collective-permute-start.30 = (bf16[128,6144]{1,0:T(8,128)(2,1)}, bf16[128,6144]{1,0:T(8,128)(2,1)}, u32[]{:S(2)}, u32[]{:S(2)}) collective-permute-start(bf16[128,6144]{1,0:T(8,128)(2,1)} %get-tuple-element.242), channel_id=1, source_target_pairs={{0,1},{3,2},{4,5},{7,6},{8,9},{11,10},{12,13},{15,14},{16,17},{19,... | collective-permute-start | bytes 4718600 | tf_op jit(solution)/shard_map/ppermute | solution.py:1057
  329.3 32.7 %collective-permute-start.32 = (bf16[2,128,2048]{2,1,0:T(8,128)(2,1)}, bf16[2,128,2048]{2,1,0:T(8,128)(2,1)}, u32[]{:S(2)}, u32[]{:S(2)}) collective-permute-start(bf16[2,128,2048]{2,1,0:T(8,128)(2,1)} %get-tuple-element.248), channel_id=1, source_target_pairs={{0,8},{4,12},{8,0},{12,4},{16,24},{20,28},{24,16},{28,20},{1,9},{5... | collective-permute-start | bytes 3145736 | tf_op jit(solution)/shard_map/ppermute | solution.py:948
  330.6 31.4 %collective-permute-start.33 = (bf16[2,128,2048]{2,1,0:T(8,128)(2,1)}, bf16[2,128,2048]{2,1,0:T(8,128)(2,1)}, u32[]{:S(2)}, u32[]{:S(2)}) collective-permute-start(bf16[2,128,2048]{2,1,0:T(8,128)(2,1)} %get-tuple-element.250), channel_id=1, source_target_pairs={{0,16},{4,20},{8,24},{12,28},{16,0},{20,4},{24,8},{28,12},{1,17},{... | collective-permute-start | bytes 3145736 | tf_op jit(solution)/shard_map/ppermute | solution.py:948
  331.3 38.8 %collective-permute-start.31 = (bf16[384,1024]{1,0:T(8,128)(2,1)}, bf16[384,1024]{1,0:T(8,128)(2,1)}, u32[]{:S(2)}, u32[]{:S(2)}) collective-permute-start(bf16[384,1024]{1,0:T(8,128)(2,1)} %bitcast.26.refs_1_), channel_id=1, source_target_pairs={{1,0},{2,3},{5,4},{6,7},{9,8},{10,11},{13,12},{14,15},{17,16},{18,... | collective-permute-start | bytes 2359304 | tf_op jit(solution)/shard_map/ppermute | solution.py:1057
  368.2 40.0 %collective-permute-start.34 = (bf16[128,6144]{1,0:T(8,128)(2,1)}, bf16[128,6144]{1,0:T(8,128)(2,1)}, u32[]{:S(2)}, u32[]{:S(2)}) collective-permute-start(bf16[128,6144]{1,0:T(8,128)(2,1)} %bitcast.27), channel_id=1, source_target_pairs={{1,2},{2,1},{5,6},{6,5},{9,10},{10,9},{13,14},{14,13},{17,18},{18,... | collective-permute-start | bytes 4718600 | tf_op jit(solution)/shard_map/ppermute | solution.py:1057
  390.0 28.8 %collective-permute-start.37 = (bf16[4,128,1024]{2,1,0:T(8,128)(2,1)S(1)}, bf16[4,128,1024]{2,1,0:T(8,128)(2,1)S(1)}, u32[]{:S(2)}, u32[]{:S(2)}) collective-permute-start(bf16[4,128,1024]{2,1,0:T(8,128)(2,1)S(1)} %get-tuple-element.267), channel_id=1, source_target_pairs={{0,4},{4,0},{8,12},{12,8},{16,20},{20,16},{24,28},{28,24},{1,5},{5... | collective-permute-start | bytes 3145736 | tf_op jit(solution)/shard_map/ppermute | solution.py:948
  390.1 28.7 %collective-permute-start.38 = (bf16[4,128,1024]{2,1,0:T(8,128)(2,1)S(1)}, bf16[4,128,1024]{2,1,0:T(8,128)(2,1)S(1)}, u32[]{:S(2)}, u32[]{:S(2)}) collective-permute-start(bf16[4,128,1024]{2,1,0:T(8,128)(2,1)S(1)} %get-tuple-element.269), channel_id=1, source_target_pairs={{0,4},{4,0},{8,12},{12,8},{16,20},{20,16},{24,28},{28,24},{1,5},{5... | collective-permute-start | bytes 3145736 | tf_op jit(solution)/shard_map/ppermute | solution.py:948
  390.6 43.5 %collective-permute-start.44 = (bf16[256,2048]{1,0:T(8,128)(2,1)S(1)}, bf16[256,2048]{1,0:T(8,128)(2,1)S(1)}, u32[]{:S(2)}, u32[]{:S(2)}) collective-permute-start(bf16[256,2048]{1,0:T(8,128)(2,1)S(1)} %get-tuple-element.279), channel_id=1, source_target_pairs={{0,1},{3,2},{4,5},{7,6},{8,9},{11,10},{12,13},{15,14},{16,17},{19,... | collective-permute-start | bytes 3145736 | tf_op jit(solution)/shard_map/ppermute | solution.py:1057
  421.1 43.6 %collective-permute-start.50 = (bf16[128,6144]{1,0:T(8,128)(2,1)}, bf16[128,6144]{1,0:T(8,128)(2,1)S(1)}, u32[]{:S(2)}, u32[]{:S(2)}) collective-permute-start(bf16[128,6144]{1,0:T(8,128)(2,1)} %bitcast.36.refs_1_), channel_id=1, source_target_pairs={{1,0},{2,3},{5,4},{6,7},{9,8},{10,11},{13,12},{14,15},{17,16},{18,... | collective-permute-start | bytes 4718600 | tf_op jit(solution)/shard_map/ppermute | solution.py:1057
  434.3 34.7 %collective-permute-start.47 = (bf16[256,2048]{1,0:T(8,128)(2,1)S(1)}, bf16[256,2048]{1,0:T(8,128)(2,1)}, u32[]{:S(2)}, u32[]{:S(2)}) collective-permute-start(bf16[256,2048]{1,0:T(8,128)(2,1)S(1)} %bitcast.69), channel_id=1, source_target_pairs={{1,2},{2,1},{5,6},{6,5},{9,10},{10,9},{13,14},{14,13},{17,18},{18,... | collective-permute-start | bytes 3145736 | tf_op jit(solution)/shard_map/ppermute | solution.py:1057
  436.0 31.9 %collective-permute-start.48 = (bf16[1,128,1024]{2,1,0:T(8,128)(2,1)}, bf16[1,128,1024]{2,1,0:T(8,128)(2,1)S(1)}, u32[]{:S(2)}, u32[]{:S(2)}) collective-permute-start(bf16[1,128,1024]{2,1,0:T(8,128)(2,1)} %get-tuple-element.288), channel_id=1, source_target_pairs={{0,16},{4,20},{8,24},{12,28},{16,0},{20,4},{24,8},{28,12},{1,17},{... | collective-permute-start | bytes 786440 | tf_op jit(solution)/shard_map/ppermute | solution.py:948
  437.2 30.7 %collective-permute-start.49 = (bf16[1,128,1024]{2,1,0:T(8,128)(2,1)}, bf16[1,128,1024]{2,1,0:T(8,128)(2,1)}, u32[]{:S(2)}, u32[]{:S(2)}) collective-permute-start(bf16[1,128,1024]{2,1,0:T(8,128)(2,1)} %get-tuple-element.290), channel_id=1, source_target_pairs={{0,8},{4,12},{8,0},{12,4},{16,24},{20,28},{24,16},{28,20},{1,9},{5... | collective-permute-start | bytes 786440 | tf_op jit(solution)/shard_map/ppermute | solution.py:948
  470.5 43.6 %collective-permute-start.51 = (bf16[256,2048]{1,0:T(8,128)(2,1)S(1)}, bf16[256,2048]{1,0:T(8,128)(2,1)S(1)}, u32[]{:S(2)}, u32[]{:S(2)}) collective-permute-start(bf16[256,2048]{1,0:T(8,128)(2,1)S(1)} %bitcast.65), channel_id=1, source_target_pairs={{1,0},{2,3},{5,4},{6,7},{9,8},{10,11},{13,12},{14,15},{17,16},{18,... | collective-permute-start | bytes 3145736 | tf_op jit(solution)/shard_map/ppermute | solution.py:1057
  471.8 27.7 %collective-permute-start.52 = (bf16[128,1024]{1,0:T(8,128)(2,1)S(1)}, bf16[128,1024]{1,0:T(8,128)(2,1)S(1)}, u32[]{:S(2)}, u32[]{:S(2)}) collective-permute-start(bf16[128,1024]{1,0:T(8,128)(2,1)S(1)} %get-tuple-element.297), channel_id=1, source_target_pairs={{0,1},{1,0},{2,3},{3,2},{4,5},{5,4},{6,7},{7,6},{8,9},{9,8},{10,11... | collective-permute-start | bytes 786440 | tf_op jit(solution)/shard_map/ppermute | solution.py:948
  475.8 24.0 %collective-permute-start.40 = (f32[18,128]{1,0:T(8,128)S(1)}, f32[18,128]{1,0:T(8,128)S(1)}, u32[]{:S(2)}, u32[]{:S(2)}) collective-permute-start(f32[18,128]{1,0:T(8,128)S(1)} %bitcast_add_fusion), channel_id=1, source_target_pairs={{0,8},{4,12},{8,0},{12,4},{16,24},{20,28},{24,16},{28,20},{1,9},{5... | collective-permute-start | bytes 27656 | tf_op jit(solution)/shard_map/ppermute | solution.py:948
  (87 other events, 933.8 us)
Sparse Core Ops, SparseCore 0:
  14.8 145.1 all-gather.2
  198.2 100.8 reduce-scatter.1

commit v3 on v2

--- a/solution.py
+++ b/solution.py
@@ -339,17 +339,18 @@
     return high, (v - high.astype(F32)).astype(BF16)
 
 
-def feed_forward(mixed, tokens, grad, gain, stack):
+def middle_block(mixed, lse, factors, tokens, grad, gain, stack):
     rows, inner = mixed.shape
-    count, _, width = stack.shape
+    count, height, width = stack.shape
     unit = width // count
     hidden = 3 * width
     block = 256
+    per_row = block // unit if unit < block else 1
 
     def body(
-        mixed_hbm, tok_hbm, dy_hbm, gain_ref, stack_ref,
-        out_ref, low_ref, h_ref, both_ref, mid_ref,
-        w, acc, mixed_ref, tok_ref, dy_ref, sems,
+        mixed_hbm, lse_ref, fac_ref, tok_hbm, dy_hbm, gain_ref, stack_ref,
+        out_ref, low_ref, h_ref, both_ref, gm_ref, gb_ref, gg_ref, dm_ref, parcel_ref,
+        w, mid, acc, deltas, mixed_ref, tok_ref, dy_ref, sems,
     ):
         def move(first, many, sem):
             here = (slice(None), pl.ds(first * unit, many * unit))
@@ -359,11 +360,11 @@
             pltpu.make_async_copy(a, b, sems.at[8 + i])
             for i, (a, b) in enumerate(((mixed_hbm, mixed_ref), (tok_hbm, tok_ref), (dy_hbm, dy_ref)))
         ]
+        loads[0].start()
         out_copy = move(9, 2, 0)
         gate_copies = [move(3 + i, 1, 1 + i) for i in range(3)]
         up_copies = [move(6 + i, 1, 4 + i) for i in range(3)]
         down_copy = move(0, 3, 7)
-        loads[0].start()
         out_copy.start()
         loads[1].start()
         loads[2].start()
@@ -378,16 +379,17 @@
         for j in range(width // block):
             cols = slice(j * block, (j + 1) * block)
             part = w[:, 9 * unit : 11 * unit, cols].reshape(inner, block)
-            mid_ref[:, cols] = tok_ref[:, cols].astype(F32) + mm(mixed_ref[...], part)
-        x = mid_ref[...]
+            mid[:, cols] = tok_ref[:, cols].astype(F32) + mm(mixed_ref[...], part)
+        x = mid[...]
         low_ref[...] = (x * factor_of(x) * gain_ref[...]).astype(BF16)
 
         for i in range(3):
             gate_copies[i].wait()
             up_copies[i].wait()
-            for j in range(width // block):
-                cols = slice(j * block, (j + 1) * block)
-                to = slice(i * width + j * block, i * width + (j + 1) * block)
+
+            def forward(j, _):
+                cols = pl.ds(pl.multiple_of(j * block, block), block)
+                to = pl.ds(pl.multiple_of(i * width + j * block, block), block)
                 g = mm(low_ref[...], w[:, (3 + i) * unit : (4 + i) * unit, cols].reshape(width, block))
                 u = mm(low_ref[...], w[:, (6 + i) * unit : (7 + i) * unit, cols].reshape(width, block))
                 s = 1.0 / (1.0 + jnp.exp(-g))
@@ -395,120 +397,89 @@
                 h_ref[:, to] = (act * u).astype(BF16)
                 both_ref[0, :, to] = (u * (s + act * (1.0 - s))).astype(BF16)
                 both_ref[1, :, to] = act.astype(BF16)
+                return 0
+
+            lax.fori_loop(0, width // block, forward, 0, unroll=True)
 
         down_copy.wait()
+        acc[...] = mid[...]
         wide = 384
         owners = wide // (3 * unit)
-        acc[...] = mid_ref[...]
-        for j in range(hidden // wide):
-            cols = slice(j * wide, (j + 1) * wide)
-            part = w[j * owners : (j + 1) * owners, 0 : 3 * unit, :].reshape(wide, width)
+
+        def down(j, _):
+            cols = pl.ds(pl.multiple_of(j * wide, wide), wide)
+            part = w[pl.ds(j * owners, owners), 0 : 3 * unit, :].reshape(wide, width)
             dh = mm_nt(dy_ref[...], part)
             both_ref[0, :, cols] = (both_ref[0, :, cols].astype(F32) * dh).astype(BF16)
             both_ref[1, :, cols] = (both_ref[1, :, cols].astype(F32) * dh).astype(BF16)
             acc[...] += mm(h_ref[:, cols], part)
+            return 0
+
+        lax.fori_loop(0, hidden // wide, down, 0, unroll=True)
         out_ref[...] = acc[...].astype(BF16)
 
+        owners_in = block // unit
+        for b in range(width // block):
+            at = slice(b * owners_in, (b + 1) * owners_in)
+            total = None
+            for i in range(3):
+                cols = slice(i * width, (i + 1) * width)
+                for side in range(2):
+                    first = (3 + 3 * side + i) * unit
+                    part = w[at, first : first + unit, :].reshape(block, width)
+                    term = mm_nt(both_ref[side, :, cols], part)
+                    total = term if total is None else total + term
+            acc[:, b * block : (b + 1) * block] = total
+
+        back, terms = norm_back(mid[...], gain_ref[...], acc[...])
+        grad_mid = dy_ref[...].astype(F32) + back
+        gm_ref[...] = grad_mid
+        gb_ref[...] = grad_mid.astype(BF16)
+        gg_ref[...] = jnp.sum(terms, axis=0, keepdims=True)
+
+        owners_out = block // (2 * unit)
+
+        def mixed_back(j, _):
+            cols = pl.ds(pl.multiple_of(j * block, block), block)
+            part = w[pl.ds(j * owners_out, owners_out), 9 * unit : 11 * unit, :].reshape(block, width)
+            dm = mm_nt(gb_ref[...], part).astype(BF16)
+            dm_ref[:, cols] = dm
+            terms = (dm.astype(F32) * mixed_ref[:, cols].astype(F32)).T
+            for k in range(block // HEAD_DIM):
+                delta = jnp.sum(terms[k * HEAD_DIM : (k + 1) * HEAD_DIM], axis=0, keepdims=True)
+                deltas[pl.ds(j * (block // HEAD_DIM) + k, 1), :] = delta
+            return 0
+
+        lax.fori_loop(0, inner // block, mixed_back, 0, unroll=True)
+        parcel_ref[:rows, :] = gb_ref[...]
+        parcel_ref[rows:, :] = jnp.zeros((3 * HEADS, width), BF16)
+        extras = (lse_ref[:, 0, :], deltas[...], fac_ref[:, 0, :])
+        for which, values in enumerate(extras):
+            at = rows + which * HEADS
+            for side, piece in enumerate(high_low(values)):
+                parcel_ref[at : at + HEADS, side * rows : (side + 1) * rows] = piece
+
     full = (rows, width)
     return call(
-        "feed_forward", body, [mixed, tokens, grad, gain, stack],
-        [IN_HBM, IN_HBM, IN_HBM, whole((1, width)), IN_HBM],
-        [whole(full), IN_VMEM, IN_VMEM, IN_VMEM, IN_VMEM],
+        "middle_block", body, [mixed, lse, factors, tokens, grad, gain, stack],
+        [IN_HBM, whole(lse.shape), whole(factors.shape), IN_HBM, IN_HBM, whole((1, width)), IN_HBM],
+        [whole(full), IN_VMEM, IN_VMEM, IN_VMEM, whole(full), IN_VMEM, IN_VMEM, whole((rows, inner)), IN_VMEM],
         [
             shape(full, BF16), shape(full, BF16), shape((rows, hidden), BF16),
-            shape((2, rows, hidden), BF16), shape(full, F32),
+            shape((2, rows, hidden), BF16), shape(full, F32), shape(full, BF16),
+            shape((1, width), F32), shape((rows, inner), BF16), shape((rows + 3 * HEADS, width), BF16),
         ],
         scratch=[
-            pltpu.VMEM(stack.shape, BF16),
+            pltpu.VMEM((count, height, width), BF16),
             pltpu.VMEM(full, F32),
+            pltpu.VMEM(full, F32),
+            pltpu.VMEM((HEADS, rows), F32),
             pltpu.VMEM((rows, inner), BF16),
             pltpu.VMEM(full, BF16),
             pltpu.VMEM(full, BF16),
             pltpu.SemaphoreType.DMA((11,)),
         ],
-        vmem=40,
-    )
-
-
-def branch_back(both, middle, grad, gain, mixed, lse, factors, stack):
-    _, rows, hidden = both.shape
-    count, _, width = stack.shape
-    unit = width // count
-    inner = mixed.shape[1]
-    block = 256
-
-    def body(
-        both_ref, mid_ref, dy_ref, gain_ref, mixed_ref, lse_ref, fac_ref, stack_ref,
-        gm_ref, gb_ref, gg_ref, dm_ref, parcel_ref,
-        w, acc, deltas, sems,
-    ):
-        owners_in = block // unit
-        steps = width // block
-        copies_in = []
-        for b in range(steps):
-            here = (pl.ds(b * owners_in, owners_in), pl.ds(3 * unit, 6 * unit))
-            to = (pl.ds(b * owners_in, owners_in), pl.ds(0, 6 * unit))
-            copies_in.append(pltpu.make_async_copy(stack_ref.at[here], w.at[to], sems.at[b]))
-        here, to = (slice(None), pl.ds(9 * unit, 2 * unit)), (slice(None), pl.ds(6 * unit, 2 * unit))
-        out_copy = pltpu.make_async_copy(stack_ref.at[here], w.at[to], sems.at[steps])
-        for copy in copies_in + [out_copy]:
-            copy.start()
-
-        for b in range(steps):
-            copies_in[b].wait()
-            at = slice(b * owners_in, (b + 1) * owners_in)
-            total = None
-            for i in range(6):
-                part = w[at, i * unit : (i + 1) * unit, :].reshape(block, width)
-                term = mm_nt(both_ref[i // 3, :, (i % 3) * width : (i % 3 + 1) * width], part)
-                total = term if total is None else total + term
-            acc[:, b * block : (b + 1) * block] = total
-
-        back, terms = norm_back(mid_ref[...], gain_ref[...], acc[...])
-        grad_mid = dy_ref[...].astype(F32) + back
-        gm_ref[...] = grad_mid
-        gb_ref[...] = grad_mid.astype(BF16)
-        gg_ref[...] = jnp.sum(terms, axis=0, keepdims=True)
-
-        out_copy.wait()
-        owners_out = block // (2 * unit)
-        for j in range(inner // block):
-            cols = slice(j * block, (j + 1) * block)
-            at = slice(j * owners_out, (j + 1) * owners_out)
-            dm = mm_nt(gb_ref[...], w[at, 6 * unit : 8 * unit, :].reshape(block, width)).astype(BF16)
-            dm_ref[:, cols] = dm
-            terms = (dm.astype(F32) * mixed_ref[:, cols].astype(F32)).T
-            for k in range(block // HEAD_DIM):
-                head = j * (block // HEAD_DIM) + k
-                deltas[head : head + 1, :] = jnp.sum(
-                    terms[k * HEAD_DIM : (k + 1) * HEAD_DIM], axis=0, keepdims=True
-                )
-        parcel_ref[:rows, :] = gb_ref[...]
-        parcel_ref[rows:, :] = jnp.zeros((3 * HEADS, width), BF16)
-        for which, values in enumerate((lse_ref[:, 0, :], deltas[...], fac_ref[:, 0, :])):
-            at = rows + which * HEADS
-            for side, piece in enumerate(high_low(values)):
-                parcel_ref[at : at + HEADS, side * rows : (side + 1) * rows] = piece
-
-    full = (rows, width)
-    return call(
-        "branch_back", body, [both, middle, grad, gain, mixed, lse, factors, stack],
-        [
-            IN_VMEM, IN_VMEM, whole(full), whole((1, width)), whole((rows, inner)), whole(lse.shape),
-            whole(factors.shape), IN_HBM,
-        ],
-        [whole(full), IN_VMEM, IN_VMEM, whole((rows, inner)), IN_VMEM],
-        [
-            shape(full, F32), shape(full, BF16), shape((1, width), F32), shape((rows, inner), BF16),
-            shape((rows + 3 * HEADS, width), BF16),
-        ],
-        scratch=[
-            pltpu.VMEM((count, 8 * unit, width), BF16),
-            pltpu.VMEM(full, F32),
-            pltpu.VMEM((HEADS, rows), F32),
-            pltpu.SemaphoreType.DMA((width // block + 1,)),
-        ],
-        vmem=32,
+        vmem=44,
     )
 
 
@@ -722,7 +693,7 @@
             pl.BlockSpec((owners, unit, width), lambda *_: (0, 9, 0)),
             pl.BlockSpec((owners, unit, width), lambda *_: (0, 10, 0)),
         ]
-        + [IN_VMEM] * len(parcels),
+        + [whole(parcel.shape) for parcel in parcels],
         [
             pl.BlockSpec((2, 1, half, inner), lambda k, at, me: (0, at[k], 0, 0)),
             pl.BlockSpec((2, 1, numbers, half), lambda k, at, me: (0, at[k], 0, 0)),
@@ -1099,6 +1070,7 @@
             *copies(
                 "pass_on", came, lambda _, ins, outs: list(zip(ins, outs)),
                 [shape(c.shape, c.dtype) for c in came],
+                in_specs=[whole(c.shape) for c in came], out_specs=[whole(c.shape) for c in came],
             )
         )
 
@@ -1107,11 +1079,30 @@
             self.step()
 
 
-def sum_everywhere(x):
-    for axis in ("dp", "ctx"):
-        for bit in bits_of(lax.axis_size(axis)):
-            x = x + swap(x, axis, bit)
-    return x
+class Everywhere:
+    def __init__(self, x):
+        self.left = [("dp", bit) for bit in bits_of(lax.axis_size("dp"))]
+        self.left += [("ctx", bit) for bit in bits_of(lax.axis_size("ctx"))]
+        self.total = x
+        self.came = swap(x, *self.left.pop(0))
+
+    def step(self):
+        def body(a_ref, b_ref, out_ref):
+            out_ref[...] = a_ref[...] + b_ref[...]
+
+        self.total = call(
+            "add_small", body, [self.total, self.came], [IN_VMEM] * 2, [IN_VMEM],
+            [shape(self.total.shape, F32)],
+        )[0]
+        if self.left:
+            self.came = swap(self.total, *self.left.pop(0))
+            return True
+        return False
+
+    def finish(self):
+        while self.step():
+            pass
+        return self.total
 
 
 def on_device(
@@ -1216,9 +1207,9 @@
     mixed, lse = attend(
         queries, keys, values, query_open[:, None], query_stream[:, None], key_stream[None, :]
     )
-    output, normed_mid, hidden, d_both, middle = feed_forward(
-        mixed, own_tokens, grad_out, gain_mlp, stack
-    )
+    (
+        output, normed_mid, hidden, d_both, grad_middle, grad_branch, mlp_part, grad_mixed, parcel,
+    ) = middle_block(mixed, lse, factors, own_tokens, grad_out, gain_mlp, stack)
 
     order = [2 * k for k in range(dp_size // 2)] + [2 * k + 1 for k in range(dp_size // 2)]
     owners = (dp_at ^ jnp.array(order, jnp.int32)).astype(jnp.int32)
@@ -1240,37 +1231,35 @@
         return Sum(pair[:1], pair[1:], [(0, half), (half, half)], odd), half
 
     half_heads = KV_HEADS // 2
-    down, down_half = halves_of(weight_grad(hidden, grad_out, owners))
+    parcels = Relay(parcel)
     wide_grad = weight_grad(normed_mid, d_both, block=1024)[0]
     wide_grad = lax.psum_scatter(wide_grad, "dp", scatter_dimension=0, tiled=True)
-    down.over_dp()
-    grad_middle, grad_branch, mlp_part, grad_mixed, parcel = branch_back(
-        d_both, middle, grad_out, gain_mlp, mixed, lse, factors, stack
-    )
-    parcels = Relay(parcel)
-    for _ in range(later_dp):
-        down.over_dp()
-    out_kept, out_sent = weight_grad(mixed, grad_branch, owners, beside=True)
     query_args = (
         queries, grad_mixed, mixed, keys, values, lse, query_open[:, None], query_stream[:, None],
         key_stream[None, :], query_raw, gain_query, cos_own, sin_own,
     )
     d_query, query_part = query_back(*query_args, 0, half_heads)
+    out_kept, out_sent = weight_grad(mixed, grad_branch, owners, beside=True)
+
     parcels.step()
-    down = Line(down.joined())
+
     d_query, query_more = query_back(*query_args, half_heads, half_heads, (d_query,))
+
     parcels.finish()
-    down.step()
     query_kept, query_sent = weight_grad(normed, d_query, owners)
     outer = Sum([out_kept, query_kept], [out_sent, query_sent], [(0, unit), (0, unit)], odd)
+
+    every_query = all_queries(normed_pack, attn_w, gain_query, cos_pack, sin_pack)
+
+    touch([parcels.from_left[-1], parcels.from_right[-1]])
+    down_grad = weight_grad(hidden, grad_out, block=256)[0]
+    down_grad = lax.psum_scatter(down_grad, "dp", scatter_dimension=0, tiled=True)
+    outer.over_dp()
     wide_grad = copies(
         "take", [wide_grad], lambda _, ins, outs: [(ins[0], outs[0])], [shape(wide_grad.shape, BF16)]
     )[0]
     wide = Line(wide_grad)
-    every_query = all_queries(normed_pack, attn_w, gain_query, cos_pack, sin_pack)
-    touch([parcels.from_left[-1], parcels.from_right[-1]])
-    down.finish()
-    outer.over_dp()
+
     parcels = [parcel] + parcels.from_left + parcels.from_right
     grad_mixed_pack, far = all_grad_mixed(
         grad_mixed, parcels, stack, places, ctx_at.astype(jnp.int32)[None], rows
@@ -1282,30 +1271,54 @@
         key_open[None, :], key_stream[None, :], query_stream[:, None],
         key_raw, gain_key, cos_own, sin_own, ctx_at.astype(jnp.int32)[None], ctx_size,
     )
-    wide.step()
     d_pair, key_part = key_back(*key_args, 0, half_heads)
+
     for _ in range(later_dp):
         outer.over_dp()
-    down_grad = down.place([(2 * down_half, width)], [(everything, 0, everything)])[0]
+    wide.step()
+
     d_pair, key_more = key_back(*key_args, half_heads, half_heads, (d_pair,))
     query_part, key_part = query_part + query_more, key_part + key_more
+
     outer = Line(outer.joined())
     key_kept, key_sent, value_kept, value_sent = weight_grad(normed, d_pair, owners, apart=True)
     pair = Sum([key_kept, value_kept], [key_sent, value_sent], [(0, unit), (0, unit)], odd)
+
+    d_normed = normed_back(d_query, d_pair, attn_w)
+    input_grad, attn_part = input_back(d_normed, own_tokens, gain_attn, grad_middle)
+
     wide.finish()
-    d_normed = normed_back(d_query, d_pair, attn_w)
     pair.over_dp()
-    input_grad, attn_part = input_back(d_normed, own_tokens, gain_attn, grad_middle)
+    down_grad = copies(
+        "take", [down_grad], lambda _, ins, outs: [(ins[0], outs[0])], [shape(down_grad.shape, BF16)]
+    )[0]
+    down = Line(down_grad)
+    small = Everywhere(
+        jnp.concatenate([attn_part, mlp_part, query_part, key_part], axis=1).reshape(-1, HEAD_DIM)
+    )
+
     for _ in range(later_dp):
         pair.over_dp()
+    small.step()
     outer.step()
+
+    pair.to_ctx()
+    small.step()
+    down.step()
     gate_grad, up_grad = wide.place(
         [(unit, 3 * width)] * 2,
         [((everything, slice(k * 3 * width, (k + 1) * 3 * width)), k, everything) for k in range(2)],
     )
-    pair.to_ctx()
+
+    pair.over_ctx()
+    small.step()
     outer.finish()
-    pair.over_ctx()
+
+    for _ in range(later_ctx):
+        pair.over_ctx()
+        small.step()
+    down.finish()
+    small = small.finish().reshape(-1)
     near, far_half = slice(0, width), slice(width, 2 * width)
     first, second = slice(0, unit), slice(unit, 2 * unit)
     w_out_grad, query_grad = outer.place(
@@ -1316,14 +1329,11 @@
             ((second, everything), 1, everything),
         ],
     )
-    for _ in range(later_ctx):
-        pair.over_ctx()
+    down_grad = down.place([down_grad.shape], [(everything, 0, everything)])[0]
     key_grad, value_grad = place(
         [pair.total], odd, [(unit, width)] * 2, [(0, k, everything, k, everything) for k in range(2)]
     )
 
-    parts = [attn_part, mlp_part, query_part, key_part]
-    small = sum_everywhere(jnp.concatenate(parts, axis=1).reshape(-1, HEAD_DIM)).reshape(-1)
     attn_gain_grad = lax.dynamic_slice(small, (dp_at * unit,), (unit,))
     mlp_gain_grad = lax.dynamic_slice(small, (width + dp_at * unit,), (unit,))
     query_gain_grad = small[2 * width : 2 * width + HEAD_DIM]

time: 536 us -> 526 us (0.981)
  starting transfers between devices: 91 us -> 73.7 us
  local copies, waits for them, and re-layouts: 31.1 us -> 45.2 us
  Pallas kernels: 242 us -> 236 us
    ppermute x9, starting transfers between devices: 38.2 us -> 20.4 us  [send(): self.came = lax.ppermute(self.total, 'ctx', pairs)]
    ppermute x9, waiting for transfers between devices: 26.6 us -> 9.64 us  [send(): self.came = lax.ppermute(self.total, 'ctx', pairs)]
    unnamed x124 -> x200, local copies, waits for them, and re-layouts: 22 us -> 38.8 us
    ppermute x6, waiting for transfers between devices: 13.3 us -> 21.7 us  [send(): lax.ppermute(left, 'ctx', [(i + 1, i) for i in range(self.size - 1 - step)])]
    ppermute x34 -> x29, waiting for transfers between devices: 94.8 us -> 100 us  [swap(): return lax.ppermute(x, axis, [(i, i ^ bit) for i in range(size)])]
    pallas_call x51 -> x53, Pallas kernels: 242 us -> 236 us  [call(): pl.pallas_call(without, grid_spec=pltpu.PrefetchScalarGridSpec(num_scalar...]
    ppermute x34 -> x29, starting transfers between devices: 30 us -> 31.2 us  [swap(): return lax.ppermute(x, axis, [(i, i ^ bit) for i in range(size)])]
  transfers between devices with their start and end apart: 57 -> 53, of which waited for: 19 -> 26; matrix products, arithmetic and copies ran while one was open for 3% -> 3% of each run, Pallas kernels for 38% -> 37%
where the time goes in v3:
time: 526 us; the launch traced here: 521 us
  Pallas kernels  236 us (45%)
  waiting for transfers between devices  139 us (26%)
  starting transfers between devices  73.7 us (14%)
  local copies, waits for them, and re-layouts  45.2 us (9%)
  between operations  15 us (3%)
  other arithmetic  11.3 us (2%)
    pallas_call x53, Pallas kernels, call(): pl.pallas_call(without, grid_spec=pltpu.PrefetchScalarGridSpec(num_scalar...  236 us
    ppermute x29, waiting for transfers between devices, swap(): return lax.ppermute(x, axis, [(i, i ^ bit) for i in range(size)])  100 us
    unnamed x200, local copies, waits for them, and re-layouts  38.8 us
    ppermute x29, starting transfers between devices, swap(): return lax.ppermute(x, axis, [(i, i ^ bit) for i in range(size)])  31.2 us
    ppermute x6, waiting for transfers between devices, send(): lax.ppermute(left, 'ctx', [(i + 1, i) for i in range(self.size - 1 - step)])  21.7 us
    ppermute x9, starting transfers between devices, send(): self.came = lax.ppermute(self.total, 'ctx', pairs)  20.4 us
    ppermute x6, starting transfers between devices, send(): lax.ppermute(right, 'ctx', [(i, i + 1) for i in range(step, self.size - 1)])  14.1 us
  transfers between devices with their start and end apart: 53, of which 26 were waited for; matrix products, arithmetic and copies ran while one was open for 3% of the time, Pallas kernels for 37%

profile of v3, /device:TPU:0, one launch (start us, length us, event | category | flops | bytes accessed | tf_op | source)
XLA Modules:
  0.0 520.7 jit_solution(12402955543779551767)
XLA Ops:
  17.1 5.6 %collective-permute-start.9 = (bf16[384,1024]{1,0:T(8,128)(2,1)S(1)}, bf16[384,1024]{1,0:T(8,128)(2,1)S(1)}, u32[]{:S(2)}, u32[]{:S(2)}) collective-permute-start(bf16[384,1024]{1,0:T(8,128)(2,1)S(1)} %bitcast.52), channel_id=1, source_target_pairs={{0,1},{1,2},{2,3},{4,5},{5,6},{6,7},{8,9},{9,10},{10,11},{12,13},{... | collective-permute-start | bytes 2359304 | tf_op jit(solution)/shard_map/ppermute | solution.py:1062
  27.0 4.4 fusion
  31.5 6.8 %collective-permute-done.10.refs_1_.refs_7_ = bf16[384,1024]{1,0:T(8,128)(2,1)S(1)} collective-permute-done((bf16[384,1024]{1,0:T(8,128)(2,1)S(1)}, bf16[384,1024]{1,0:T(8,128)(2,1)S(1)}, u32[]{:S(2)}, u32[]{:S(2)}) %collective-permute-start.10) | collective-permute-done | bytes 786464 | tf_op jit(solution)/shard_map/ppermute | solution.py:1064
  45.0 26.6 %collective-permute-done.1.refs_1_.refs_3_ = bf16[128,4224]{1,0:T(8,128)(2,1)} collective-permute-done((bf16[128,4224]{1,0:T(8,128)(2,1)}, bf16[128,4224]{1,0:T(8,128)(2,1)}, u32[]{:S(2)}, u32[]{:S(2)}) %collective-permute-start.1) | collective-permute-done | bytes 1081376 | tf_op jit(solution)/shard_map/ppermute | solution.py:919
  78.2 12.4 %collective-permute-done.5.refs_7_ = bf16[128,2048]{1,0:T(8,128)(2,1)} collective-permute-done((bf16[128,2048]{1,0:T(8,128)(2,1)S(1)}, bf16[128,2048]{1,0:T(8,128)(2,1)}, u32[]{:S(2)}, u32[]{:S(2)}) %collective-permute-start.5) | collective-permute-done | bytes 524320 | tf_op jit(solution)/shard_map/ppermute | solution.py:919
  102.9 8.1 %assemble_weights.1 = (bf16[1024,4224]{1,0:T(8,128)(2,1)}, bf16[1024,128]{1,0:T(8,128)(2,1)S(1)}, f32[8,128]{1,0:T(8,128)S(1)}) custom-call(s32[8]{0:T(128)S(1)} %iota_xor_fusion.refs_0_, bf16[128,4224]{1,0:T(8,128)(2,1)} %get-tuple-element.159.refs_1_, bf16[128,4224]{1,0:T(8,128)(2,1)} %collective-permute-done.refs_2_, ...), custom_call_target="tpu_custom_call" | custom-call | tf_op jit(solution)/shard_map/assemble_weights/pallas_call | solution.py:64
  112.2 8.9 %project_queries.1 = (bf16[384,2048]{1,0:T(8,128)(2,1)}, bf16[384,2048]{1,0:T(8,128)(2,1)}, f32[16,8,384]{2,1,0:T(8,128)S(1)}, f32[8,128]{1,0:T(8,128)S(1)}) custom-call(bf16[384,1024]{1,0:T(8,128)(2,1)S(1)} %get-tuple-element.168.refs_0_.refs_1_, bf16[1024,4224]{1,0:T(8,128)(2,1)} %get-tuple-element.169.refs_1_.refs_2_.refs_3_.refs_4_, ...), custom_call_target="tpu_custom_call" | custom-call | tf_op jit(solution)/shard_map/project_queries/pallas_call | solution.py:64
  122.0 4.8 norm_pack.1
  128.9 12.8 %project_keys_values.1 = (bf16[1536,1024]{1,0:T(8,128)(2,1)}, bf16[1536,1024]{1,0:T(8,128)(2,1)}, bf16[1536,1024]{1,0:T(8,128)(2,1)}, f32[8,128]{1,0:T(8,128)S(1)}) custom-call(bf16[1536,1024]{1,0:T(8,128)(2,1)S(1)} %bitcast.57, bf16[1024,4224]{1,0:T(8,128)(2,1)} %get-tuple-element.169.refs_1_.refs_2_.refs_3_.refs_4_, ...), custom_call_target="tpu_custom_call" | custom-call | tf_op jit(solution)/shard_map/project_keys_values/pallas_call | solution.py:64
  141.7 13.9 %attend.1 = (bf16[384,2048]{1,0:T(8,128)(2,1)}, f32[16,8,384]{2,1,0:T(8,128)S(1)}, f32[8,128]{1,0:T(8,128)S(1)}) custom-call(bf16[384,2048]{1,0:T(8,128)(2,1)} %get-tuple-element.171.refs_0_, bf16[1536,1024]{1,0:T(8,128)(2,1)} %get-tuple-element.177.refs_1_.refs_3_, bf16[1536,1024]{1,0:T(8,128)(2,1)} %get-tuple-element.178.refs_2_.refs_4_, ...), custom_call_target="tpu_custom_call" | custom-call | tf_op jit(solution)/shard_map/attend/pallas_call | solution.py:64
  155.6 5.1 all-gather.3.cloned.1.call-done
  162.1 28.2 %middle_block.1 = (bf16[384,1024]{1,0:T(8,128)(2,1)}, bf16[384,1024]{1,0:T(8,128)(2,1)S(1)}, bf16[384,3072]{1,0:T(8,128)(2,1)S(1)}, bf16[2,384,3072]{2,1,0:T(8,1...) custom-call(bf16[384,2048]{1,0:T(8,128)(2,1)S(1)} %copy-done, ...), custom_call_target="tpu_custom_call" | custom-call | tf_op jit(solution)/shard_map/middle_block/pallas_call | solution.py:64
  194.2 9.4 %weight_grad.5 = (bf16[1024,6144]{1,0:T(8,128)(2,1)}, f32[8,128]{1,0:T(8,128)S(1)}) custom-call(bf16[384,1024]{1,0:T(8,128)(2,1)S(1)} %get-tuple-element.188.refs_0_, bf16[2,384,3072]{2,1,0:T(8,128)(2,1)S(1)} %copy-done.18, f32[8,128]{1,0:T(8,128)S(1)} %get-tuple-element.190.refs_2_), custom_call_target="tpu_custom_call" | custom-call | tf_op jit(solution)/shard_map/weight_grad/pallas_call | solution.py:64
  206.1 4.6 collective-permute-start.15
  210.8 13.6 %query_back.2 = (bf16[384,2048]{1,0:T(8,128)(2,1)}, f32[1,128]{1,0:T(1,128)S(1)}, f32[8,128]{1,0:T(8,128)S(1)}) custom-call(bf16[384,2048]{1,0:T(8,128)(2,1)} %get-tuple-element.171.refs_0_, bf16[384,2048]{1,0:T(8,128)(2,1)} %get-tuple-element.186.refs_1_.refs_2_, bf16[384,2048]{1,0:T(8,128)(2,1)} %get-tuple-element.180.refs_0_.refs_2_.refs_1_, ...), custom_call_target="tpu_custom_call" | custom-call | tf_op jit(solution)/shard_map/query_back/pallas_call | solution.py:64
  235.5 12.9 %query_back.3 = (bf16[384,2048]{1,0:T(8,128)(2,1)}, f32[1,128]{1,0:T(1,128)S(1)}, f32[8,128]{1,0:T(8,128)S(1)}) custom-call(bf16[384,2048]{1,0:T(8,128)(2,1)} %get-tuple-element.171.refs_0_, bf16[384,2048]{1,0:T(8,128)(2,1)} %get-tuple-element.186.refs_1_.refs_2_, ...), custom_call_target="tpu_custom_call", output_to_operand_aliasing={{0}: (13, {})} | custom-call | tf_op jit(solution)/shard_map/query_back/pallas_call | solution.py:64
  249.1 11.0 %collective-permute-done.18.refs_1_.refs_10_ = bf16[432,1024]{1,0:T(8,128)(2,1)S(1)} collective-permute-done((bf16[432,1024]{1,0:T(8,128)(2,1)}, bf16[432,1024]{1,0:T(8,128)(2,1)S(1)}, u32[]{:S(2)}, u32[]{:S(2)}) %collective-permute-start.18) | collective-permute-done | bytes 884768 | tf_op jit(solution)/shard_map/ppermute | solution.py:1064
  269.1 14.2 %all_queries.1 = (bf16[1536,2048]{1,0:T(8,128)(2,1)}, f32[8,128]{1,0:T(8,128)S(1)}) custom-call(bf16[1536,1024]{1,0:T(8,128)(2,1)S(1)} %bitcast.58, bf16[1024,4224]{1,0:T(8,128)(2,1)} %get-tuple-element.169.refs_1_.refs_2_.refs_3_.refs_4_, f32[1,128]{1,0:T(1,128)S(1)} %copy-done.64, f32[1536,128]{1,0:T(8,128)S(1)} %copy-done.15, f32[1536,128]{1,0:T(8,128)S(1)} %copy-done.17, ...), custom_call_target="tpu_custom_call" | custom-call | tf_op jit(solution)/shard_map/all_queries/pallas_call | solution.py:64
  286.3 6.1 %weight_grad.8 = (bf16[3072,1024]{1,0:T(8,128)(2,1)}, f32[8,128]{1,0:T(8,128)S(1)}) custom-call(bf16[384,3072]{1,0:T(8,128)(2,1)S(1)} %copy-done.32, bf16[384,1024]{1,0:T(8,128)(2,1)S(1)} %bitcast.60, f32[8,128]{1,0:T(8,128)S(1)} %touch.3.refs_2_), custom_call_target="tpu_custom_call" | custom-call | tf_op jit(solution)/shard_map/weight_grad/pallas_call | solution.py:64
  311.0 4.5 collective-permute-start.23
  318.0 11.9 %all_grad_mixed.1 = (bf16[2,4,192,2048]{3,2,1,0:T(8,128)(2,1)}, f32[2,4,48,192]{3,2,1,0:T(8,128)S(1)}, f32[8,128]{1,0:T(8,128)S(1)}) custom-call(s32[4]{0:T(128)S(1)} %copy-done.74, s32[1]{0:T(128)} %bitcast.6.refs_1_.refs_0_, bf16[384,2048]{1,0:T(8,128)(2,1)S(1)} %copy-done.2, bf16[8,1408,1024]{2,1,0:T(8,128)(2,1)} %bitcast.79, ...), custom_call_target="tpu_custom_call" | custom-call | tf_op jit(solution)/shard_map/all_grad_mixed/pallas_call | solution.py:64
  332.9 12.6 %key_back.2 = (bf16[2,384,1024]{2,1,0:T(8,128)(2,1)}, f32[1,128]{1,0:T(1,128)S(1)}, f32[8,128]{1,0:T(8,128)S(1)}) custom-call(s32[1]{0:T(128)} %bitcast.6.refs_1_.refs_0_, bf16[1536,2048]{1,0:T(8,128)(2,1)} %get-tuple-element.204.refs_1_, bf16[1536,2048]{1,0:T(8,128)(2,1)} %bitcast.85, bf16[2,4,192,1024]{3,2,1,0:T(8,128)(2,1)} %bitcast.81, ...), custom_call_target="tpu_custom_call" | custom-call | tf_op jit(solution)/shard_map/key_back/pallas_call | solution.py:64
  345.5 11.3 %collective-permute-done.24.refs_1_ = bf16[2,128,2048]{2,1,0:T(8,128)(2,1)} collective-permute-done((bf16[2,128,2048]{2,1,0:T(8,128)(2,1)}, bf16[2,128,2048]{2,1,0:T(8,128)(2,1)}, u32[]{:S(2)}, u32[]{:S(2)}) %collective-permute-start.24) | collective-permute-done | bytes 1048608 | tf_op jit(solution)/shard_map/ppermute | solution.py:919
  365.3 12.4 %key_back.3 = (bf16[2,384,1024]{2,1,0:T(8,128)(2,1)}, f32[1,128]{1,0:T(1,128)S(1)}, f32[8,128]{1,0:T(8,128)S(1)}) custom-call(s32[1]{0:T(128)} %bitcast.6.refs_1_.refs_0_, bf16[1536,2048]{1,0:T(8,128)(2,1)} %get-tuple-element.204.refs_1_, bf16[1536,2048]{1,0:T(8,128)(2,1)} %bitcast.86, ...), custom_call_target="tpu_custom_call", output_to_operand_aliasing={{0}: (13, {})} | custom-call | tf_op jit(solution)/shard_map/key_back/pallas_call | solution.py:64
  387.6 7.3 %normed_back.1 = (f32[384,1024]{1,0:T(8,128)}, f32[8,128]{1,0:T(8,128)S(1)}) custom-call(bf16[384,2048]{1,0:T(8,128)(2,1)S(1)} %copy-done.3, bf16[2,384,1024]{2,1,0:T(8,128)(2,1)S(1)} %copy-done.4, bf16[1024,4224]{1,0:T(8,128)(2,1)} %get-tuple-element.169.refs_1_.refs_2_.refs_3_.refs_4_, ...), custom_call_target="tpu_custom_call" | custom-call | tf_op jit(solution)/shard_map/normed_back/pallas_call | solution.py:64
  406.9 5.5 %collective-permute-start.41 = (bf16[384,1024]{1,0:T(8,128)(2,1)}, bf16[384,1024]{1,0:T(8,128)(2,1)}, u32[]{:S(2)}, u32[]{:S(2)}) collective-permute-start(bf16[384,1024]{1,0:T(8,128)(2,1)} %get-tuple-element.276), channel_id=1, source_target_pairs={{0,1},{3,2},{4,5},{7,6},{8,9},{11,10},{12,13},{15,14},{16,17},{19,... | collective-permute-start | bytes 2359304 | tf_op jit(solution)/shard_map/ppermute | solution.py:1028
  429.7 4.6 collective-permute-done.35.refs_2_
  446.1 4.6 collective-permute-start.39
  464.1 17.3 %collective-permute-done.43 = bf16[128,1024]{1,0:T(8,128)(2,1)S(1)} collective-permute-done((bf16[128,1024]{1,0:T(8,128)(2,1)S(1)}, bf16[128,1024]{1,0:T(8,128)(2,1)S(1)}, u32[]{:S(2)}, u32[]{:S(2)}) %collective-permute-start.43) | collective-permute-done | bytes 262176 | tf_op jit(solution)/shard_map/ppermute | solution.py:919
  481.5 7.5 %collective-permute-done.42.refs_1_ = f32[18,128]{1,0:T(8,128)S(1)} collective-permute-done((f32[18,128]{1,0:T(8,128)S(1)}, f32[18,128]{1,0:T(8,128)S(1)}, u32[]{:S(2)}, u32[]{:S(2)}) %collective-permute-start.42) | collective-permute-done | bytes 9248 | tf_op jit(solution)/shard_map/ppermute | solution.py:919
  491.8 4.4 collective-permute-start.45
  500.6 9.6 %collective-permute-done.49.refs_2_ = bf16[384,1024]{1,0:T(8,128)(2,1)} collective-permute-done((bf16[384,1024]{1,0:T(8,128)(2,1)S(1)}, bf16[384,1024]{1,0:T(8,128)(2,1)}, u32[]{:S(2)}, u32[]{:S(2)}) %collective-permute-start.49) | collective-permute-done | bytes 786464 | tf_op jit(solution)/shard_map/ppermute | solution.py:1028
  (367 shorter events, 182.4 us)
Async XLA Ops:
  7.2 153.6 %all-gather.3.cloned.1.call-start = ((), (), s32[]{:S(2)}) async-start(), calls=%async_computation.4 | async-start | bytes 25952256 | tf_op jit(solution)/shard_map/all_gather | solution.py:1160
  14.7 293.2 %reduce-scatter.3.cloned.1.call-start = ((), (), s32[]{:S(2)}) async-start(), calls=%async_computation.2 | async-start | bytes 14155776 | tf_op jit(solution)/shard_map/reduce_scatter | solution.py:1236
  15.8 22.5 %collective-permute-start.10 = (bf16[384,1024]{1,0:T(8,128)(2,1)S(1)}, bf16[384,1024]{1,0:T(8,128)(2,1)S(1)}, u32[]{:S(2)}, u32[]{:S(2)}) collective-permute-start(bf16[384,1024]{1,0:T(8,128)(2,1)S(1)} %bitcast.51), channel_id=1, source_target_pairs={{1,0},{2,1},{3,2},{5,4},{6,5},{7,6},{9,8},{10,9},{11,10},{13,12},{... | collective-permute-start | bytes 2359304 | tf_op jit(solution)/shard_map/ppermute | solution.py:1064
  17.1 22.3 %collective-permute-start.9 = (bf16[384,1024]{1,0:T(8,128)(2,1)S(1)}, bf16[384,1024]{1,0:T(8,128)(2,1)S(1)}, u32[]{:S(2)}, u32[]{:S(2)}) collective-permute-start(bf16[384,1024]{1,0:T(8,128)(2,1)S(1)} %bitcast.52), channel_id=1, source_target_pairs={{0,1},{1,2},{2,3},{4,5},{5,6},{6,7},{8,9},{9,10},{10,11},{12,13},{... | collective-permute-start | bytes 2359304 | tf_op jit(solution)/shard_map/ppermute | solution.py:1062
  22.7 50.8 %collective-permute-start.3 = (bf16[128,4224]{1,0:T(8,128)(2,1)}, bf16[128,4224]{1,0:T(8,128)(2,1)}, u32[]{:S(2)}, u32[]{:S(2)}) collective-permute-start(bf16[128,4224]{1,0:T(8,128)(2,1)} %get-tuple-element.159.refs_1_), channel_id=1, source_target_pairs={{0,16},{4,20},{8,24},{12,28},{16,0},{20,4},{24,8},{28,12},{1,17},{... | collective-permute-start | bytes 3244040 | tf_op jit(solution)/shard_map/ppermute | solution.py:919
  24.7 46.9 %collective-permute-start.1 = (bf16[128,4224]{1,0:T(8,128)(2,1)}, bf16[128,4224]{1,0:T(8,128)(2,1)}, u32[]{:S(2)}, u32[]{:S(2)}) collective-permute-start(bf16[128,4224]{1,0:T(8,128)(2,1)} %get-tuple-element.159.refs_1_), channel_id=1, source_target_pairs={{0,8},{4,12},{8,0},{12,4},{16,24},{20,28},{24,16},{28,20},{1,9},{5... | collective-permute-start | bytes 3244040 | tf_op jit(solution)/shard_map/ppermute | solution.py:919
  26.2 72.1 %collective-permute-start = (bf16[128,4224]{1,0:T(8,128)(2,1)}, bf16[128,4224]{1,0:T(8,128)(2,1)}, u32[]{:S(2)}, u32[]{:S(2)}) collective-permute-start(bf16[128,4224]{1,0:T(8,128)(2,1)} %get-tuple-element.159.refs_1_), channel_id=1, source_target_pairs={{0,4},{4,0},{8,12},{12,8},{16,20},{20,16},{24,28},{28,24},{1,5},{5... | collective-permute-start | bytes 3244040 | tf_op jit(solution)/shard_map/ppermute | solution.py:919
  42.9 34.2 %collective-permute-start.11 = (bf16[384,1024]{1,0:T(8,128)(2,1)}, bf16[384,1024]{1,0:T(8,128)(2,1)S(1)}, u32[]{:S(2)}, u32[]{:S(2)}) collective-permute-start(bf16[384,1024]{1,0:T(8,128)(2,1)} %get-tuple-element.162), channel_id=1, source_target_pairs={{1,2},{2,3},{5,6},{6,7},{9,10},{10,11},{13,14},{14,15},{17,18},{18... | collective-permute-start | bytes 2359304 | tf_op jit(solution)/shard_map/ppermute | solution.py:1062
  43.6 33.5 %collective-permute-start.12 = (bf16[384,1024]{1,0:T(8,128)(2,1)}, bf16[384,1024]{1,0:T(8,128)(2,1)S(1)}, u32[]{:S(2)}, u32[]{:S(2)}) collective-permute-start(bf16[384,1024]{1,0:T(8,128)(2,1)} %get-tuple-element.163), channel_id=1, source_target_pairs={{1,0},{2,1},{5,4},{6,5},{9,8},{10,9},{13,12},{14,13},{17,16},{18,1... | collective-permute-start | bytes 2359304 | tf_op jit(solution)/shard_map/ppermute | solution.py:1064
  77.1 25.7 %collective-permute-start.4 = (bf16[128,4224]{1,0:T(8,128)(2,1)}, bf16[128,4224]{1,0:T(8,128)(2,1)}, u32[]{:S(2)}, u32[]{:S(2)}) collective-permute-start(bf16[128,4224]{1,0:T(8,128)(2,1)} %collective-permute-done.3.refs_2_.refs_5_), channel_id=1, source_target_pairs={{0,4},{4,0},{8,12},{12,8},{16,20},{20,16},{24,28},{28,24},{1,5},{5... | collective-permute-start | bytes 3244040 | tf_op jit(solution)/shard_map/ppermute | solution.py:919
  77.2 25.7 %collective-permute-start.2 = (bf16[128,4224]{1,0:T(8,128)(2,1)}, bf16[128,4224]{1,0:T(8,128)(2,1)}, u32[]{:S(2)}, u32[]{:S(2)}) collective-permute-start(bf16[128,4224]{1,0:T(8,128)(2,1)} %collective-permute-done.1.refs_1_.refs_3_), channel_id=1, source_target_pairs={{0,4},{4,0},{8,12},{12,8},{16,20},{20,16},{24,28},{28,24},{1,5},{5... | collective-permute-start | bytes 3244040 | tf_op jit(solution)/shard_map/ppermute | solution.py:919
  98.3 22.8 %collective-permute-start.13 = (bf16[384,1024]{1,0:T(8,128)(2,1)}, bf16[384,1024]{1,0:T(8,128)(2,1)}, u32[]{:S(2)}, u32[]{:S(2)}) collective-permute-start(bf16[384,1024]{1,0:T(8,128)(2,1)} %get-tuple-element.172), channel_id=1, source_target_pairs={{2,3},{6,7},{10,11},{14,15},{18,19},{22,23},{26,27},{30,31}} | collective-permute-start | bytes 2359304 | tf_op jit(solution)/shard_map/ppermute | solution.py:1062
  100.0 22.0 %collective-permute-start.14 = (bf16[384,1024]{1,0:T(8,128)(2,1)}, bf16[384,1024]{1,0:T(8,128)(2,1)}, u32[]{:S(2)}, u32[]{:S(2)}) collective-permute-start(bf16[384,1024]{1,0:T(8,128)(2,1)} %get-tuple-element.173), channel_id=1, source_target_pairs={{1,0},{5,4},{9,8},{13,12},{17,16},{21,20},{25,24},{29,28}} | collective-permute-start | bytes 2359304 | tf_op jit(solution)/shard_map/ppermute | solution.py:1064
  203.7 201.1 %reduce-scatter.5.cloned.1.call-start = ((), (), s32[]{:S(2)}) async-start(), calls=%async_computation.3 | async-start | bytes 7077888 | tf_op jit(solution)/shard_map/reduce_scatter | solution.py:1256
  204.8 23.7 %collective-permute-start.16 = (bf16[432,1024]{1,0:T(8,128)(2,1)S(1)}, bf16[432,1024]{1,0:T(8,128)(2,1)S(1)}, u32[]{:S(2)}, u32[]{:S(2)}) collective-permute-start(bf16[432,1024]{1,0:T(8,128)(2,1)S(1)} %copy-done.45), channel_id=1, source_target_pairs={{1,0},{2,1},{3,2},{5,4},{6,5},{7,6},{9,8},{10,9},{11,10},{13,12},{... | collective-permute-start | bytes 2654216 | tf_op jit(solution)/shard_map/ppermute | solution.py:1064
  206.1 23.6 %collective-permute-start.15 = (bf16[432,1024]{1,0:T(8,128)(2,1)S(1)}, bf16[432,1024]{1,0:T(8,128)(2,1)S(1)}, u32[]{:S(2)}, u32[]{:S(2)}) collective-permute-start(bf16[432,1024]{1,0:T(8,128)(2,1)S(1)} %copy-done.45), channel_id=1, source_target_pairs={{0,1},{1,2},{2,3},{4,5},{5,6},{6,7},{8,9},{9,10},{10,11},{12,13},{... | collective-permute-start | bytes 2654216 | tf_op jit(solution)/shard_map/ppermute | solution.py:1062
  234.2 25.8 %collective-permute-start.18 = (bf16[432,1024]{1,0:T(8,128)(2,1)}, bf16[432,1024]{1,0:T(8,128)(2,1)S(1)}, u32[]{:S(2)}, u32[]{:S(2)}) collective-permute-start(bf16[432,1024]{1,0:T(8,128)(2,1)} %get-tuple-element.200), channel_id=1, source_target_pairs={{1,0},{2,1},{5,4},{6,5},{9,8},{10,9},{13,12},{14,13},{17,16},{18,1... | collective-permute-start | bytes 2654216 | tf_op jit(solution)/shard_map/ppermute | solution.py:1064
  263.8 19.6 %collective-permute-start.19 = (bf16[432,1024]{1,0:T(8,128)(2,1)}, bf16[432,1024]{1,0:T(8,128)(2,1)S(1)}, u32[]{:S(2)}, u32[]{:S(2)}) collective-permute-start(bf16[432,1024]{1,0:T(8,128)(2,1)} %get-tuple-element.205), channel_id=1, source_target_pairs={{2,3},{6,7},{10,11},{14,15},{18,19},{22,23},{26,27},{30,31}} | collective-permute-start | bytes 2654216 | tf_op jit(solution)/shard_map/ppermute | solution.py:1062
  264.6 21.7 %collective-permute-start.20 = (bf16[432,1024]{1,0:T(8,128)(2,1)}, bf16[432,1024]{1,0:T(8,128)(2,1)S(1)}, u32[]{:S(2)}, u32[]{:S(2)}) collective-permute-start(bf16[432,1024]{1,0:T(8,128)(2,1)} %get-tuple-element.206), channel_id=1, source_target_pairs={{1,0},{5,4},{9,8},{13,12},{17,16},{21,20},{25,24},{29,28}} | collective-permute-start | bytes 2654216 | tf_op jit(solution)/shard_map/ppermute | solution.py:1064
  311.0 50.7 %collective-permute-start.23 = (bf16[128,6144]{1,0:T(8,128)(2,1)}, bf16[128,6144]{1,0:T(8,128)(2,1)}, u32[]{:S(2)}, u32[]{:S(2)}) collective-permute-start(bf16[128,6144]{1,0:T(8,128)(2,1)} %get-tuple-element.222), channel_id=1, source_target_pairs={{0,1},{3,2},{4,5},{7,6},{8,9},{11,10},{12,13},{15,14},{16,17},{19,... | collective-permute-start | bytes 4718600 | tf_op jit(solution)/shard_map/ppermute | solution.py:1028
  315.5 41.3 %collective-permute-start.24 = (bf16[2,128,2048]{2,1,0:T(8,128)(2,1)}, bf16[2,128,2048]{2,1,0:T(8,128)(2,1)}, u32[]{:S(2)}, u32[]{:S(2)}) collective-permute-start(bf16[2,128,2048]{2,1,0:T(8,128)(2,1)} %copy-done.78), channel_id=1, source_target_pairs={{0,8},{4,12},{8,0},{12,4},{16,24},{20,28},{24,16},{28,20},{1,9},{5... | collective-permute-start | bytes 3145736 | tf_op jit(solution)/shard_map/ppermute | solution.py:919
  316.9 41.8 %collective-permute-start.25 = (bf16[2,128,2048]{2,1,0:T(8,128)(2,1)}, bf16[2,128,2048]{2,1,0:T(8,128)(2,1)}, u32[]{:S(2)}, u32[]{:S(2)}) collective-permute-start(bf16[2,128,2048]{2,1,0:T(8,128)(2,1)} %copy-done.77), channel_id=1, source_target_pairs={{0,16},{4,20},{8,24},{12,28},{16,0},{20,4},{24,8},{28,12},{1,17},{... | collective-permute-start | bytes 3145736 | tf_op jit(solution)/shard_map/ppermute | solution.py:919
  364.5 33.7 %collective-permute-start.31 = (bf16[128,6144]{1,0:T(8,128)(2,1)S(1)}, bf16[128,6144]{1,0:T(8,128)(2,1)S(1)}, u32[]{:S(2)}, u32[]{:S(2)}) collective-permute-start(bf16[128,6144]{1,0:T(8,128)(2,1)S(1)} %bitcast.61), channel_id=1, source_target_pairs={{1,2},{2,1},{5,6},{6,5},{9,10},{10,9},{13,14},{14,13},{17,18},{18,... | collective-permute-start | bytes 4718600 | tf_op jit(solution)/shard_map/ppermute | solution.py:1028
  385.3 37.5 %collective-permute-start.37 = (bf16[256,2048]{1,0:T(8,128)(2,1)}, bf16[256,2048]{1,0:T(8,128)(2,1)}, u32[]{:S(2)}, u32[]{:S(2)}) collective-permute-start(bf16[256,2048]{1,0:T(8,128)(2,1)} %get-tuple-element.268), channel_id=1, source_target_pairs={{0,1},{3,2},{4,5},{7,6},{8,9},{11,10},{12,13},{15,14},{16,17},{19,... | collective-permute-start | bytes 3145736 | tf_op jit(solution)/shard_map/ppermute | solution.py:1028
  401.8 49.7 %collective-permute-start.40 = (bf16[128,6144]{1,0:T(8,128)(2,1)S(1)}, bf16[128,6144]{1,0:T(8,128)(2,1)S(1)}, u32[]{:S(2)}, u32[]{:S(2)}) collective-permute-start(bf16[128,6144]{1,0:T(8,128)(2,1)S(1)} %bitcast.63), channel_id=1, source_target_pairs={{1,0},{2,3},{5,4},{6,7},{9,8},{10,11},{13,12},{14,15},{17,16},{18,... | collective-permute-start | bytes 4718600 | tf_op jit(solution)/shard_map/ppermute | solution.py:1028
  406.9 35.3 %collective-permute-start.41 = (bf16[384,1024]{1,0:T(8,128)(2,1)}, bf16[384,1024]{1,0:T(8,128)(2,1)}, u32[]{:S(2)}, u32[]{:S(2)}) collective-permute-start(bf16[384,1024]{1,0:T(8,128)(2,1)} %get-tuple-element.276), channel_id=1, source_target_pairs={{0,1},{3,2},{4,5},{7,6},{8,9},{11,10},{12,13},{15,14},{16,17},{19,... | collective-permute-start | bytes 2359304 | tf_op jit(solution)/shard_map/ppermute | solution.py:1028
  425.5 32.7 %collective-permute-start.44 = (bf16[256,2048]{1,0:T(8,128)(2,1)}, bf16[256,2048]{1,0:T(8,128)(2,1)}, u32[]{:S(2)}, u32[]{:S(2)}) collective-permute-start(bf16[256,2048]{1,0:T(8,128)(2,1)} %bitcast.35), channel_id=1, source_target_pairs={{1,2},{2,1},{5,6},{6,5},{9,10},{10,9},{13,14},{14,13},{17,18},{18,... | collective-permute-start | bytes 3145736 | tf_op jit(solution)/shard_map/ppermute | solution.py:1028
  444.5 44.4 %collective-permute-start.46 = (bf16[384,1024]{1,0:T(8,128)(2,1)}, bf16[384,1024]{1,0:T(8,128)(2,1)}, u32[]{:S(2)}, u32[]{:S(2)}) collective-permute-start(bf16[384,1024]{1,0:T(8,128)(2,1)} %bitcast.37), channel_id=1, source_target_pairs={{1,2},{2,1},{5,6},{6,5},{9,10},{10,9},{13,14},{14,13},{17,18},{18,... | collective-permute-start | bytes 2359304 | tf_op jit(solution)/shard_map/ppermute | solution.py:1028
  456.4 25.0 %collective-permute-start.43 = (bf16[128,1024]{1,0:T(8,128)(2,1)S(1)}, bf16[128,1024]{1,0:T(8,128)(2,1)S(1)}, u32[]{:S(2)}, u32[]{:S(2)}) collective-permute-start(bf16[128,1024]{1,0:T(8,128)(2,1)S(1)} %bitcast.73), channel_id=1, source_target_pairs={{0,2},{1,3},{2,0},{3,1},{4,6},{5,7},{6,4},{7,5},{8,10},{9,11},{10,... | collective-permute-start | bytes 786440 | tf_op jit(solution)/shard_map/ppermute | solution.py:919
  460.0 39.1 %collective-permute-start.47 = (bf16[256,2048]{1,0:T(8,128)(2,1)S(1)}, bf16[256,2048]{1,0:T(8,128)(2,1)S(1)}, u32[]{:S(2)}, u32[]{:S(2)}) collective-permute-start(bf16[256,2048]{1,0:T(8,128)(2,1)S(1)} %bitcast.65), channel_id=1, source_target_pairs={{1,0},{2,3},{5,4},{6,7},{9,8},{10,11},{13,12},{14,15},{17,16},{18,... | collective-permute-start | bytes 3145736 | tf_op jit(solution)/shard_map/ppermute | solution.py:1028
  461.3 27.6 %collective-permute-start.42 = (f32[18,128]{1,0:T(8,128)S(1)}, f32[18,128]{1,0:T(8,128)S(1)}, u32[]{:S(2)}, u32[]{:S(2)}) collective-permute-start(f32[18,128]{1,0:T(8,128)S(1)} %get-tuple-element.281.refs_0_), channel_id=1, source_target_pairs={{0,1},{1,0},{2,3},{3,2},{4,5},{5,4},{6,7},{7,6},{8,9},{9,8},{10,11... | collective-permute-start | bytes 27656 | tf_op jit(solution)/shard_map/ppermute | solution.py:919
  490.5 19.7 %collective-permute-start.49 = (bf16[384,1024]{1,0:T(8,128)(2,1)S(1)}, bf16[384,1024]{1,0:T(8,128)(2,1)}, u32[]{:S(2)}, u32[]{:S(2)}) collective-permute-start(bf16[384,1024]{1,0:T(8,128)(2,1)S(1)} %bitcast.67), channel_id=1, source_target_pairs={{1,0},{2,3},{5,4},{6,7},{9,8},{10,11},{13,12},{14,15},{17,16},{18,... | collective-permute-start | bytes 2359304 | tf_op jit(solution)/shard_map/ppermute | solution.py:1028
  (121 other events, 1262.4 us)
Sparse Core Ops, SparseCore 0:
  14.8 145.8 all-gather.2
  203.8 92.3 reduce-scatter.2
  299.6 80.5 reduce-scatter.4

commit v4 on v3

--- a/solution.py
+++ b/solution.py
@@ -21,11 +21,15 @@
 F32 = jnp.float32
 BF16 = jnp.bfloat16
 MIB = 1 << 20
-VMEM_MIB = 20
+VMEM_MIB = 16
 LARGE = 1 << 18
 
 
 ORDER = []
+
+
+def room(pack):
+    return VMEM_MIB * max(1, pack // 1536)
 
 
 def shape(dims, dtype):
@@ -147,7 +151,7 @@
 
     return call(
         name, body, sources, in_specs or [IN_VMEM] * count, out_specs or [IN_VMEM] * len(out_shape), out_shape,
-        prefetch=prefetch, after=after,
+        prefetch=prefetch, after=after, vmem=24,
     )
 
 
@@ -290,7 +294,7 @@
             pl.BlockSpec((width, block), lambda j: (0, (inner + cols) // block + j)),
         ]
         + [IN_VMEM] * 3,
-        [col, col, col], [shape((rows, cols), BF16)] * 3, grid=(cols // block,),
+        [col, col, col], [shape((rows, cols), BF16)] * 3, grid=(cols // block,), vmem=room(rows),
     )
 
 
@@ -329,7 +333,7 @@
         [col, key, key, whole((rows, 1)), whole((rows, 1)), whole((1, pack))],
         [col, pl.BlockSpec((GROUPS, 8, rows), lambda g: (g, 0, 0))],
         [shape((rows, HEADS * HEAD_DIM), BF16), shape((HEADS, 8, rows), F32)],
-        grid=(KV_HEADS,),
+        grid=(KV_HEADS,), vmem=room(pack),
         scratch=[pltpu.VMEM((rows, pack), F32)],
     )
 
@@ -365,17 +369,15 @@
         gate_copies = [move(3 + i, 1, 1 + i) for i in range(3)]
         up_copies = [move(6 + i, 1, 4 + i) for i in range(3)]
         down_copy = move(0, 3, 7)
-        out_copy.start()
-        loads[1].start()
-        loads[2].start()
+        for copy in (out_copy, loads[1], loads[2]):
+            copy.start()
+        for copy in [out_copy] + loads:
+            copy.wait()
         for a, b in zip(gate_copies, up_copies):
             a.start()
             b.start()
         down_copy.start()
 
-        for load in loads:
-            load.wait()
-        out_copy.wait()
         for j in range(width // block):
             cols = slice(j * block, (j + 1) * block)
             part = w[:, 9 * unit : 11 * unit, cols].reshape(inner, block)
@@ -545,7 +547,7 @@
         + [ANY] * len(earlier),
         [col, whole((1, HEAD_DIM))],
         [shape((rows, HEADS * HEAD_DIM), BF16), shape((1, HEAD_DIM), F32)],
-        grid=(count,),
+        grid=(count,), vmem=room(pack),
         scratch=[pltpu.VMEM((rows, pack), F32)],
         aliases={13: 0} if earlier else None,
     )
@@ -616,7 +618,7 @@
         + [ANY] * len(earlier),
         [pl.BlockSpec((2, rows, HEAD_DIM), lambda g, at: (0, 0, first + g)), whole((1, HEAD_DIM))],
         [shape((2, rows, KV_HEADS * HEAD_DIM), BF16), shape((1, HEAD_DIM), F32)],
-        grid=(count,),
+        grid=(count,), vmem=room(pack),
         scratch=[pltpu.VMEM((rows, pack), F32), pltpu.VMEM((2, rows, HEAD_DIM), F32)],
         prefetch=[ctx_at], aliases={12: 0} if earlier else None,
     )
@@ -640,7 +642,7 @@
         "all_queries", body, [x, weights, gain, cos, sin],
         [IN_VMEM, pl.BlockSpec((width, block), lambda j: (0, j)), IN_VMEM, IN_VMEM, IN_VMEM],
         [pl.BlockSpec((rows, block), lambda j: (0, j))], [shape((rows, cols), BF16)],
-        grid=(cols // block,),
+        grid=(cols // block,), vmem=room(rows),
     )[0]
 
 
@@ -1252,8 +1254,6 @@
     every_query = all_queries(normed_pack, attn_w, gain_query, cos_pack, sin_pack)
 
     touch([parcels.from_left[-1], parcels.from_right[-1]])
-    down_grad = weight_grad(hidden, grad_out, block=256)[0]
-    down_grad = lax.psum_scatter(down_grad, "dp", scatter_dimension=0, tiled=True)
     outer.over_dp()
     wide_grad = copies(
         "take", [wide_grad], lambda _, ins, outs: [(ins[0], outs[0])], [shape(wide_grad.shape, BF16)]
@@ -1276,6 +1276,8 @@
     for _ in range(later_dp):
         outer.over_dp()
     wide.step()
+    down_grad = weight_grad(hidden, grad_out, block=256)[0]
+    down_grad = lax.psum_scatter(down_grad, "dp", scatter_dimension=0, tiled=True)
 
     d_pair, key_more = key_back(*key_args, half_heads, half_heads, (d_pair,))
     query_part, key_part = query_part + query_more, key_part + key_more
@@ -1289,22 +1291,23 @@
 
     wide.finish()
     pair.over_dp()
-    down_grad = copies(
-        "take", [down_grad], lambda _, ins, outs: [(ins[0], outs[0])], [shape(down_grad.shape, BF16)]
-    )[0]
-    down = Line(down_grad)
     small = Everywhere(
         jnp.concatenate([attn_part, mlp_part, query_part, key_part], axis=1).reshape(-1, HEAD_DIM)
     )
+    small.step()
 
     for _ in range(later_dp):
         pair.over_dp()
+    outer.step()
     small.step()
-    outer.step()
+    down_grad = copies(
+        "take", [down_grad], lambda _, ins, outs: [(ins[0], outs[0])], [shape(down_grad.shape, BF16)],
+        in_specs=[whole(down_grad.shape)], out_specs=[whole(down_grad.shape)],
+    )[0]
+    down_sum = lax.psum(down_grad, "ctx")
 
     pair.to_ctx()
     small.step()
-    down.step()
     gate_grad, up_grad = wide.place(
         [(unit, 3 * width)] * 2,
         [((everything, slice(k * 3 * width, (k + 1) * 3 * width)), k, everything) for k in range(2)],
@@ -1313,11 +1316,10 @@
     pair.over_ctx()
     small.step()
     outer.finish()
+    touch([down_sum])
 
     for _ in range(later_ctx):
         pair.over_ctx()
-        small.step()
-    down.finish()
     small = small.finish().reshape(-1)
     near, far_half = slice(0, width), slice(width, 2 * width)
     first, second = slice(0, unit), slice(unit, 2 * unit)
@@ -1329,7 +1331,7 @@
             ((second, everything), 1, everything),
         ],
     )
-    down_grad = down.place([down_grad.shape], [(everything, 0, everything)])[0]
+    down_grad = down_sum.astype(F32)
     key_grad, value_grad = place(
         [pair.total], odd, [(unit, width)] * 2, [(0, k, everything, k, everything) for k in range(2)]
     )

time: 526 us -> 508 us (0.966)
  starting transfers between devices: 73.7 us -> 58.7 us
  Pallas kernels: 236 us -> 227 us
  waiting for transfers between devices: 139 us -> 147 us
    psum x0 -> x1, waiting for transfers between devices: none -> 42.9 us  [on_device(): down_sum = lax.psum(down_grad, 'ctx')]
    ppermute x29, waiting for transfers between devices: 100 us -> 67.2 us  [swap(): return lax.ppermute(x, axis, [(i, i ^ bit) for i in range(size)])]
    ppermute x9 -> x6, waiting for transfers between devices: 9.64 us -> 0.02 us  [send(): self.came = lax.ppermute(self.total, 'ctx', pairs)]
    ppermute x9 -> x6, starting transfers between devices: 20.4 us -> 11.5 us  [send(): self.came = lax.ppermute(self.total, 'ctx', pairs)]
    pallas_call x53 -> x51, Pallas kernels: 236 us -> 227 us  [call(): pl.pallas_call(without, grid_spec=pltpu.PrefetchScalarGridSpec(num_scalar...]
    ppermute x6, waiting for transfers between devices: 21.7 us -> 29 us  [send(): lax.ppermute(left, 'ctx', [(i + 1, i) for i in range(self.size - 1 - step)])]
    ppermute x29, starting transfers between devices: 31.2 us -> 24.8 us  [swap(): return lax.ppermute(x, axis, [(i, i ^ bit) for i in range(size)])]
    unnamed x200 -> x186, local copies, waits for them, and re-layouts: 38.8 us -> 35.6 us
  transfers between devices with their start and end apart: 53 -> 51, of which waited for: 26 -> 20; matrix products, arithmetic and copies ran while one was open for 3% -> 3% of each run, Pallas kernels for 37% -> 34%
where the time goes in v4:
time: 508 us; the launch traced here: 502 us
  Pallas kernels  227 us (45%)
  waiting for transfers between devices  147 us (29%)
  starting transfers between devices  58.7 us (12%)
  local copies, waits for them, and re-layouts  42 us (8%)
  between operations  15.1 us (3%)
  other arithmetic  12.6 us (2%)
    pallas_call x51, Pallas kernels, call(): pl.pallas_call(without, grid_spec=pltpu.PrefetchScalarGridSpec(num_scalar...  227 us
    ppermute x29, waiting for transfers between devices, swap(): return lax.ppermute(x, axis, [(i, i ^ bit) for i in range(size)])  67.2 us
    psum x1, waiting for transfers between devices, on_device(): down_sum = lax.psum(down_grad, 'ctx')  42.9 us
    unnamed x186, local copies, waits for them, and re-layouts  35.6 us
    ppermute x6, waiting for transfers between devices, send(): lax.ppermute(left, 'ctx', [(i + 1, i) for i in range(self.size - 1 - step)])  29 us
    ppermute x29, starting transfers between devices, swap(): return lax.ppermute(x, axis, [(i, i ^ bit) for i in range(size)])  24.8 us
    ppermute x6, starting transfers between devices, send(): lax.ppermute(right, 'ctx', [(i, i + 1) for i in range(step, self.size - 1)])  13.9 us
    ppermute x6, starting transfers between devices, send(): self.came = lax.ppermute(self.total, 'ctx', pairs)  11.5 us
  transfers between devices with their start and end apart: 51, of which 20 were waited for; matrix products, arithmetic and copies ran while one was open for 3% of the time, Pallas kernels for 34%

profile of v4, /device:TPU:0, one launch (start us, length us, event | category | flops | bytes accessed | tf_op | source)
XLA Modules:
  0.0 502.4 jit_solution(18272480285136384325)
XLA Ops:
  17.1 5.6 %collective-permute-start.9 = (bf16[384,1024]{1,0:T(8,128)(2,1)S(1)}, bf16[384,1024]{1,0:T(8,128)(2,1)S(1)}, u32[]{:S(2)}, u32[]{:S(2)}) collective-permute-start(bf16[384,1024]{1,0:T(8,128)(2,1)S(1)} %bitcast.47), channel_id=1, source_target_pairs={{0,1},{1,2},{2,3},{4,5},{5,6},{6,7},{8,9},{9,10},{10,11},{12,13},{... | collective-permute-start | bytes 2359304 | tf_op jit(solution)/shard_map/ppermute | solution.py:1064
  27.1 4.4 fusion
  31.5 6.8 %collective-permute-done.10.refs_1_.refs_7_ = bf16[384,1024]{1,0:T(8,128)(2,1)S(1)} collective-permute-done((bf16[384,1024]{1,0:T(8,128)(2,1)S(1)}, bf16[384,1024]{1,0:T(8,128)(2,1)S(1)}, u32[]{:S(2)}, u32[]{:S(2)}) %collective-permute-start.10) | collective-permute-done | bytes 786464 | tf_op jit(solution)/shard_map/ppermute | solution.py:1066
  45.0 26.6 %collective-permute-done.1.refs_1_.refs_3_ = bf16[128,4224]{1,0:T(8,128)(2,1)} collective-permute-done((bf16[128,4224]{1,0:T(8,128)(2,1)}, bf16[128,4224]{1,0:T(8,128)(2,1)}, u32[]{:S(2)}, u32[]{:S(2)}) %collective-permute-start.1) | collective-permute-done | bytes 1081376 | tf_op jit(solution)/shard_map/ppermute | solution.py:921
  78.2 12.4 %collective-permute-done.5.refs_7_ = bf16[128,2048]{1,0:T(8,128)(2,1)} collective-permute-done((bf16[128,2048]{1,0:T(8,128)(2,1)S(1)}, bf16[128,2048]{1,0:T(8,128)(2,1)}, u32[]{:S(2)}, u32[]{:S(2)}) %collective-permute-start.5) | collective-permute-done | bytes 524320 | tf_op jit(solution)/shard_map/ppermute | solution.py:921
  103.2 8.1 %assemble_weights.1 = (bf16[1024,4224]{1,0:T(8,128)(2,1)}, bf16[1024,128]{1,0:T(8,128)(2,1)S(1)}, f32[8,128]{1,0:T(8,128)S(1)}) custom-call(s32[8]{0:T(128)S(1)} %iota_xor_fusion.refs_0_, bf16[128,4224]{1,0:T(8,128)(2,1)} %get-tuple-element.153.refs_1_, bf16[128,4224]{1,0:T(8,128)(2,1)} %collective-permute-done.refs_2_, ...), custom_call_target="tpu_custom_call" | custom-call | tf_op jit(solution)/shard_map/assemble_weights/pallas_call | solution.py:68
  112.5 8.8 %project_queries.1 = (bf16[384,2048]{1,0:T(8,128)(2,1)}, bf16[384,2048]{1,0:T(8,128)(2,1)}, f32[16,8,384]{2,1,0:T(8,128)S(1)}, f32[8,128]{1,0:T(8,128)S(1)}) custom-call(bf16[384,1024]{1,0:T(8,128)(2,1)S(1)} %get-tuple-element.162.refs_0_.refs_1_, bf16[1024,4224]{1,0:T(8,128)(2,1)} %get-tuple-element.163.refs_1_.refs_2_.refs_3_.refs_4_, ...), custom_call_target="tpu_custom_call" | custom-call | tf_op jit(solution)/shard_map/project_queries/pallas_call | solution.py:68
  122.0 4.7 norm_pack.1
  128.8 12.9 %project_keys_values.1 = (bf16[1536,1024]{1,0:T(8,128)(2,1)}, bf16[1536,1024]{1,0:T(8,128)(2,1)}, bf16[1536,1024]{1,0:T(8,128)(2,1)}, f32[8,128]{1,0:T(8,128)S(1)}) custom-call(bf16[1536,1024]{1,0:T(8,128)(2,1)S(1)} %bitcast.52, bf16[1024,4224]{1,0:T(8,128)(2,1)} %get-tuple-element.163.refs_1_.refs_2_.refs_3_.refs_4_, ...), custom_call_target="tpu_custom_call" | custom-call | tf_op jit(solution)/shard_map/project_keys_values/pallas_call | solution.py:68
  141.7 13.9 %attend.1 = (bf16[384,2048]{1,0:T(8,128)(2,1)}, f32[16,8,384]{2,1,0:T(8,128)S(1)}, f32[8,128]{1,0:T(8,128)S(1)}) custom-call(bf16[384,2048]{1,0:T(8,128)(2,1)} %get-tuple-element.165.refs_0_, bf16[1536,1024]{1,0:T(8,128)(2,1)} %get-tuple-element.171.refs_1_.refs_3_, bf16[1536,1024]{1,0:T(8,128)(2,1)} %get-tuple-element.172.refs_2_.refs_4_, ...), custom_call_target="tpu_custom_call" | custom-call | tf_op jit(solution)/shard_map/attend/pallas_call | solution.py:68
  155.7 5.1 %all-gather.3.cloned.1.call-done = bf16[11264,1024]{1,0:T(8,128)(2,1)} async-done(((bf16[1408,1024]{1,0:T(8,128)(2,1)}), bf16[11264,1024]{1,0:T(8,128)(2,1)}) %all-gather.3.cloned.1.call-update) | async-done | bytes 23068688 | tf_op jit(solution)/shard_map/all_gather | solution.py:1162
  162.2 28.1 %middle_block.1 = (bf16[384,1024]{1,0:T(8,128)(2,1)}, bf16[384,1024]{1,0:T(8,128)(2,1)S(1)}, bf16[384,3072]{1,0:T(8,128)(2,1)S(1)}, bf16[2,384,3072]{2,1,0:T(8,1...) custom-call(bf16[384,2048]{1,0:T(8,128)(2,1)S(1)} %copy-done, ...), custom_call_target="tpu_custom_call" | custom-call | tf_op jit(solution)/shard_map/middle_block/pallas_call | solution.py:68
  190.3 3.8 copy-done.18
  194.1 9.5 %weight_grad.5 = (bf16[1024,6144]{1,0:T(8,128)(2,1)}, f32[8,128]{1,0:T(8,128)S(1)}) custom-call(bf16[384,1024]{1,0:T(8,128)(2,1)S(1)} %get-tuple-element.182.refs_0_, bf16[2,384,3072]{2,1,0:T(8,128)(2,1)S(1)} %copy-done.18, f32[8,128]{1,0:T(8,128)S(1)} %get-tuple-element.184.refs_2_), custom_call_target="tpu_custom_call" | custom-call | tf_op jit(solution)/shard_map/weight_grad/pallas_call | solution.py:68
  206.1 4.6 collective-permute-start.15
  210.8 14.2 %query_back.2 = (bf16[384,2048]{1,0:T(8,128)(2,1)}, f32[1,128]{1,0:T(1,128)S(1)}, f32[8,128]{1,0:T(8,128)S(1)}) custom-call(bf16[384,2048]{1,0:T(8,128)(2,1)} %get-tuple-element.165.refs_0_, bf16[384,2048]{1,0:T(8,128)(2,1)} %get-tuple-element.180.refs_1_.refs_2_, bf16[384,2048]{1,0:T(8,128)(2,1)} %get-tuple-element.174.refs_0_.refs_2_.refs_1_, ...), custom_call_target="tpu_custom_call" | custom-call | tf_op jit(solution)/shard_map/query_back/pallas_call | solution.py:68
  235.5 12.9 %query_back.3 = (bf16[384,2048]{1,0:T(8,128)(2,1)}, f32[1,128]{1,0:T(1,128)S(1)}, f32[8,128]{1,0:T(8,128)S(1)}) custom-call(bf16[384,2048]{1,0:T(8,128)(2,1)} %get-tuple-element.165.refs_0_, bf16[384,2048]{1,0:T(8,128)(2,1)} %get-tuple-element.180.refs_1_.refs_2_, ...), custom_call_target="tpu_custom_call", output_to_operand_aliasing={{0}: (13, {})} | custom-call | tf_op jit(solution)/shard_map/query_back/pallas_call | solution.py:68
  248.9 11.2 %collective-permute-done.18.refs_1_.refs_10_ = bf16[432,1024]{1,0:T(8,128)(2,1)S(1)} collective-permute-done((bf16[432,1024]{1,0:T(8,128)(2,1)}, bf16[432,1024]{1,0:T(8,128)(2,1)S(1)}, u32[]{:S(2)}, u32[]{:S(2)}) %collective-permute-start.18) | collective-permute-done | bytes 884768 | tf_op jit(solution)/shard_map/ppermute | solution.py:1066
  269.1 12.5 %all_queries.1 = (bf16[1536,2048]{1,0:T(8,128)(2,1)}, f32[8,128]{1,0:T(8,128)S(1)}) custom-call(bf16[1536,1024]{1,0:T(8,128)(2,1)S(1)} %bitcast.53, bf16[1024,4224]{1,0:T(8,128)(2,1)} %get-tuple-element.163.refs_1_.refs_2_.refs_3_.refs_4_, f32[1,128]{1,0:T(1,128)S(1)} %copy-done.61, f32[1536,128]{1,0:T(8,128)S(1)} %copy-done.15, f32[1536,128]{1,0:T(8,128)S(1)} %copy-done.17, ...), custom_call_target="tpu_custom_call" | custom-call | tf_op jit(solution)/shard_map/all_queries/pallas_call | solution.py:68
  281.6 10.3 %collective-permute-done.20.refs_2_.refs_11_ = bf16[432,1024]{1,0:T(8,128)(2,1)S(1)} collective-permute-done((bf16[432,1024]{1,0:T(8,128)(2,1)}, bf16[432,1024]{1,0:T(8,128)(2,1)S(1)}, u32[]{:S(2)}, u32[]{:S(2)}) %collective-permute-start.20) | collective-permute-done | bytes 884768 | tf_op jit(solution)/shard_map/ppermute | solution.py:1066
  306.8 11.9 %all_grad_mixed.1 = (bf16[2,4,192,2048]{3,2,1,0:T(8,128)(2,1)}, f32[2,4,48,192]{3,2,1,0:T(8,128)S(1)}, f32[8,128]{1,0:T(8,128)S(1)}) custom-call(s32[4]{0:T(128)S(1)} %copy-done.71, s32[1]{0:T(128)} %bitcast.6.refs_1_.refs_0_, bf16[384,2048]{1,0:T(8,128)(2,1)S(1)} %copy-done.2, bf16[8,1408,1024]{2,1,0:T(8,128)(2,1)} %bitcast.74, ...), custom_call_target="tpu_custom_call" | custom-call | tf_op jit(solution)/shard_map/all_grad_mixed/pallas_call | solution.py:68
  321.7 12.8 %key_back.2 = (bf16[2,384,1024]{2,1,0:T(8,128)(2,1)}, f32[1,128]{1,0:T(1,128)S(1)}, f32[8,128]{1,0:T(8,128)S(1)}) custom-call(s32[1]{0:T(128)} %bitcast.6.refs_1_.refs_0_, bf16[1536,2048]{1,0:T(8,128)(2,1)} %get-tuple-element.198.refs_1_, bf16[1536,2048]{1,0:T(8,128)(2,1)} %bitcast.80, bf16[2,4,192,1024]{3,2,1,0:T(8,128)(2,1)} %bitcast.76, ...), custom_call_target="tpu_custom_call" | custom-call | tf_op jit(solution)/shard_map/key_back/pallas_call | solution.py:68
  342.7 6.2 %weight_grad.8 = (bf16[3072,1024]{1,0:T(8,128)(2,1)}, f32[8,128]{1,0:T(8,128)S(1)}) custom-call(bf16[384,3072]{1,0:T(8,128)(2,1)S(1)} %copy-done.34, bf16[384,1024]{1,0:T(8,128)(2,1)S(1)} %bitcast.55, f32[8,128]{1,0:T(8,128)S(1)} %get-tuple-element.222.refs_2_), custom_call_target="tpu_custom_call" | custom-call | tf_op jit(solution)/shard_map/weight_grad/pallas_call | solution.py:68
  351.9 12.9 %key_back.3 = (bf16[2,384,1024]{2,1,0:T(8,128)(2,1)}, f32[1,128]{1,0:T(1,128)S(1)}, f32[8,128]{1,0:T(8,128)S(1)}) custom-call(s32[1]{0:T(128)} %bitcast.6.refs_1_.refs_0_, bf16[1536,2048]{1,0:T(8,128)(2,1)} %get-tuple-element.198.refs_1_, bf16[1536,2048]{1,0:T(8,128)(2,1)} %bitcast.81, ...), custom_call_target="tpu_custom_call", output_to_operand_aliasing={{0}: (13, {})} | custom-call | tf_op jit(solution)/shard_map/key_back/pallas_call | solution.py:68
  369.9 3.9 collective-permute-start.33
  373.8 7.6 %normed_back.1 = (f32[384,1024]{1,0:T(8,128)}, f32[8,128]{1,0:T(8,128)S(1)}) custom-call(bf16[384,2048]{1,0:T(8,128)(2,1)S(1)} %copy-done.3, bf16[2,384,1024]{2,1,0:T(8,128)(2,1)S(1)} %copy-done.4, bf16[1024,4224]{1,0:T(8,128)(2,1)} %get-tuple-element.163.refs_1_.refs_2_.refs_3_.refs_4_, ...), custom_call_target="tpu_custom_call" | custom-call | tf_op jit(solution)/shard_map/normed_back/pallas_call | solution.py:68
  390.4 10.9 %collective-permute-done.34.refs_1_ = bf16[2,128,1024]{2,1,0:T(8,128)(2,1)S(1)} collective-permute-done((bf16[2,128,1024]{2,1,0:T(8,128)(2,1)S(1)}, bf16[2,128,1024]{2,1,0:T(8,128)(2,1)S(1)}, u32[]{:S(2)}, u32[]{:S(2)}) %collective-permute-start.34) | collective-permute-done | bytes 524320 | tf_op jit(solution)/shard_map/ppermute | solution.py:921
  410.0 6.3 %collective-permute-done.32.refs_1_ = f32[18,128]{1,0:T(8,128)S(1)} collective-permute-done((f32[18,128]{1,0:T(8,128)S(1)}, f32[18,128]{1,0:T(8,128)S(1)}, u32[]{:S(2)}, u32[]{:S(2)}) %collective-permute-start.32) | collective-permute-done | bytes 9248 | tf_op jit(solution)/shard_map/ppermute | solution.py:921
  423.8 4.4 collective-permute-start.40
  428.3 3.6 collective-permute-done.36.refs_1_
  442.2 42.9 %all-reduce.2.cloned.1.call-done.refs_1_ = bf16[384,1024]{1,0:T(8,128)(2,1)} async-done(((bf16[384,1024]{1,0:T(8,128)(2,1)}), bf16[384,1024]{1,0:T(8,128)(2,1)}) %all-reduce.2.cloned.1.call-update) | async-done | bytes 786448 | tf_op jit(solution)/shard_map/psum | solution.py:1307
  490.6 4.0 collective-permute-done.46.refs_2_
  (349 shorter events, 143.6 us)
Async XLA Ops:
  7.2 153.6 %all-gather.3.cloned.1.call-start = ((), (), s32[]{:S(2)}) async-start(), calls=%async_computation.5 | async-start | bytes 25952256 | tf_op jit(solution)/shard_map/all_gather | solution.py:1162
  14.7 284.0 %reduce-scatter.3.cloned.1.call-start = ((), (), s32[]{:S(2)}) async-start(), calls=%async_computation.2 | async-start | bytes 14155776 | tf_op jit(solution)/shard_map/reduce_scatter | solution.py:1238
  15.8 22.5 %collective-permute-start.10 = (bf16[384,1024]{1,0:T(8,128)(2,1)S(1)}, bf16[384,1024]{1,0:T(8,128)(2,1)S(1)}, u32[]{:S(2)}, u32[]{:S(2)}) collective-permute-start(bf16[384,1024]{1,0:T(8,128)(2,1)S(1)} %bitcast.46), channel_id=1, source_target_pairs={{1,0},{2,1},{3,2},{5,4},{6,5},{7,6},{9,8},{10,9},{11,10},{13,12},{... | collective-permute-start | bytes 2359304 | tf_op jit(solution)/shard_map/ppermute | solution.py:1066
  17.1 22.3 %collective-permute-start.9 = (bf16[384,1024]{1,0:T(8,128)(2,1)S(1)}, bf16[384,1024]{1,0:T(8,128)(2,1)S(1)}, u32[]{:S(2)}, u32[]{:S(2)}) collective-permute-start(bf16[384,1024]{1,0:T(8,128)(2,1)S(1)} %bitcast.47), channel_id=1, source_target_pairs={{0,1},{1,2},{2,3},{4,5},{5,6},{6,7},{8,9},{9,10},{10,11},{12,13},{... | collective-permute-start | bytes 2359304 | tf_op jit(solution)/shard_map/ppermute | solution.py:1064
  22.7 50.8 %collective-permute-start.3 = (bf16[128,4224]{1,0:T(8,128)(2,1)}, bf16[128,4224]{1,0:T(8,128)(2,1)}, u32[]{:S(2)}, u32[]{:S(2)}) collective-permute-start(bf16[128,4224]{1,0:T(8,128)(2,1)} %get-tuple-element.153.refs_1_), channel_id=1, source_target_pairs={{0,16},{4,20},{8,24},{12,28},{16,0},{20,4},{24,8},{28,12},{1,17},{... | collective-permute-start | bytes 3244040 | tf_op jit(solution)/shard_map/ppermute | solution.py:921
  24.8 46.9 %collective-permute-start.1 = (bf16[128,4224]{1,0:T(8,128)(2,1)}, bf16[128,4224]{1,0:T(8,128)(2,1)}, u32[]{:S(2)}, u32[]{:S(2)}) collective-permute-start(bf16[128,4224]{1,0:T(8,128)(2,1)} %get-tuple-element.153.refs_1_), channel_id=1, source_target_pairs={{0,8},{4,12},{8,0},{12,4},{16,24},{20,28},{24,16},{28,20},{1,9},{5... | collective-permute-start | bytes 3244040 | tf_op jit(solution)/shard_map/ppermute | solution.py:921
  26.2 72.1 %collective-permute-start = (bf16[128,4224]{1,0:T(8,128)(2,1)}, bf16[128,4224]{1,0:T(8,128)(2,1)}, u32[]{:S(2)}, u32[]{:S(2)}) collective-permute-start(bf16[128,4224]{1,0:T(8,128)(2,1)} %get-tuple-element.153.refs_1_), channel_id=1, source_target_pairs={{0,4},{4,0},{8,12},{12,8},{16,20},{20,16},{24,28},{28,24},{1,5},{5... | collective-permute-start | bytes 3244040 | tf_op jit(solution)/shard_map/ppermute | solution.py:921
  42.9 34.2 %collective-permute-start.11 = (bf16[384,1024]{1,0:T(8,128)(2,1)}, bf16[384,1024]{1,0:T(8,128)(2,1)S(1)}, u32[]{:S(2)}, u32[]{:S(2)}) collective-permute-start(bf16[384,1024]{1,0:T(8,128)(2,1)} %get-tuple-element.156), channel_id=1, source_target_pairs={{1,2},{2,3},{5,6},{6,7},{9,10},{10,11},{13,14},{14,15},{17,18},{18... | collective-permute-start | bytes 2359304 | tf_op jit(solution)/shard_map/ppermute | solution.py:1064
  43.6 33.5 %collective-permute-start.12 = (bf16[384,1024]{1,0:T(8,128)(2,1)}, bf16[384,1024]{1,0:T(8,128)(2,1)S(1)}, u32[]{:S(2)}, u32[]{:S(2)}) collective-permute-start(bf16[384,1024]{1,0:T(8,128)(2,1)} %get-tuple-element.157), channel_id=1, source_target_pairs={{1,0},{2,1},{5,4},{6,5},{9,8},{10,9},{13,12},{14,13},{17,16},{18,1... | collective-permute-start | bytes 2359304 | tf_op jit(solution)/shard_map/ppermute | solution.py:1066
  74.6 18.1 %collective-permute-start.6 = (bf16[128,2176]{1,0:T(8,128)(2,1)S(1)}, bf16[128,2176]{1,0:T(8,128)(2,1)}, u32[]{:S(2)}, u32[]{:S(2)}) collective-permute-start(bf16[128,2176]{1,0:T(8,128)(2,1)S(1)} %slice.37), channel_id=1, source_target_pairs={{0,8},{4,12},{8,0},{12,4},{16,24},{20,28},{24,16},{28,20},{1,9},{5... | collective-permute-start | bytes 1671176 | tf_op jit(solution)/shard_map/ppermute | solution.py:921
  77.2 26.0 %collective-permute-start.4 = (bf16[128,4224]{1,0:T(8,128)(2,1)}, bf16[128,4224]{1,0:T(8,128)(2,1)}, u32[]{:S(2)}, u32[]{:S(2)}) collective-permute-start(bf16[128,4224]{1,0:T(8,128)(2,1)} %collective-permute-done.3.refs_2_.refs_5_), channel_id=1, source_target_pairs={{0,4},{4,0},{8,12},{12,8},{16,20},{20,16},{24,28},{28,24},{1,5},{5... | collective-permute-start | bytes 3244040 | tf_op jit(solution)/shard_map/ppermute | solution.py:921
  77.2 26.0 %collective-permute-start.2 = (bf16[128,4224]{1,0:T(8,128)(2,1)}, bf16[128,4224]{1,0:T(8,128)(2,1)}, u32[]{:S(2)}, u32[]{:S(2)}) collective-permute-start(bf16[128,4224]{1,0:T(8,128)(2,1)} %collective-permute-done.1.refs_1_.refs_3_), channel_id=1, source_target_pairs={{0,4},{4,0},{8,12},{12,8},{16,20},{20,16},{24,28},{28,24},{1,5},{5... | collective-permute-start | bytes 3244040 | tf_op jit(solution)/shard_map/ppermute | solution.py:921
  98.4 22.9 %collective-permute-start.13 = (bf16[384,1024]{1,0:T(8,128)(2,1)}, bf16[384,1024]{1,0:T(8,128)(2,1)}, u32[]{:S(2)}, u32[]{:S(2)}) collective-permute-start(bf16[384,1024]{1,0:T(8,128)(2,1)} %get-tuple-element.166), channel_id=1, source_target_pairs={{2,3},{6,7},{10,11},{14,15},{18,19},{22,23},{26,27},{30,31}} | collective-permute-start | bytes 2359304 | tf_op jit(solution)/shard_map/ppermute | solution.py:1064
  100.0 22.0 %collective-permute-start.14 = (bf16[384,1024]{1,0:T(8,128)(2,1)}, bf16[384,1024]{1,0:T(8,128)(2,1)}, u32[]{:S(2)}, u32[]{:S(2)}) collective-permute-start(bf16[384,1024]{1,0:T(8,128)(2,1)} %get-tuple-element.167), channel_id=1, source_target_pairs={{1,0},{5,4},{9,8},{13,12},{17,16},{21,20},{25,24},{29,28}} | collective-permute-start | bytes 2359304 | tf_op jit(solution)/shard_map/ppermute | solution.py:1066
  203.7 212.6 %reduce-scatter.5.cloned.1.call-start = ((), (), s32[]{:S(2)}) async-start(), calls=%async_computation.3 | async-start | bytes 7077888 | tf_op jit(solution)/shard_map/reduce_scatter | solution.py:1280
  204.8 23.7 %collective-permute-start.16 = (bf16[432,1024]{1,0:T(8,128)(2,1)S(1)}, bf16[432,1024]{1,0:T(8,128)(2,1)S(1)}, u32[]{:S(2)}, u32[]{:S(2)}) collective-permute-start(bf16[432,1024]{1,0:T(8,128)(2,1)S(1)} %copy-done.45), channel_id=1, source_target_pairs={{1,0},{2,1},{3,2},{5,4},{6,5},{7,6},{9,8},{10,9},{11,10},{13,12},{... | collective-permute-start | bytes 2654216 | tf_op jit(solution)/shard_map/ppermute | solution.py:1066
  206.1 23.6 %collective-permute-start.15 = (bf16[432,1024]{1,0:T(8,128)(2,1)S(1)}, bf16[432,1024]{1,0:T(8,128)(2,1)S(1)}, u32[]{:S(2)}, u32[]{:S(2)}) collective-permute-start(bf16[432,1024]{1,0:T(8,128)(2,1)S(1)} %copy-done.45), channel_id=1, source_target_pairs={{0,1},{1,2},{2,3},{4,5},{5,6},{6,7},{8,9},{9,10},{10,11},{12,13},{... | collective-permute-start | bytes 2654216 | tf_op jit(solution)/shard_map/ppermute | solution.py:1064
  234.0 26.0 %collective-permute-start.18 = (bf16[432,1024]{1,0:T(8,128)(2,1)}, bf16[432,1024]{1,0:T(8,128)(2,1)S(1)}, u32[]{:S(2)}, u32[]{:S(2)}) collective-permute-start(bf16[432,1024]{1,0:T(8,128)(2,1)} %get-tuple-element.194), channel_id=1, source_target_pairs={{1,0},{2,1},{5,4},{6,5},{9,8},{10,9},{13,12},{14,13},{17,16},{18,1... | collective-permute-start | bytes 2654216 | tf_op jit(solution)/shard_map/ppermute | solution.py:1066
  235.3 58.5 %collective-permute-start.21 = (bf16[4,128,2048]{2,1,0:T(8,128)(2,1)S(1)}, bf16[4,128,2048]{2,1,0:T(8,128)(2,1)S(1)}, u32[]{:S(2)}, u32[]{:S(2)}) collective-permute-start(bf16[4,128,2048]{2,1,0:T(8,128)(2,1)S(1)} %get-tuple-element.203), channel_id=1, source_target_pairs={{0,4},{4,0},{8,12},{12,8},{16,20},{20,16},{24,28},{28,24},{1,5},{5... | collective-permute-start | bytes 6291464 | tf_op jit(solution)/shard_map/ppermute | solution.py:921
  267.0 26.9 %collective-permute-start.22 = (bf16[4,128,2048]{2,1,0:T(8,128)(2,1)S(1)}, bf16[4,128,2048]{2,1,0:T(8,128)(2,1)S(1)}, u32[]{:S(2)}, u32[]{:S(2)}) collective-permute-start(bf16[4,128,2048]{2,1,0:T(8,128)(2,1)S(1)} %get-tuple-element.205), channel_id=1, source_target_pairs={{0,4},{4,0},{8,12},{12,8},{16,20},{20,16},{24,28},{28,24},{1,5},{5... | collective-permute-start | bytes 6291464 | tf_op jit(solution)/shard_map/ppermute | solution.py:921
  267.8 24.1 %collective-permute-start.20 = (bf16[432,1024]{1,0:T(8,128)(2,1)}, bf16[432,1024]{1,0:T(8,128)(2,1)S(1)}, u32[]{:S(2)}, u32[]{:S(2)}) collective-permute-start(bf16[432,1024]{1,0:T(8,128)(2,1)} %get-tuple-element.200), channel_id=1, source_target_pairs={{1,0},{5,4},{9,8},{13,12},{17,16},{21,20},{25,24},{29,28}} | collective-permute-start | bytes 2654216 | tf_op jit(solution)/shard_map/ppermute | solution.py:1066
  301.5 37.6 %collective-permute-start.23 = (bf16[128,6144]{1,0:T(8,128)(2,1)}, bf16[128,6144]{1,0:T(8,128)(2,1)}, u32[]{:S(2)}, u32[]{:S(2)}) collective-permute-start(bf16[128,6144]{1,0:T(8,128)(2,1)} %get-tuple-element.215), channel_id=1, source_target_pairs={{0,1},{3,2},{4,5},{7,6},{8,9},{11,10},{12,13},{15,14},{16,17},{19,... | collective-permute-start | bytes 4718600 | tf_op jit(solution)/shard_map/ppermute | solution.py:1030
  304.2 30.2 %collective-permute-start.24 = (bf16[2,128,2048]{2,1,0:T(8,128)(2,1)}, bf16[2,128,2048]{2,1,0:T(8,128)(2,1)}, u32[]{:S(2)}, u32[]{:S(2)}) collective-permute-start(bf16[2,128,2048]{2,1,0:T(8,128)(2,1)} %copy-done.73), channel_id=1, source_target_pairs={{0,8},{4,12},{8,0},{12,4},{16,24},{20,28},{24,16},{28,20},{1,9},{5... | collective-permute-start | bytes 3145736 | tf_op jit(solution)/shard_map/ppermute | solution.py:921
  305.7 28.7 %collective-permute-start.25 = (bf16[2,128,2048]{2,1,0:T(8,128)(2,1)}, bf16[2,128,2048]{2,1,0:T(8,128)(2,1)}, u32[]{:S(2)}, u32[]{:S(2)}) collective-permute-start(bf16[2,128,2048]{2,1,0:T(8,128)(2,1)} %copy-done.72), channel_id=1, source_target_pairs={{0,16},{4,20},{8,24},{12,28},{16,0},{20,4},{24,8},{28,12},{1,17},{... | collective-permute-start | bytes 3145736 | tf_op jit(solution)/shard_map/ppermute | solution.py:921
  348.9 136.2 %all-reduce.2.cloned.1.call-start = ((), (), s32[]{:S(2)}) async-start(), calls=%async_computation.4 | async-start | bytes 1572864 | tf_op jit(solution)/shard_map/psum | solution.py:1307
  351.1 33.5 %collective-permute-start.31 = (bf16[128,6144]{1,0:T(8,128)(2,1)}, bf16[128,6144]{1,0:T(8,128)(2,1)S(1)}, u32[]{:S(2)}, u32[]{:S(2)}) collective-permute-start(bf16[128,6144]{1,0:T(8,128)(2,1)} %bitcast.56), channel_id=1, source_target_pairs={{1,2},{2,1},{5,6},{6,5},{9,10},{10,9},{13,14},{14,13},{17,18},{18,... | collective-permute-start | bytes 4718600 | tf_op jit(solution)/shard_map/ppermute | solution.py:1030
  369.9 34.3 %collective-permute-start.33 = (bf16[256,2048]{1,0:T(8,128)(2,1)S(1)}, bf16[256,2048]{1,0:T(8,128)(2,1)S(1)}, u32[]{:S(2)}, u32[]{:S(2)}) collective-permute-start(bf16[256,2048]{1,0:T(8,128)(2,1)S(1)} %get-tuple-element.251), channel_id=1, source_target_pairs={{0,1},{3,2},{4,5},{7,6},{8,9},{11,10},{12,13},{15,14},{16,17},{19,... | collective-permute-start | bytes 3145736 | tf_op jit(solution)/shard_map/ppermute | solution.py:1030
  387.2 44.7 %collective-permute-start.41 = (bf16[128,6144]{1,0:T(8,128)(2,1)S(1)}, bf16[128,6144]{1,0:T(8,128)(2,1)S(1)}, u32[]{:S(2)}, u32[]{:S(2)}) collective-permute-start(bf16[128,6144]{1,0:T(8,128)(2,1)S(1)} %bitcast.58), channel_id=1, source_target_pairs={{1,0},{2,3},{5,4},{6,7},{9,8},{10,11},{13,12},{14,15},{17,16},{18,... | collective-permute-start | bytes 4718600 | tf_op jit(solution)/shard_map/ppermute | solution.py:1030
  405.4 30.7 %collective-permute-start.44 = (bf16[256,2048]{1,0:T(8,128)(2,1)}, bf16[256,2048]{1,0:T(8,128)(2,1)}, u32[]{:S(2)}, u32[]{:S(2)}) collective-permute-start(bf16[256,2048]{1,0:T(8,128)(2,1)} %bitcast.33), channel_id=1, source_target_pairs={{1,2},{2,1},{5,6},{6,5},{9,10},{10,9},{13,14},{14,13},{17,18},{18,... | collective-permute-start | bytes 3145736 | tf_op jit(solution)/shard_map/ppermute | solution.py:1030
  437.9 51.3 %collective-permute-start.45 = (bf16[256,2048]{1,0:T(8,128)(2,1)S(1)}, bf16[256,2048]{1,0:T(8,128)(2,1)S(1)}, u32[]{:S(2)}, u32[]{:S(2)}) collective-permute-start(bf16[256,2048]{1,0:T(8,128)(2,1)S(1)} %bitcast.60), channel_id=1, source_target_pairs={{1,0},{2,3},{5,4},{6,7},{9,8},{10,11},{13,12},{14,15},{17,16},{18,... | collective-permute-start | bytes 3145736 | tf_op jit(solution)/shard_map/ppermute | solution.py:1030
  439.2 47.0 %collective-permute-start.43 = (bf16[128,1024]{1,0:T(8,128)(2,1)S(1)}, bf16[128,1024]{1,0:T(8,128)(2,1)S(1)}, u32[]{:S(2)}, u32[]{:S(2)}) collective-permute-start(bf16[128,1024]{1,0:T(8,128)(2,1)S(1)} %bitcast.67), channel_id=1, source_target_pairs={{0,2},{1,3},{2,0},{3,1},{4,6},{5,7},{6,4},{7,5},{8,10},{9,11},{10,... | collective-permute-start | bytes 786440 | tf_op jit(solution)/shard_map/ppermute | solution.py:921
  441.8 44.9 %collective-permute-start.42 = (f32[18,128]{1,0:T(8,128)S(1)}, f32[18,128]{1,0:T(8,128)S(1)}, u32[]{:S(2)}, u32[]{:S(2)}) collective-permute-start(f32[18,128]{1,0:T(8,128)S(1)} %get-tuple-element.275.refs_0_), channel_id=1, source_target_pairs={{0,2},{1,3},{2,0},{3,1},{4,6},{5,7},{6,4},{7,5},{8,10},{9,11},{10,... | collective-permute-start | bytes 27656 | tf_op jit(solution)/shard_map/ppermute | solution.py:921
  (112 other events, 1052.0 us)
Sparse Core Ops, SparseCore 0:
  14.8 145.8 all-gather.2
  203.8 92.4 reduce-scatter.2
  349.0 63.7 reduce-scatter.4
  428.3 56.7 all-reduce.1

commit v5 on v4

--- a/solution.py
+++ b/solution.py
@@ -1300,13 +1300,13 @@
         pair.over_dp()
     outer.step()
     small.step()
+
+    pair.to_ctx()
     down_grad = copies(
         "take", [down_grad], lambda _, ins, outs: [(ins[0], outs[0])], [shape(down_grad.shape, BF16)],
         in_specs=[whole(down_grad.shape)], out_specs=[whole(down_grad.shape)],
     )[0]
     down_sum = lax.psum(down_grad, "ctx")
-
-    pair.to_ctx()
     small.step()
     gate_grad, up_grad = wide.place(
         [(unit, 3 * width)] * 2,

time: 508 us -> 508 us (level)
  transfers between devices with their start and end apart: 51 -> 51, of which waited for: 20 -> 19; matrix products, arithmetic and copies ran while one was open for 3% -> 3% of each run, Pallas kernels for 34% -> 34%
where the time goes in v5:
time: 508 us; the launch traced here: 502 us
  Pallas kernels  227 us (45%)
  waiting for transfers between devices  147 us (29%)
  starting transfers between devices  58.7 us (12%)
  local copies, waits for them, and re-layouts  42 us (8%)
  between operations  15.1 us (3%)
  other arithmetic  12.6 us (2%)
    pallas_call x51, Pallas kernels, call(): pl.pallas_call(without, grid_spec=pltpu.PrefetchScalarGridSpec(num_scalar...  227 us
    ppermute x29, waiting for transfers between devices, swap(): return lax.ppermute(x, axis, [(i, i ^ bit) for i in range(size)])  67.2 us
    psum x1, waiting for transfers between devices, on_device(): down_sum = lax.psum(down_grad, 'ctx')  42.7 us
    unnamed x186, local copies, waits for them, and re-layouts  35.6 us
    ppermute x6, waiting for transfers between devices, send(): lax.ppermute(left, 'ctx', [(i + 1, i) for i in range(self.size - 1 - step)])  29 us
    ppermute x29, starting transfers between devices, swap(): return lax.ppermute(x, axis, [(i, i ^ bit) for i in range(size)])  24.8 us
    ppermute x6, starting transfers between devices, send(): lax.ppermute(right, 'ctx', [(i, i + 1) for i in range(step, self.size - 1)])  13.9 us
    ppermute x6, starting transfers between devices, send(): self.came = lax.ppermute(self.total, 'ctx', pairs)  11.5 us
  transfers between devices with their start and end apart: 51, of which 19 were waited for; matrix products, arithmetic and copies ran while one was open for 3% of the time, Pallas kernels for 34%

profile of v5, /device:TPU:0, one launch (start us, length us, event | category | flops | bytes accessed | tf_op | source)
XLA Modules:
  0.0 502.3 jit_solution(11924255776959847414)
XLA Ops:
  17.1 5.6 %collective-permute-start.9 = (bf16[384,1024]{1,0:T(8,128)(2,1)S(1)}, bf16[384,1024]{1,0:T(8,128)(2,1)S(1)}, u32[]{:S(2)}, u32[]{:S(2)}) collective-permute-start(bf16[384,1024]{1,0:T(8,128)(2,1)S(1)} %bitcast.47), channel_id=1, source_target_pairs={{0,1},{1,2},{2,3},{4,5},{5,6},{6,7},{8,9},{9,10},{10,11},{12,13},{... | collective-permute-start | bytes 2359304 | tf_op jit(solution)/shard_map/ppermute | solution.py:1064
  27.1 4.4 fusion
  31.5 6.8 %collective-permute-done.10.refs_1_.refs_7_ = bf16[384,1024]{1,0:T(8,128)(2,1)S(1)} collective-permute-done((bf16[384,1024]{1,0:T(8,128)(2,1)S(1)}, bf16[384,1024]{1,0:T(8,128)(2,1)S(1)}, u32[]{:S(2)}, u32[]{:S(2)}) %collective-permute-start.10) | collective-permute-done | bytes 786464 | tf_op jit(solution)/shard_map/ppermute | solution.py:1066
  45.0 26.6 %collective-permute-done.1.refs_1_.refs_3_ = bf16[128,4224]{1,0:T(8,128)(2,1)} collective-permute-done((bf16[128,4224]{1,0:T(8,128)(2,1)}, bf16[128,4224]{1,0:T(8,128)(2,1)}, u32[]{:S(2)}, u32[]{:S(2)}) %collective-permute-start.1) | collective-permute-done | bytes 1081376 | tf_op jit(solution)/shard_map/ppermute | solution.py:921
  78.2 12.4 %collective-permute-done.5.refs_7_ = bf16[128,2048]{1,0:T(8,128)(2,1)} collective-permute-done((bf16[128,2048]{1,0:T(8,128)(2,1)S(1)}, bf16[128,2048]{1,0:T(8,128)(2,1)}, u32[]{:S(2)}, u32[]{:S(2)}) %collective-permute-start.5) | collective-permute-done | bytes 524320 | tf_op jit(solution)/shard_map/ppermute | solution.py:921
  103.2 8.1 %assemble_weights.1 = (bf16[1024,4224]{1,0:T(8,128)(2,1)}, bf16[1024,128]{1,0:T(8,128)(2,1)S(1)}, f32[8,128]{1,0:T(8,128)S(1)}) custom-call(s32[8]{0:T(128)S(1)} %iota_xor_fusion.refs_0_, bf16[128,4224]{1,0:T(8,128)(2,1)} %get-tuple-element.153.refs_1_, bf16[128,4224]{1,0:T(8,128)(2,1)} %collective-permute-done.refs_2_, ...), custom_call_target="tpu_custom_call" | custom-call | tf_op jit(solution)/shard_map/assemble_weights/pallas_call | solution.py:68
  112.5 8.8 %project_queries.1 = (bf16[384,2048]{1,0:T(8,128)(2,1)}, bf16[384,2048]{1,0:T(8,128)(2,1)}, f32[16,8,384]{2,1,0:T(8,128)S(1)}, f32[8,128]{1,0:T(8,128)S(1)}) custom-call(bf16[384,1024]{1,0:T(8,128)(2,1)S(1)} %get-tuple-element.162.refs_0_.refs_1_, bf16[1024,4224]{1,0:T(8,128)(2,1)} %get-tuple-element.163.refs_1_.refs_2_.refs_3_.refs_4_, ...), custom_call_target="tpu_custom_call" | custom-call | tf_op jit(solution)/shard_map/project_queries/pallas_call | solution.py:68
  122.0 4.7 norm_pack.1
  128.8 12.9 %project_keys_values.1 = (bf16[1536,1024]{1,0:T(8,128)(2,1)}, bf16[1536,1024]{1,0:T(8,128)(2,1)}, bf16[1536,1024]{1,0:T(8,128)(2,1)}, f32[8,128]{1,0:T(8,128)S(1)}) custom-call(bf16[1536,1024]{1,0:T(8,128)(2,1)S(1)} %bitcast.52, bf16[1024,4224]{1,0:T(8,128)(2,1)} %get-tuple-element.163.refs_1_.refs_2_.refs_3_.refs_4_, ...), custom_call_target="tpu_custom_call" | custom-call | tf_op jit(solution)/shard_map/project_keys_values/pallas_call | solution.py:68
  141.7 13.9 %attend.1 = (bf16[384,2048]{1,0:T(8,128)(2,1)}, f32[16,8,384]{2,1,0:T(8,128)S(1)}, f32[8,128]{1,0:T(8,128)S(1)}) custom-call(bf16[384,2048]{1,0:T(8,128)(2,1)} %get-tuple-element.165.refs_0_, bf16[1536,1024]{1,0:T(8,128)(2,1)} %get-tuple-element.171.refs_1_.refs_3_, bf16[1536,1024]{1,0:T(8,128)(2,1)} %get-tuple-element.172.refs_2_.refs_4_, ...), custom_call_target="tpu_custom_call" | custom-call | tf_op jit(solution)/shard_map/attend/pallas_call | solution.py:68
  155.7 5.1 %all-gather.3.cloned.1.call-done = bf16[11264,1024]{1,0:T(8,128)(2,1)} async-done(((bf16[1408,1024]{1,0:T(8,128)(2,1)}), bf16[11264,1024]{1,0:T(8,128)(2,1)}) %all-gather.3.cloned.1.call-update) | async-done | bytes 23068688 | tf_op jit(solution)/shard_map/all_gather | solution.py:1162
  162.2 28.1 %middle_block.1 = (bf16[384,1024]{1,0:T(8,128)(2,1)}, bf16[384,1024]{1,0:T(8,128)(2,1)S(1)}, bf16[384,3072]{1,0:T(8,128)(2,1)S(1)}, bf16[2,384,3072]{2,1,0:T(8,1...) custom-call(bf16[384,2048]{1,0:T(8,128)(2,1)S(1)} %copy-done, ...), custom_call_target="tpu_custom_call" | custom-call | tf_op jit(solution)/shard_map/middle_block/pallas_call | solution.py:68
  190.3 3.8 copy-done.18
  194.1 9.5 %weight_grad.5 = (bf16[1024,6144]{1,0:T(8,128)(2,1)}, f32[8,128]{1,0:T(8,128)S(1)}) custom-call(bf16[384,1024]{1,0:T(8,128)(2,1)S(1)} %get-tuple-element.182.refs_0_, bf16[2,384,3072]{2,1,0:T(8,128)(2,1)S(1)} %copy-done.18, f32[8,128]{1,0:T(8,128)S(1)} %get-tuple-element.184.refs_2_), custom_call_target="tpu_custom_call" | custom-call | tf_op jit(solution)/shard_map/weight_grad/pallas_call | solution.py:68
  206.1 4.6 collective-permute-start.15
  210.8 14.2 %query_back.2 = (bf16[384,2048]{1,0:T(8,128)(2,1)}, f32[1,128]{1,0:T(1,128)S(1)}, f32[8,128]{1,0:T(8,128)S(1)}) custom-call(bf16[384,2048]{1,0:T(8,128)(2,1)} %get-tuple-element.165.refs_0_, bf16[384,2048]{1,0:T(8,128)(2,1)} %get-tuple-element.180.refs_1_.refs_2_, bf16[384,2048]{1,0:T(8,128)(2,1)} %get-tuple-element.174.refs_0_.refs_2_.refs_1_, ...), custom_call_target="tpu_custom_call" | custom-call | tf_op jit(solution)/shard_map/query_back/pallas_call | solution.py:68
  235.5 12.9 %query_back.3 = (bf16[384,2048]{1,0:T(8,128)(2,1)}, f32[1,128]{1,0:T(1,128)S(1)}, f32[8,128]{1,0:T(8,128)S(1)}) custom-call(bf16[384,2048]{1,0:T(8,128)(2,1)} %get-tuple-element.165.refs_0_, bf16[384,2048]{1,0:T(8,128)(2,1)} %get-tuple-element.180.refs_1_.refs_2_, ...), custom_call_target="tpu_custom_call", output_to_operand_aliasing={{0}: (13, {})} | custom-call | tf_op jit(solution)/shard_map/query_back/pallas_call | solution.py:68
  248.9 11.2 %collective-permute-done.18.refs_1_.refs_10_ = bf16[432,1024]{1,0:T(8,128)(2,1)S(1)} collective-permute-done((bf16[432,1024]{1,0:T(8,128)(2,1)}, bf16[432,1024]{1,0:T(8,128)(2,1)S(1)}, u32[]{:S(2)}, u32[]{:S(2)}) %collective-permute-start.18) | collective-permute-done | bytes 884768 | tf_op jit(solution)/shard_map/ppermute | solution.py:1066
  269.1 12.5 %all_queries.1 = (bf16[1536,2048]{1,0:T(8,128)(2,1)}, f32[8,128]{1,0:T(8,128)S(1)}) custom-call(bf16[1536,1024]{1,0:T(8,128)(2,1)S(1)} %bitcast.53, bf16[1024,4224]{1,0:T(8,128)(2,1)} %get-tuple-element.163.refs_1_.refs_2_.refs_3_.refs_4_, f32[1,128]{1,0:T(1,128)S(1)} %copy-done.61, f32[1536,128]{1,0:T(8,128)S(1)} %copy-done.15, f32[1536,128]{1,0:T(8,128)S(1)} %copy-done.17, ...), custom_call_target="tpu_custom_call" | custom-call | tf_op jit(solution)/shard_map/all_queries/pallas_call | solution.py:68
  281.6 10.3 %collective-permute-done.20.refs_2_.refs_11_ = bf16[432,1024]{1,0:T(8,128)(2,1)S(1)} collective-permute-done((bf16[432,1024]{1,0:T(8,128)(2,1)}, bf16[432,1024]{1,0:T(8,128)(2,1)S(1)}, u32[]{:S(2)}, u32[]{:S(2)}) %collective-permute-start.20) | collective-permute-done | bytes 884768 | tf_op jit(solution)/shard_map/ppermute | solution.py:1066
  306.8 11.9 %all_grad_mixed.1 = (bf16[2,4,192,2048]{3,2,1,0:T(8,128)(2,1)}, f32[2,4,48,192]{3,2,1,0:T(8,128)S(1)}, f32[8,128]{1,0:T(8,128)S(1)}) custom-call(s32[4]{0:T(128)S(1)} %copy-done.71, s32[1]{0:T(128)} %bitcast.6.refs_1_.refs_0_, bf16[384,2048]{1,0:T(8,128)(2,1)S(1)} %copy-done.2, bf16[8,1408,1024]{2,1,0:T(8,128)(2,1)} %bitcast.74, ...), custom_call_target="tpu_custom_call" | custom-call | tf_op jit(solution)/shard_map/all_grad_mixed/pallas_call | solution.py:68
  321.7 12.8 %key_back.2 = (bf16[2,384,1024]{2,1,0:T(8,128)(2,1)}, f32[1,128]{1,0:T(1,128)S(1)}, f32[8,128]{1,0:T(8,128)S(1)}) custom-call(s32[1]{0:T(128)} %bitcast.6.refs_1_.refs_0_, bf16[1536,2048]{1,0:T(8,128)(2,1)} %get-tuple-element.198.refs_1_, bf16[1536,2048]{1,0:T(8,128)(2,1)} %bitcast.80, bf16[2,4,192,1024]{3,2,1,0:T(8,128)(2,1)} %bitcast.76, ...), custom_call_target="tpu_custom_call" | custom-call | tf_op jit(solution)/shard_map/key_back/pallas_call | solution.py:68
  342.7 6.2 %weight_grad.8 = (bf16[3072,1024]{1,0:T(8,128)(2,1)}, f32[8,128]{1,0:T(8,128)S(1)}) custom-call(bf16[384,3072]{1,0:T(8,128)(2,1)S(1)} %copy-done.34, bf16[384,1024]{1,0:T(8,128)(2,1)S(1)} %bitcast.55, f32[8,128]{1,0:T(8,128)S(1)} %get-tuple-element.222.refs_2_), custom_call_target="tpu_custom_call" | custom-call | tf_op jit(solution)/shard_map/weight_grad/pallas_call | solution.py:68
  351.9 12.9 %key_back.3 = (bf16[2,384,1024]{2,1,0:T(8,128)(2,1)}, f32[1,128]{1,0:T(1,128)S(1)}, f32[8,128]{1,0:T(8,128)S(1)}) custom-call(s32[1]{0:T(128)} %bitcast.6.refs_1_.refs_0_, bf16[1536,2048]{1,0:T(8,128)(2,1)} %get-tuple-element.198.refs_1_, bf16[1536,2048]{1,0:T(8,128)(2,1)} %bitcast.81, ...), custom_call_target="tpu_custom_call", output_to_operand_aliasing={{0}: (13, {})} | custom-call | tf_op jit(solution)/shard_map/key_back/pallas_call | solution.py:68
  369.9 3.9 collective-permute-start.33
  373.8 7.6 %normed_back.1 = (f32[384,1024]{1,0:T(8,128)}, f32[8,128]{1,0:T(8,128)S(1)}) custom-call(bf16[384,2048]{1,0:T(8,128)(2,1)S(1)} %copy-done.3, bf16[2,384,1024]{2,1,0:T(8,128)(2,1)S(1)} %copy-done.4, bf16[1024,4224]{1,0:T(8,128)(2,1)} %get-tuple-element.163.refs_1_.refs_2_.refs_3_.refs_4_, ...), custom_call_target="tpu_custom_call" | custom-call | tf_op jit(solution)/shard_map/normed_back/pallas_call | solution.py:68
  390.4 10.9 %collective-permute-done.34.refs_1_ = bf16[2,128,1024]{2,1,0:T(8,128)(2,1)S(1)} collective-permute-done((bf16[2,128,1024]{2,1,0:T(8,128)(2,1)S(1)}, bf16[2,128,1024]{2,1,0:T(8,128)(2,1)S(1)}, u32[]{:S(2)}, u32[]{:S(2)}) %collective-permute-start.34) | collective-permute-done | bytes 524320 | tf_op jit(solution)/shard_map/ppermute | solution.py:921
  410.0 6.3 %collective-permute-done.32.refs_1_ = f32[18,128]{1,0:T(8,128)S(1)} collective-permute-done((f32[18,128]{1,0:T(8,128)S(1)}, f32[18,128]{1,0:T(8,128)S(1)}, u32[]{:S(2)}, u32[]{:S(2)}) %collective-permute-start.32) | collective-permute-done | bytes 9248 | tf_op jit(solution)/shard_map/ppermute | solution.py:921
  421.7 4.4 collective-permute-start.40
  428.3 3.6 collective-permute-done.36.refs_1_
  442.2 42.7 %all-reduce.2.cloned.1.call-done.refs_1_ = bf16[384,1024]{1,0:T(8,128)(2,1)} async-done(((bf16[384,1024]{1,0:T(8,128)(2,1)}), bf16[384,1024]{1,0:T(8,128)(2,1)}) %all-reduce.2.cloned.1.call-update) | async-done | bytes 786448 | tf_op jit(solution)/shard_map/psum | solution.py:1309
  490.5 4.0 collective-permute-done.46.refs_2_
  (349 shorter events, 143.6 us)
Async XLA Ops:
  7.2 153.6 %all-gather.3.cloned.1.call-start = ((), (), s32[]{:S(2)}) async-start(), calls=%async_computation.5 | async-start | bytes 25952256 | tf_op jit(solution)/shard_map/all_gather | solution.py:1162
  14.7 284.0 %reduce-scatter.3.cloned.1.call-start = ((), (), s32[]{:S(2)}) async-start(), calls=%async_computation.2 | async-start | bytes 14155776 | tf_op jit(solution)/shard_map/reduce_scatter | solution.py:1238
  15.8 22.5 %collective-permute-start.10 = (bf16[384,1024]{1,0:T(8,128)(2,1)S(1)}, bf16[384,1024]{1,0:T(8,128)(2,1)S(1)}, u32[]{:S(2)}, u32[]{:S(2)}) collective-permute-start(bf16[384,1024]{1,0:T(8,128)(2,1)S(1)} %bitcast.46), channel_id=1, source_target_pairs={{1,0},{2,1},{3,2},{5,4},{6,5},{7,6},{9,8},{10,9},{11,10},{13,12},{... | collective-permute-start | bytes 2359304 | tf_op jit(solution)/shard_map/ppermute | solution.py:1066
  17.1 22.3 %collective-permute-start.9 = (bf16[384,1024]{1,0:T(8,128)(2,1)S(1)}, bf16[384,1024]{1,0:T(8,128)(2,1)S(1)}, u32[]{:S(2)}, u32[]{:S(2)}) collective-permute-start(bf16[384,1024]{1,0:T(8,128)(2,1)S(1)} %bitcast.47), channel_id=1, source_target_pairs={{0,1},{1,2},{2,3},{4,5},{5,6},{6,7},{8,9},{9,10},{10,11},{12,13},{... | collective-permute-start | bytes 2359304 | tf_op jit(solution)/shard_map/ppermute | solution.py:1064
  22.7 50.8 %collective-permute-start.3 = (bf16[128,4224]{1,0:T(8,128)(2,1)}, bf16[128,4224]{1,0:T(8,128)(2,1)}, u32[]{:S(2)}, u32[]{:S(2)}) collective-permute-start(bf16[128,4224]{1,0:T(8,128)(2,1)} %get-tuple-element.153.refs_1_), channel_id=1, source_target_pairs={{0,16},{4,20},{8,24},{12,28},{16,0},{20,4},{24,8},{28,12},{1,17},{... | collective-permute-start | bytes 3244040 | tf_op jit(solution)/shard_map/ppermute | solution.py:921
  24.8 46.9 %collective-permute-start.1 = (bf16[128,4224]{1,0:T(8,128)(2,1)}, bf16[128,4224]{1,0:T(8,128)(2,1)}, u32[]{:S(2)}, u32[]{:S(2)}) collective-permute-start(bf16[128,4224]{1,0:T(8,128)(2,1)} %get-tuple-element.153.refs_1_), channel_id=1, source_target_pairs={{0,8},{4,12},{8,0},{12,4},{16,24},{20,28},{24,16},{28,20},{1,9},{5... | collective-permute-start | bytes 3244040 | tf_op jit(solution)/shard_map/ppermute | solution.py:921
  26.2 72.1 %collective-permute-start = (bf16[128,4224]{1,0:T(8,128)(2,1)}, bf16[128,4224]{1,0:T(8,128)(2,1)}, u32[]{:S(2)}, u32[]{:S(2)}) collective-permute-start(bf16[128,4224]{1,0:T(8,128)(2,1)} %get-tuple-element.153.refs_1_), channel_id=1, source_target_pairs={{0,4},{4,0},{8,12},{12,8},{16,20},{20,16},{24,28},{28,24},{1,5},{5... | collective-permute-start | bytes 3244040 | tf_op jit(solution)/shard_map/ppermute | solution.py:921
  42.9 34.2 %collective-permute-start.11 = (bf16[384,1024]{1,0:T(8,128)(2,1)}, bf16[384,1024]{1,0:T(8,128)(2,1)S(1)}, u32[]{:S(2)}, u32[]{:S(2)}) collective-permute-start(bf16[384,1024]{1,0:T(8,128)(2,1)} %get-tuple-element.156), channel_id=1, source_target_pairs={{1,2},{2,3},{5,6},{6,7},{9,10},{10,11},{13,14},{14,15},{17,18},{18... | collective-permute-start | bytes 2359304 | tf_op jit(solution)/shard_map/ppermute | solution.py:1064
  43.6 33.5 %collective-permute-start.12 = (bf16[384,1024]{1,0:T(8,128)(2,1)}, bf16[384,1024]{1,0:T(8,128)(2,1)S(1)}, u32[]{:S(2)}, u32[]{:S(2)}) collective-permute-start(bf16[384,1024]{1,0:T(8,128)(2,1)} %get-tuple-element.157), channel_id=1, source_target_pairs={{1,0},{2,1},{5,4},{6,5},{9,8},{10,9},{13,12},{14,13},{17,16},{18,1... | collective-permute-start | bytes 2359304 | tf_op jit(solution)/shard_map/ppermute | solution.py:1066
  74.6 18.1 %collective-permute-start.6 = (bf16[128,2176]{1,0:T(8,128)(2,1)S(1)}, bf16[128,2176]{1,0:T(8,128)(2,1)}, u32[]{:S(2)}, u32[]{:S(2)}) collective-permute-start(bf16[128,2176]{1,0:T(8,128)(2,1)S(1)} %slice.37), channel_id=1, source_target_pairs={{0,8},{4,12},{8,0},{12,4},{16,24},{20,28},{24,16},{28,20},{1,9},{5... | collective-permute-start | bytes 1671176 | tf_op jit(solution)/shard_map/ppermute | solution.py:921
  77.2 26.0 %collective-permute-start.4 = (bf16[128,4224]{1,0:T(8,128)(2,1)}, bf16[128,4224]{1,0:T(8,128)(2,1)}, u32[]{:S(2)}, u32[]{:S(2)}) collective-permute-start(bf16[128,4224]{1,0:T(8,128)(2,1)} %collective-permute-done.3.refs_2_.refs_5_), channel_id=1, source_target_pairs={{0,4},{4,0},{8,12},{12,8},{16,20},{20,16},{24,28},{28,24},{1,5},{5... | collective-permute-start | bytes 3244040 | tf_op jit(solution)/shard_map/ppermute | solution.py:921
  77.2 26.0 %collective-permute-start.2 = (bf16[128,4224]{1,0:T(8,128)(2,1)}, bf16[128,4224]{1,0:T(8,128)(2,1)}, u32[]{:S(2)}, u32[]{:S(2)}) collective-permute-start(bf16[128,4224]{1,0:T(8,128)(2,1)} %collective-permute-done.1.refs_1_.refs_3_), channel_id=1, source_target_pairs={{0,4},{4,0},{8,12},{12,8},{16,20},{20,16},{24,28},{28,24},{1,5},{5... | collective-permute-start | bytes 3244040 | tf_op jit(solution)/shard_map/ppermute | solution.py:921
  98.4 22.9 %collective-permute-start.13 = (bf16[384,1024]{1,0:T(8,128)(2,1)}, bf16[384,1024]{1,0:T(8,128)(2,1)}, u32[]{:S(2)}, u32[]{:S(2)}) collective-permute-start(bf16[384,1024]{1,0:T(8,128)(2,1)} %get-tuple-element.166), channel_id=1, source_target_pairs={{2,3},{6,7},{10,11},{14,15},{18,19},{22,23},{26,27},{30,31}} | collective-permute-start | bytes 2359304 | tf_op jit(solution)/shard_map/ppermute | solution.py:1064
  100.0 22.0 %collective-permute-start.14 = (bf16[384,1024]{1,0:T(8,128)(2,1)}, bf16[384,1024]{1,0:T(8,128)(2,1)}, u32[]{:S(2)}, u32[]{:S(2)}) collective-permute-start(bf16[384,1024]{1,0:T(8,128)(2,1)} %get-tuple-element.167), channel_id=1, source_target_pairs={{1,0},{5,4},{9,8},{13,12},{17,16},{21,20},{25,24},{29,28}} | collective-permute-start | bytes 2359304 | tf_op jit(solution)/shard_map/ppermute | solution.py:1066
  203.7 222.3 %reduce-scatter.5.cloned.1.call-start = ((), (), s32[]{:S(2)}) async-start(), calls=%async_computation.3 | async-start | bytes 7077888 | tf_op jit(solution)/shard_map/reduce_scatter | solution.py:1280
  204.8 23.7 %collective-permute-start.16 = (bf16[432,1024]{1,0:T(8,128)(2,1)S(1)}, bf16[432,1024]{1,0:T(8,128)(2,1)S(1)}, u32[]{:S(2)}, u32[]{:S(2)}) collective-permute-start(bf16[432,1024]{1,0:T(8,128)(2,1)S(1)} %copy-done.45), channel_id=1, source_target_pairs={{1,0},{2,1},{3,2},{5,4},{6,5},{7,6},{9,8},{10,9},{11,10},{13,12},{... | collective-permute-start | bytes 2654216 | tf_op jit(solution)/shard_map/ppermute | solution.py:1066
  206.1 23.6 %collective-permute-start.15 = (bf16[432,1024]{1,0:T(8,128)(2,1)S(1)}, bf16[432,1024]{1,0:T(8,128)(2,1)S(1)}, u32[]{:S(2)}, u32[]{:S(2)}) collective-permute-start(bf16[432,1024]{1,0:T(8,128)(2,1)S(1)} %copy-done.45), channel_id=1, source_target_pairs={{0,1},{1,2},{2,3},{4,5},{5,6},{6,7},{8,9},{9,10},{10,11},{12,13},{... | collective-permute-start | bytes 2654216 | tf_op jit(solution)/shard_map/ppermute | solution.py:1064
  234.0 26.0 %collective-permute-start.18 = (bf16[432,1024]{1,0:T(8,128)(2,1)}, bf16[432,1024]{1,0:T(8,128)(2,1)S(1)}, u32[]{:S(2)}, u32[]{:S(2)}) collective-permute-start(bf16[432,1024]{1,0:T(8,128)(2,1)} %get-tuple-element.194), channel_id=1, source_target_pairs={{1,0},{2,1},{5,4},{6,5},{9,8},{10,9},{13,12},{14,13},{17,16},{18,1... | collective-permute-start | bytes 2654216 | tf_op jit(solution)/shard_map/ppermute | solution.py:1066
  235.3 58.5 %collective-permute-start.21 = (bf16[4,128,2048]{2,1,0:T(8,128)(2,1)S(1)}, bf16[4,128,2048]{2,1,0:T(8,128)(2,1)S(1)}, u32[]{:S(2)}, u32[]{:S(2)}) collective-permute-start(bf16[4,128,2048]{2,1,0:T(8,128)(2,1)S(1)} %get-tuple-element.203), channel_id=1, source_target_pairs={{0,4},{4,0},{8,12},{12,8},{16,20},{20,16},{24,28},{28,24},{1,5},{5... | collective-permute-start | bytes 6291464 | tf_op jit(solution)/shard_map/ppermute | solution.py:921
  267.0 26.9 %collective-permute-start.22 = (bf16[4,128,2048]{2,1,0:T(8,128)(2,1)S(1)}, bf16[4,128,2048]{2,1,0:T(8,128)(2,1)S(1)}, u32[]{:S(2)}, u32[]{:S(2)}) collective-permute-start(bf16[4,128,2048]{2,1,0:T(8,128)(2,1)S(1)} %get-tuple-element.205), channel_id=1, source_target_pairs={{0,4},{4,0},{8,12},{12,8},{16,20},{20,16},{24,28},{28,24},{1,5},{5... | collective-permute-start | bytes 6291464 | tf_op jit(solution)/shard_map/ppermute | solution.py:921
  267.8 24.1 %collective-permute-start.20 = (bf16[432,1024]{1,0:T(8,128)(2,1)}, bf16[432,1024]{1,0:T(8,128)(2,1)S(1)}, u32[]{:S(2)}, u32[]{:S(2)}) collective-permute-start(bf16[432,1024]{1,0:T(8,128)(2,1)} %get-tuple-element.200), channel_id=1, source_target_pairs={{1,0},{5,4},{9,8},{13,12},{17,16},{21,20},{25,24},{29,28}} | collective-permute-start | bytes 2654216 | tf_op jit(solution)/shard_map/ppermute | solution.py:1066
  301.5 37.6 %collective-permute-start.23 = (bf16[128,6144]{1,0:T(8,128)(2,1)}, bf16[128,6144]{1,0:T(8,128)(2,1)}, u32[]{:S(2)}, u32[]{:S(2)}) collective-permute-start(bf16[128,6144]{1,0:T(8,128)(2,1)} %get-tuple-element.215), channel_id=1, source_target_pairs={{0,1},{3,2},{4,5},{7,6},{8,9},{11,10},{12,13},{15,14},{16,17},{19,... | collective-permute-start | bytes 4718600 | tf_op jit(solution)/shard_map/ppermute | solution.py:1030
  304.2 30.2 %collective-permute-start.24 = (bf16[2,128,2048]{2,1,0:T(8,128)(2,1)}, bf16[2,128,2048]{2,1,0:T(8,128)(2,1)}, u32[]{:S(2)}, u32[]{:S(2)}) collective-permute-start(bf16[2,128,2048]{2,1,0:T(8,128)(2,1)} %copy-done.73), channel_id=1, source_target_pairs={{0,8},{4,12},{8,0},{12,4},{16,24},{20,28},{24,16},{28,20},{1,9},{5... | collective-permute-start | bytes 3145736 | tf_op jit(solution)/shard_map/ppermute | solution.py:921
  305.7 28.7 %collective-permute-start.25 = (bf16[2,128,2048]{2,1,0:T(8,128)(2,1)}, bf16[2,128,2048]{2,1,0:T(8,128)(2,1)}, u32[]{:S(2)}, u32[]{:S(2)}) collective-permute-start(bf16[2,128,2048]{2,1,0:T(8,128)(2,1)} %copy-done.72), channel_id=1, source_target_pairs={{0,16},{4,20},{8,24},{12,28},{16,0},{20,4},{24,8},{28,12},{1,17},{... | collective-permute-start | bytes 3145736 | tf_op jit(solution)/shard_map/ppermute | solution.py:921
  348.9 136.0 %all-reduce.2.cloned.1.call-start = ((), (), s32[]{:S(2)}) async-start(), calls=%async_computation.4 | async-start | bytes 1572864 | tf_op jit(solution)/shard_map/psum | solution.py:1309
  351.1 33.5 %collective-permute-start.31 = (bf16[128,6144]{1,0:T(8,128)(2,1)}, bf16[128,6144]{1,0:T(8,128)(2,1)S(1)}, u32[]{:S(2)}, u32[]{:S(2)}) collective-permute-start(bf16[128,6144]{1,0:T(8,128)(2,1)} %bitcast.56), channel_id=1, source_target_pairs={{1,2},{2,1},{5,6},{6,5},{9,10},{10,9},{13,14},{14,13},{17,18},{18,... | collective-permute-start | bytes 4718600 | tf_op jit(solution)/shard_map/ppermute | solution.py:1030
  369.9 34.3 %collective-permute-start.33 = (bf16[256,2048]{1,0:T(8,128)(2,1)S(1)}, bf16[256,2048]{1,0:T(8,128)(2,1)S(1)}, u32[]{:S(2)}, u32[]{:S(2)}) collective-permute-start(bf16[256,2048]{1,0:T(8,128)(2,1)S(1)} %get-tuple-element.251), channel_id=1, source_target_pairs={{0,1},{3,2},{4,5},{7,6},{8,9},{11,10},{12,13},{15,14},{16,17},{19,... | collective-permute-start | bytes 3145736 | tf_op jit(solution)/shard_map/ppermute | solution.py:1030
  387.2 44.7 %collective-permute-start.41 = (bf16[128,6144]{1,0:T(8,128)(2,1)S(1)}, bf16[128,6144]{1,0:T(8,128)(2,1)S(1)}, u32[]{:S(2)}, u32[]{:S(2)}) collective-permute-start(bf16[128,6144]{1,0:T(8,128)(2,1)S(1)} %bitcast.58), channel_id=1, source_target_pairs={{1,0},{2,3},{5,4},{6,7},{9,8},{10,11},{13,12},{14,15},{17,16},{18,... | collective-permute-start | bytes 4718600 | tf_op jit(solution)/shard_map/ppermute | solution.py:1030
  405.4 30.7 %collective-permute-start.44 = (bf16[256,2048]{1,0:T(8,128)(2,1)}, bf16[256,2048]{1,0:T(8,128)(2,1)}, u32[]{:S(2)}, u32[]{:S(2)}) collective-permute-start(bf16[256,2048]{1,0:T(8,128)(2,1)} %bitcast.33), channel_id=1, source_target_pairs={{1,2},{2,1},{5,6},{6,5},{9,10},{10,9},{13,14},{14,13},{17,18},{18,... | collective-permute-start | bytes 3145736 | tf_op jit(solution)/shard_map/ppermute | solution.py:1030
  437.9 51.1 %collective-permute-start.45 = (bf16[256,2048]{1,0:T(8,128)(2,1)S(1)}, bf16[256,2048]{1,0:T(8,128)(2,1)S(1)}, u32[]{:S(2)}, u32[]{:S(2)}) collective-permute-start(bf16[256,2048]{1,0:T(8,128)(2,1)S(1)} %bitcast.60), channel_id=1, source_target_pairs={{1,0},{2,3},{5,4},{6,7},{9,8},{10,11},{13,12},{14,15},{17,16},{18,... | collective-permute-start | bytes 3145736 | tf_op jit(solution)/shard_map/ppermute | solution.py:1030
  439.2 46.9 %collective-permute-start.43 = (bf16[128,1024]{1,0:T(8,128)(2,1)S(1)}, bf16[128,1024]{1,0:T(8,128)(2,1)S(1)}, u32[]{:S(2)}, u32[]{:S(2)}) collective-permute-start(bf16[128,1024]{1,0:T(8,128)(2,1)S(1)} %bitcast.68), channel_id=1, source_target_pairs={{0,2},{1,3},{2,0},{3,1},{4,6},{5,7},{6,4},{7,5},{8,10},{9,11},{10,... | collective-permute-start | bytes 786440 | tf_op jit(solution)/shard_map/ppermute | solution.py:921
  441.1 45.4 %collective-permute-start.42 = (f32[18,128]{1,0:T(8,128)S(1)}, f32[18,128]{1,0:T(8,128)S(1)}, u32[]{:S(2)}, u32[]{:S(2)}) collective-permute-start(f32[18,128]{1,0:T(8,128)S(1)} %get-tuple-element.275.refs_0_), channel_id=1, source_target_pairs={{0,2},{1,3},{2,0},{3,1},{4,6},{5,7},{6,4},{7,5},{8,10},{9,11},{10,... | collective-permute-start | bytes 27656 | tf_op jit(solution)/shard_map/ppermute | solution.py:921
  (112 other events, 1049.3 us)
Sparse Core Ops, SparseCore 0:
  14.8 145.8 all-gather.2
  203.8 92.4 reduce-scatter.2
  349.0 63.7 reduce-scatter.4
  428.3 56.6 all-reduce.1
